TPU v7x, 128 devices: a whole 4x4x4 slice. The times are simulated.
128 devices in a mesh: gx: 32 (over z, y, core), gy: 4 (over x).
Axes of the slice: x: 4, y: 4, z: 4, core: 2. Of those that a mesh axis runs over, the one named last changes fastest.
Arguments:
- source: float32 [512, 256, 128], P('gx', 'gy'), may hold values from -6 to 6
- density: float32 [512, 256, 128], P('gx', 'gy'), may hold values from 0.5 to 5
- darcy_drag: float32 [512, 256, 128], P('gx', 'gy'), may hold values from 1 to 30
- porous_rows: int32 [256], P('gy'), may hold values 0 or 1
Outputs:
- solution: float32 [512, 256, 128], P('gx', 'gy')
- residual: float32 [512, 256, 128], P('gx', 'gy')
Inputs may be any that keep to these rules, and one draw needn't show every extreme that they name: `porous_rows`: 1 marks a wall-normal index inside the porous layer, 0 one outside.
All inputs are finite; a program needn't handle non-finite values. No bound on the sum of `porous_rows` on one device may be relied on, other than what follows from the above.
Results may differ from a plain program's by a relative error of at most 0.0003.
Values sent between devices are 32-bit elements; how exact they have to be, the bound alone decides.
No kernel may reach another device: no remote copies, remote signals or barrier semaphores. Data moves between devices by JAX's collectives and lax.ppermute only.
A program may use at most 192 MiB of HBM per device.

v0:
```python
import jax
import jax.numpy as jnp
from jax import lax
from jax.sharding import PartitionSpec as P

LEVELS = 7
SWEEPS_COARSE = 16


damping = 0.8
helmholtz_base = 0.0002


def with_halo(block, sides, width):
    for axis, dim in sides:
        count = lax.axis_size(axis)
        forward = [(i, i + 1) for i in range(count - 1)]
        backward = [(target, source) for source, target in forward]
        low = lax.ppermute(
            lax.slice_in_dim(block, block.shape[dim] - width, None, axis=dim), axis, forward
        )
        high = lax.ppermute(lax.slice_in_dim(block, 0, width, axis=dim), axis, backward)
        block = jnp.concatenate([low, block, high], axis=dim)
    return block


def zero_pad(values):
    return jnp.pad(values, ((1, 1), (1, 1), (0, 0)))


def face_coeffs(padded):
    centre = padded[1:-1, 1:-1, :]

    def harmonic(neighbour):
        total = centre + neighbour
        positive = total > 0.0
        safe_total = jnp.where(positive, total, 1.0)
        return jnp.where(positive, 2.0 * centre * neighbour / safe_total, 0.0)

    return (
        harmonic(padded[2:, 1:-1, :]),
        harmonic(padded[:-2, 1:-1, :]),
        harmonic(padded[1:-1, 2:, :]),
        harmonic(padded[1:-1, :-2, :]),
        harmonic(jnp.roll(centre, -1, 2)),
        harmonic(jnp.roll(centre, 1, 2)),
    )


def operate(padded, face_list, helmholtz):
    values = padded[1:-1, 1:-1, :]
    beside = (
        padded[2:, 1:-1, :],
        padded[:-2, 1:-1, :],
        padded[1:-1, 2:, :],
        padded[1:-1, :-2, :],
        jnp.roll(values, -1, 2),
        jnp.roll(values, 1, 2),
    )
    applied = helmholtz * values
    for coeff, neighbour in zip(face_list, beside):
        applied = applied + coeff * (values - neighbour)
    return applied


def halving(shape):
    return tuple((2 for length in shape))


def coarsen(values):
    split_shape = []
    for length, stride in zip(values.shape, halving(values.shape)):
        split_shape += [length // stride, stride]
    return jnp.mean(values.reshape(split_shape), axis=(1, 3, 5))


def refine(values, factor):
    for axis_num, stride in enumerate(factor):
        values = jnp.repeat(values, stride, axis=axis_num)
    return values


def smooth_cycle(tier_index, source, conduct):
    face_list = face_coeffs(zero_pad(conduct))
    helmholtz = helmholtz_base * 4.0**tier_index
    diagonal = helmholtz + sum(face_list)

    def residual_of(current):
        return source - operate(zero_pad(current), face_list, helmholtz)

    if tier_index == LEVELS - 1:
        current = jnp.zeros_like(source)
        for _ in range(SWEEPS_COARSE):
            current = current + damping * residual_of(current) / diagonal
        return current
    current = damping * source / diagonal
    current = current + damping * residual_of(current) / diagonal
    remain = residual_of(current)
    factor = halving(source.shape)
    correction = smooth_cycle(tier_index + 1, 4.0 * coarsen(remain), coarsen(conduct))
    current = current + refine(correction, factor)
    for _ in range(2):
        current = current + damping * residual_of(current) / diagonal
    return current


def extend(values):
    return with_halo(values, (("gx", 0), ("gy", 1)), 1)


def agglomerate(coarse_source, coarse_conduct, tier_index):
    whole_source, whole_conduct = (
        lax.all_gather(coarse_source[None], ("gx", "gy"), axis=0, tiled=True),
        lax.all_gather(coarse_conduct[None], ("gx", "gy"), axis=0, tiled=True),
    )
    count_x = lax.axis_size("gx")
    count_y = lax.axis_size("gy")
    block_x, block_y, block_z = coarse_source.shape

    def arrange(stacked):
        stacked = stacked.reshape(count_x, count_y, block_x, block_y, block_z)
        return stacked.transpose(0, 2, 1, 3, 4).reshape(
            count_x * block_x, count_y * block_y, block_z
        )

    correction = smooth_cycle(tier_index, arrange(whole_source), arrange(whole_conduct))
    start_x = lax.axis_index("gx") * block_x
    start_y = lax.axis_index("gy") * block_y
    return lax.dynamic_slice(
        correction, (start_x, start_y, jnp.int32(0)), (block_x, block_y, block_z)
    )


def per_device(source, density, darcy_drag, porous_rows):
    conduct = 1.0 / (density * (1.0 + darcy_drag * porous_rows.astype(jnp.float32)[None, :, None]))
    agglo_depth = 3
    conducts = [conduct]
    for _ in range(agglo_depth):
        conducts.append(coarsen(conducts[-1]))
    padded_list = [
        with_halo(conducts[tier_index], (("gx", 0), ("gy", 1)), 1)
        for tier_index in range(agglo_depth)
    ]

    def descend_plain(tier_index, source_now):
        face_list = face_coeffs(padded_list[tier_index])
        helmholtz = helmholtz_base * 4.0**tier_index
        diagonal = helmholtz + sum(face_list)

        def residual_of(current):
            return source_now - operate(extend(current), face_list, helmholtz)

        current = damping * source_now / diagonal
        current = current + damping * residual_of(current) / diagonal
        remain = residual_of(current)
        coarse_source = 4.0 * coarsen(remain)
        if tier_index + 1 == agglo_depth:
            correction = agglomerate(coarse_source, conducts[agglo_depth], tier_index + 1)
        else:
            correction = descend_plain(tier_index + 1, coarse_source)
        current = current + refine(correction, (2, 2, 2))
        for _ in range(2):
            current = current + damping * residual_of(current) / diagonal
        return current

    solution = descend_plain(0, source)
    top_faces = face_coeffs(padded_list[0])
    residual = source - operate(extend(solution), top_faces, helmholtz_base)
    return (solution, residual)


def solution(mesh):
    return jax.shard_map(
        per_device,
        mesh=mesh,
        in_specs=(P("gx", "gy", None), P("gx", "gy", None), P("gx", "gy", None), P("gy")),
        out_specs=(P("gx", "gy", None), P("gx", "gy", None)),
        check_vma=False,
    )
```

profile of v0, /device:TPU:38, one launch (start us, length us, event | category | flops | bytes accessed | tf_op | source)
XLA Modules:
  0.0 707.8 jit_solution(2249977028757210506)
XLA Ops:
  7.2 5.8 collective-permute-start
  13.4 34.8 %reshape.129 = f32[8,2,32,2,64,2]{5,4,3,2,1,0:T(8,128)} reshape(f32[16,64,128]{2,1,0:T(8,128)S(1)} %copy.261) | data formatting | bytes 1048576 | tf_op jit(solution)/shard_map/reshape | solution.py:74
  48.2 12.2 %reduce_sum.116 = f32[8,32,64]{2,1,0:T(8,128)S(1)} reduce(f32[8,2,32,2,64,2]{5,4,3,2,1,0:T(8,128)} %reshape.129, f32[]{:T(128)} %constant.38.clone.1), dimensions={1,3,5}, to_apply=%region_1.0 | reduce | flops 114688 | bytes 589828 | tf_op jit(solution)/shard_map/reduce_sum | solution.py:74
  63.0 5.7 div.305
  81.7 61.4 %all-gather.1 = f32[256,8,16]{2,1,0:T(8,128)S(1)} all-gather(f32[2,8,16]{2,1,0:T(8,128)S(1)} %broadcast_multiply_fusion.5), channel_id=3, replica_groups=mesh['gx'=32,'gy'=4] {'gx','gy'}, dimensions={0}, use_global_device_ids=true | all-gather | bytes 132096 | tf_op jit(solution)/shard_map/all_gather | solution.py:114
  170.7 5.6 collective-permute-start.14
  182.2 5.7 fusion.84
  190.7 5.8 collective-permute-start.4
  216.7 5.9 fusion.66
  225.3 5.8 collective-permute-start.8
  253.2 5.5 fusion.52
  261.1 35.6 %reshape.128 = f32[8,2,32,2,64,2]{5,4,3,2,1,0:T(8,128)} reshape(f32[16,64,128]{2,1,0:T(8,128)} %copy.277) | data formatting | bytes 1048576 | tf_op jit(solution)/shard_map/reshape | solution.py:74
  296.7 12.2 %reduce_sum.115 = f32[8,32,64]{2,1,0:T(8,128)S(1)} reduce(f32[8,2,32,2,64,2]{5,4,3,2,1,0:T(8,128)} %reshape.128, f32[]{:T(128)} %constant.38.clone.1), dimensions={1,3,5}, to_apply=%region_0.0 | reduce | flops 114688 | bytes 589828 | tf_op jit(solution)/shard_map/reduce_sum | solution.py:74
  315.6 5.1 collective-permute-done.17
  334.8 4.6 collective-permute-done.21
  349.5 6.5 reshape.130
  364.1 4.6 collective-permute-done.29
  381.5 4.6 collective-permute-done.33
  395.9 58.5 %all-gather = f32[256,8,16]{2,1,0:T(8,128)S(1)} all-gather(f32[2,8,16]{2,1,0:T(8,128)S(1)} %broadcast_multiply_fusion.6), channel_id=2, replica_groups=mesh['gx'=32,'gy'=4] {'gx','gy'}, dimensions={0}, use_global_device_ids=true | all-gather | bytes 132096 | tf_op jit(solution)/shard_map/all_gather | solution.py:113
  462.1 10.8 %reshape.136 = f32[32,2,16,2,8,2]{1,0,5,4,3,2:T(8,128)} reshape(f32[64,32,16]{0,2,1:T(8,128)} %fusion.102) | data formatting | bytes 262144 | tf_op jit(solution)/shard_map/reshape | solution.py:74
  472.9 4.7 reduce_sum.121
  520.2 5.5 collective-permute-start.36
  527.7 5.1 collective-permute-done.37
  545.6 4.6 collective-permute-done.41
  567.9 4.6 collective-permute-done.45
  587.2 4.6 collective-permute-done.49
  607.3 5.8 collective-permute-start.52
  632.8 5.6 fusion.41
  640.4 5.8 collective-permute-start.56
  665.9 5.6 fusion.27
  673.5 5.8 collective-permute-start.60
  698.9 6.3 fusion.13
  (501 shorter events, 344.1 us)
Async XLA Ops:
  5.3 157.4 %collective-permute-start.1 = (f32[1,64,128]{1,0,2:T(1,128)}, f32[1,64,128]{1,0,2:T(1,128)S(1)}, u32[]{:S(2)}, u32[]{:S(2)}) collective-permute-start(f32[1,64,128]{1,0,2:T(1,128)} %get-tuple-element.93), channel_id=1, source_target_pairs={{0,4},{4,8},{8,12},{12,16},{16,20},{20,24},{24,28},{28,32},{32,36}... | collective-permute-start | bytes 98312 | tf_op jit(solution)/shard_map/ppermute | solution.py:19
  7.2 156.9 %collective-permute-start = (f32[1,64,128]{1,0,2:T(1,128)}, f32[1,64,128]{1,0,2:T(1,128)S(1)}, u32[]{:S(2)}, u32[]{:S(2)}) collective-permute-start(f32[1,64,128]{1,0,2:T(1,128)} %get-tuple-element.94), channel_id=1, source_target_pairs={{4,0},{8,4},{12,8},{16,12},{20,16},{24,20},{28,24},{32,28},{36,32}... | collective-permute-start | bytes 98312 | tf_op jit(solution)/shard_map/ppermute | solution.py:22
  61.1 107.6 %collective-permute-start.12 = (f32[1,32,64]{2,1,0:T(8,128)}, f32[1,32,64]{2,1,0:T(8,128)S(1)}, u32[]{:S(2)}, u32[]{:S(2)}) collective-permute-start(f32[1,32,64]{2,1,0:T(8,128)} %get-tuple-element.180), channel_id=1, source_target_pairs={{4,0},{8,4},{12,8},{16,12},{20,16},{24,20},{28,24},{32,28},{36,32}... | collective-permute-start | bytes 24584 | tf_op jit(solution)/shard_map/ppermute | solution.py:22
  71.9 83.8 %collective-permute-start.24 = (f32[1,16,32]{2,1,0:T(8,128)S(1)}, f32[1,16,32]{2,1,0:T(8,128)S(1)}, u32[]{:S(2)}, u32[]{:S(2)}) collective-permute-start(f32[1,16,32]{2,1,0:T(8,128)S(1)} %get-tuple-element.240), channel_id=1, source_target_pairs={{4,0},{8,4},{12,8},{16,12},{20,16},{24,20},{28,24},{32,28},{36,32}... | collective-permute-start | bytes 6152 | tf_op jit(solution)/shard_map/ppermute | solution.py:22
  74.3 83.9 %collective-permute-start.25 = (f32[1,16,32]{2,1,0:T(8,128)}, f32[1,16,32]{2,1,0:T(8,128)}, u32[]{:S(2)}, u32[]{:S(2)}) collective-permute-start(f32[1,16,32]{2,1,0:T(8,128)} %get-tuple-element.241), channel_id=1, source_target_pairs={{0,4},{4,8},{8,12},{12,16},{16,20},{20,24},{24,28},{28,32},{32,36}... | collective-permute-start | bytes 6152 | tf_op jit(solution)/shard_map/ppermute | solution.py:19
  156.3 13.8 %collective-permute-start.13 = (f32[1,32,64]{2,1,0:T(8,128)}, f32[1,32,64]{2,1,0:T(8,128)S(1)}, u32[]{:S(2)}, u32[]{:S(2)}) collective-permute-start(f32[1,32,64]{2,1,0:T(8,128)} %get-tuple-element.181), channel_id=1, source_target_pairs={{0,4},{4,8},{8,12},{12,16},{16,20},{20,24},{24,28},{28,32},{32,36}... | collective-permute-start | bytes 24584 | tf_op jit(solution)/shard_map/ppermute | solution.py:19
  159.5 199.1 %collective-permute-start.26 = (f32[6,1,32]{2,1,0:T(1,128)}, f32[6,1,32]{2,1,0:T(1,128)}, u32[]{:S(2)}, u32[]{:S(2)}) collective-permute-start(f32[6,1,32]{2,1,0:T(1,128)} %get-tuple-element.211), channel_id=1, source_target_pairs={{1,0},{2,1},{3,2},{5,4},{6,5},{7,6},{9,8},{10,9},{11,10},{13,12},{... | collective-permute-start | bytes 2312 | tf_op jit(solution)/shard_map/ppermute | solution.py:22
  162.7 195.9 %collective-permute-start.27 = (f32[6,1,32]{2,1,0:T(1,128)}, f32[6,1,32]{2,1,0:T(1,128)}, u32[]{:S(2)}, u32[]{:S(2)}) collective-permute-start(f32[6,1,32]{2,1,0:T(1,128)} %get-tuple-element.210), channel_id=1, source_target_pairs={{0,1},{1,2},{2,3},{4,5},{5,6},{6,7},{8,9},{9,10},{10,11},{12,13},{... | collective-permute-start | bytes 2312 | tf_op jit(solution)/shard_map/ppermute | solution.py:19
  164.2 12.1 %collective-permute-start.2 = (f32[18,1,128]{2,1,0:T(1,128)S(1)}, f32[18,1,128]{2,1,0:T(1,128)S(1)}, u32[]{:S(2)}, u32[]{:S(2)}) collective-permute-start(f32[18,1,128]{2,1,0:T(1,128)S(1)} %get-tuple-element.118), channel_id=1, source_target_pairs={{1,0},{2,1},{3,2},{5,4},{6,5},{7,6},{9,8},{10,9},{11,10},{13,12},{... | collective-permute-start | bytes 27656 | tf_op jit(solution)/shard_map/ppermute | solution.py:22
  168.8 7.5 %collective-permute-start.3 = (f32[18,1,128]{2,1,0:T(1,128)S(1)}, f32[18,1,128]{2,1,0:T(1,128)S(1)}, u32[]{:S(2)}, u32[]{:S(2)}) collective-permute-start(f32[18,1,128]{2,1,0:T(1,128)S(1)} %get-tuple-element.117), channel_id=1, source_target_pairs={{0,1},{1,2},{2,3},{4,5},{5,6},{6,7},{8,9},{9,10},{10,11},{12,13},{... | collective-permute-start | bytes 27656 | tf_op jit(solution)/shard_map/ppermute | solution.py:19
  170.7 138.3 %collective-permute-start.14 = (f32[10,1,64]{2,1,0:T(1,128)}, f32[10,1,64]{2,1,0:T(1,128)}, u32[]{:S(2)}, u32[]{:S(2)}) collective-permute-start(f32[10,1,64]{2,1,0:T(1,128)} %get-tuple-element.151), channel_id=1, source_target_pairs={{1,0},{2,1},{3,2},{5,4},{6,5},{7,6},{9,8},{10,9},{11,10},{13,12},{... | collective-permute-start | bytes 7688 | tf_op jit(solution)/shard_map/ppermute | solution.py:22
  188.8 10.4 %collective-permute-start.5 = (f32[1,64,128]{1,0,2:T(1,128)}, f32[1,64,128]{1,0,2:T(1,128)}, u32[]{:S(2)}, u32[]{:S(2)}) collective-permute-start(f32[1,64,128]{1,0,2:T(1,128)} %get-tuple-element.88), channel_id=1, source_target_pairs={{0,4},{4,8},{8,12},{12,16},{16,20},{20,24},{24,28},{28,32},{32,36}... | collective-permute-start | bytes 98312 | tf_op jit(solution)/shard_map/ppermute | solution.py:19
  190.7 9.4 %collective-permute-start.4 = (f32[1,64,128]{1,0,2:T(1,128)}, f32[1,64,128]{1,0,2:T(1,128)}, u32[]{:S(2)}, u32[]{:S(2)}) collective-permute-start(f32[1,64,128]{1,0,2:T(1,128)} %get-tuple-element.87), channel_id=1, source_target_pairs={{4,0},{8,4},{12,8},{16,12},{20,16},{24,20},{28,24},{32,28},{36,32}... | collective-permute-start | bytes 98312 | tf_op jit(solution)/shard_map/ppermute | solution.py:22
  223.4 10.4 %collective-permute-start.9 = (f32[1,64,128]{1,0,2:T(1,128)}, f32[1,64,128]{1,0,2:T(1,128)}, u32[]{:S(2)}, u32[]{:S(2)}) collective-permute-start(f32[1,64,128]{1,0,2:T(1,128)} %get-tuple-element.82), channel_id=1, source_target_pairs={{0,4},{4,8},{8,12},{12,16},{16,20},{20,24},{24,28},{28,32},{32,36}... | collective-permute-start | bytes 98312 | tf_op jit(solution)/shard_map/ppermute | solution.py:19
  225.3 9.4 %collective-permute-start.8 = (f32[1,64,128]{1,0,2:T(1,128)}, f32[1,64,128]{1,0,2:T(1,128)}, u32[]{:S(2)}, u32[]{:S(2)}) collective-permute-start(f32[1,64,128]{1,0,2:T(1,128)} %get-tuple-element.81), channel_id=1, source_target_pairs={{4,0},{8,4},{12,8},{16,12},{20,16},{24,20},{28,24},{32,28},{36,32}... | collective-permute-start | bytes 98312 | tf_op jit(solution)/shard_map/ppermute | solution.py:22
  236.5 5.8 collective-permute-start.10
  242.4 66.6 %collective-permute-start.15 = (f32[10,1,64]{2,1,0:T(1,128)}, f32[10,1,64]{2,1,0:T(1,128)}, u32[]{:S(2)}, u32[]{:S(2)}) collective-permute-start(f32[10,1,64]{2,1,0:T(1,128)} %get-tuple-element.150), channel_id=1, source_target_pairs={{0,1},{1,2},{2,3},{4,5},{5,6},{6,7},{8,9},{9,10},{10,11},{12,13},{... | collective-permute-start | bytes 7688 | tf_op jit(solution)/shard_map/ppermute | solution.py:19
  313.5 7.2 %collective-permute-start.17 = (f32[1,32,64]{2,1,0:T(8,128)S(1)}, f32[1,32,64]{2,1,0:T(8,128)S(1)}, u32[]{:S(2)}, u32[]{:S(2)}) collective-permute-start(f32[1,32,64]{2,1,0:T(8,128)S(1)} %get-tuple-element.174), channel_id=1, source_target_pairs={{0,4},{4,8},{8,12},{12,16},{16,20},{20,24},{24,28},{28,32},{32,36}... | collective-permute-start | bytes 24584 | tf_op jit(solution)/shard_map/ppermute | solution.py:19
  332.3 7.2 %collective-permute-start.21 = (f32[1,32,64]{2,1,0:T(8,128)S(1)}, f32[1,32,64]{2,1,0:T(8,128)S(1)}, u32[]{:S(2)}, u32[]{:S(2)}) collective-permute-start(f32[1,32,64]{2,1,0:T(8,128)S(1)} %get-tuple-element.168), channel_id=1, source_target_pairs={{0,4},{4,8},{8,12},{12,16},{16,20},{20,24},{24,28},{28,32},{32,36}... | collective-permute-start | bytes 24584 | tf_op jit(solution)/shard_map/ppermute | solution.py:19
  361.6 7.1 %collective-permute-start.29 = (f32[1,16,32]{2,1,0:T(8,128)S(1)}, f32[1,16,32]{2,1,0:T(8,128)S(1)}, u32[]{:S(2)}, u32[]{:S(2)}) collective-permute-start(f32[1,16,32]{2,1,0:T(8,128)S(1)} %get-tuple-element.234), channel_id=1, source_target_pairs={{0,4},{4,8},{8,12},{12,16},{16,20},{20,24},{24,28},{28,32},{32,36}... | collective-permute-start | bytes 6152 | tf_op jit(solution)/shard_map/ppermute | solution.py:19
  379.0 7.1 %collective-permute-start.33 = (f32[1,16,32]{2,1,0:T(8,128)S(1)}, f32[1,16,32]{2,1,0:T(8,128)S(1)}, u32[]{:S(2)}, u32[]{:S(2)}) collective-permute-start(f32[1,16,32]{2,1,0:T(8,128)S(1)} %get-tuple-element.228), channel_id=1, source_target_pairs={{0,4},{4,8},{8,12},{12,16},{16,20},{20,24},{24,28},{28,32},{32,36}... | collective-permute-start | bytes 6152 | tf_op jit(solution)/shard_map/ppermute | solution.py:19
  520.2 7.5 %collective-permute-start.36 = (f32[1,16,32]{2,1,0:T(8,128)S(1)}, f32[1,16,32]{2,1,0:T(8,128)S(1)}, u32[]{:S(2)}, u32[]{:S(2)}) collective-permute-start(f32[1,16,32]{2,1,0:T(8,128)S(1)} %get-tuple-element.223), channel_id=1, source_target_pairs={{4,0},{8,4},{12,8},{16,12},{20,16},{24,20},{28,24},{32,28},{36,32}... | collective-permute-start | bytes 6152 | tf_op jit(solution)/shard_map/ppermute | solution.py:22
  525.7 7.1 %collective-permute-start.37 = (f32[1,16,32]{2,1,0:T(8,128)S(1)}, f32[1,16,32]{2,1,0:T(8,128)S(1)}, u32[]{:S(2)}, u32[]{:S(2)}) collective-permute-start(f32[1,16,32]{2,1,0:T(8,128)S(1)} %get-tuple-element.222), channel_id=1, source_target_pairs={{0,4},{4,8},{8,12},{12,16},{16,20},{20,24},{24,28},{28,32},{32,36}... | collective-permute-start | bytes 6152 | tf_op jit(solution)/shard_map/ppermute | solution.py:19
  543.1 7.1 %collective-permute-start.41 = (f32[1,16,32]{2,1,0:T(8,128)S(1)}, f32[1,16,32]{2,1,0:T(8,128)S(1)}, u32[]{:S(2)}, u32[]{:S(2)}) collective-permute-start(f32[1,16,32]{2,1,0:T(8,128)S(1)} %get-tuple-element.216), channel_id=1, source_target_pairs={{0,4},{4,8},{8,12},{12,16},{16,20},{20,24},{24,28},{28,32},{32,36}... | collective-permute-start | bytes 6152 | tf_op jit(solution)/shard_map/ppermute | solution.py:19
  565.4 7.2 %collective-permute-start.45 = (f32[1,32,64]{2,1,0:T(8,128)S(1)}, f32[1,32,64]{2,1,0:T(8,128)S(1)}, u32[]{:S(2)}, u32[]{:S(2)}) collective-permute-start(f32[1,32,64]{2,1,0:T(8,128)S(1)} %get-tuple-element.162), channel_id=1, source_target_pairs={{0,4},{4,8},{8,12},{12,16},{16,20},{20,24},{24,28},{28,32},{32,36}... | collective-permute-start | bytes 24584 | tf_op jit(solution)/shard_map/ppermute | solution.py:19
  584.7 7.2 %collective-permute-start.49 = (f32[1,32,64]{2,1,0:T(8,128)S(1)}, f32[1,32,64]{2,1,0:T(8,128)S(1)}, u32[]{:S(2)}, u32[]{:S(2)}) collective-permute-start(f32[1,32,64]{2,1,0:T(8,128)S(1)} %get-tuple-element.156), channel_id=1, source_target_pairs={{0,4},{4,8},{8,12},{12,16},{16,20},{20,24},{24,28},{28,32},{32,36}... | collective-permute-start | bytes 24584 | tf_op jit(solution)/shard_map/ppermute | solution.py:19
  605.2 11.7 %collective-permute-start.53 = (f32[1,64,128]{1,0,2:T(1,128)S(1)}, f32[1,64,128]{1,0,2:T(1,128)S(1)}, u32[]{:S(2)}, u32[]{:S(2)}) collective-permute-start(f32[1,64,128]{1,0,2:T(1,128)S(1)} %get-tuple-element.76), channel_id=1, source_target_pairs={{0,4},{4,8},{8,12},{12,16},{16,20},{20,24},{24,28},{28,32},{32,36}... | collective-permute-start | bytes 98312 | tf_op jit(solution)/shard_map/ppermute | solution.py:19
  607.3 9.7 %collective-permute-start.52 = (f32[1,64,128]{1,0,2:T(1,128)S(1)}, f32[1,64,128]{1,0,2:T(1,128)S(1)}, u32[]{:S(2)}, u32[]{:S(2)}) collective-permute-start(f32[1,64,128]{1,0,2:T(1,128)S(1)} %get-tuple-element.75), channel_id=1, source_target_pairs={{4,0},{8,4},{12,8},{16,12},{20,16},{24,20},{28,24},{32,28},{36,32}... | collective-permute-start | bytes 98312 | tf_op jit(solution)/shard_map/ppermute | solution.py:22
  638.5 11.6 %collective-permute-start.57 = (f32[1,64,128]{1,0,2:T(1,128)S(1)}, f32[1,64,128]{1,0,2:T(1,128)S(1)}, u32[]{:S(2)}, u32[]{:S(2)}) collective-permute-start(f32[1,64,128]{1,0,2:T(1,128)S(1)} %get-tuple-element.70), channel_id=1, source_target_pairs={{0,4},{4,8},{8,12},{12,16},{16,20},{20,24},{24,28},{28,32},{32,36}... | collective-permute-start | bytes 98312 | tf_op jit(solution)/shard_map/ppermute | solution.py:19
  640.4 9.8 %collective-permute-start.56 = (f32[1,64,128]{1,0,2:T(1,128)S(1)}, f32[1,64,128]{1,0,2:T(1,128)S(1)}, u32[]{:S(2)}, u32[]{:S(2)}) collective-permute-start(f32[1,64,128]{1,0,2:T(1,128)S(1)} %get-tuple-element.69), channel_id=1, source_target_pairs={{4,0},{8,4},{12,8},{16,12},{20,16},{24,20},{28,24},{32,28},{36,32}... | collective-permute-start | bytes 98312 | tf_op jit(solution)/shard_map/ppermute | solution.py:22
  671.6 11.6 %collective-permute-start.61 = (f32[1,64,128]{1,0,2:T(1,128)S(1)}, f32[1,64,128]{1,0,2:T(1,128)S(1)}, u32[]{:S(2)}, u32[]{:S(2)}) collective-permute-start(f32[1,64,128]{1,0,2:T(1,128)S(1)} %get-tuple-element.64), channel_id=1, source_target_pairs={{0,4},{4,8},{8,12},{12,16},{16,20},{20,24},{24,28},{28,32},{32,36}... | collective-permute-start | bytes 98312 | tf_op jit(solution)/shard_map/ppermute | solution.py:19
  673.5 9.8 %collective-permute-start.60 = (f32[1,64,128]{1,0,2:T(1,128)S(1)}, f32[1,64,128]{1,0,2:T(1,128)S(1)}, u32[]{:S(2)}, u32[]{:S(2)}) collective-permute-start(f32[1,64,128]{1,0,2:T(1,128)S(1)} %get-tuple-element.63), channel_id=1, source_target_pairs={{4,0},{8,4},{12,8},{16,12},{20,16},{24,20},{28,24},{32,28},{36,32}... | collective-permute-start | bytes 98312 | tf_op jit(solution)/shard_map/ppermute | solution.py:22
  (95 other events, 1360.9 us)
where the time goes:
time: 721 us; the launch traced here: 708 us
  local copies, waits for them, and re-layouts  207 us (29%)
  starting transfers between devices  161 us (22%)
  other arithmetic  129 us (18%)
  blocking collectives  120 us (17%)
  waiting for transfers between devices  87.3 us (12%)
    ppermute x32, starting transfers between devices, with_halo(): lax.ppermute(lax.slice_in_dim(block, 0, width, axis=dim), axis, backward)  106 us
    reshape x7, local copies, waits for them, and re-layouts, coarsen(): return jnp.mean(values.reshape(split_shape), axis=(1, 3, 5))  92.7 us
    ppermute x32, waiting for transfers between devices, with_halo(): lax.ppermute(lax.slice_in_dim(block, block.shape[dim] - width, None, axis...  87.2 us
    all_gather x1, blocking collectives, agglomerate(): lax.all_gather(coarse_conduct[None], ('gx', 'gy'), axis=0, tiled=True)  61.4 us
    all_gather x1, blocking collectives, agglomerate(): lax.all_gather(coarse_source[None], ('gx', 'gy'), axis=0, tiled=True)  58.5 us
    ppermute x32, starting transfers between devices, with_halo(): lax.ppermute(lax.slice_in_dim(block, block.shape[dim] - width, None, axis...  54.6 us
    unnamed x143, local copies, waits for them, and re-layouts  41.2 us
    reduce_sum x13, other arithmetic, coarsen(): return jnp.mean(values.reshape(split_shape), axis=(1, 3, 5))  39.3 us
  transfers between devices with their start and end apart: 64, of which 21 were waited for; matrix products, arithmetic and copies ran while one was open for 29% of the time, Pallas kernels for 0%

commit v1 on v0

v1 whole, which is shorter than its diff:
```python
import functools

import jax
import jax.numpy as jnp
from jax import lax
from jax.experimental import pallas as pl
from jax.experimental.pallas import tpu as pltpu
from jax.sharding import PartitionSpec as P

SWEEPS_COARSE = 16
DAMP = 0.8
KEEP = 1.0 - DAMP
H0 = 0.0002

NX, NY, NZ = 16, 64, 128
F32 = jnp.float32
VMEM = pl.BlockSpec(memory_space=pltpu.VMEM)


def call(body, outs, scratch, args, name, vmem):
    return pl.pallas_call(
        body,
        out_shape=[jax.ShapeDtypeStruct(s, F32) for s in outs],
        in_specs=[VMEM] * len(args),
        out_specs=[VMEM] * len(outs),
        scratch_shapes=[pltpu.VMEM(s, F32) for s in scratch],
        compiler_params=pltpu.CompilerParams(vmem_limit_bytes=vmem * 2**20),
        name=name,
    )(*args)


def recip(t):
    r = pl.reciprocal(t, approx=True)
    r = r * (2.0 - t * r)
    return r * (2.0 - t * r)


def harmonic(a, b):
    return (2.0 * a) * b * recip(jnp.maximum(a + b, 1e-30))


def lane(shape):
    return lax.broadcasted_iota(jnp.int32, shape, len(shape) - 1)


def lroll(v, shift):
    return pltpu.roll(v, shift % 128, v.ndim - 1)


def pair_lanes(v, s):
    first = (lane(v.shape) // s) % 2 == 0
    return v + jnp.where(first, lroll(v, -s), lroll(v, s))


def rows(lo, hi, body, unroll=1):
    def step(x, carry):
        body(x)
        return carry

    lax.fori_loop(lo, hi, step, 0, unroll=unroll)


def chunks(ys, ye, size):
    return [(y, min(size, ye - y)) for y in range(ys, ye, size)]


class Level:
    def __init__(self, depth, c, b, fx, fy, fz, fzm, w, ys, ye, size):
        self.h = H0 * 4.0**depth
        self.s = 2**depth
        self.c, self.b, self.fx, self.fy, self.fz, self.fzm, self.w = c, b, fx, fy, fz, fzm, w
        self.parts = chunks(ys, ye, size)

    def faces(self, lo, hi):
        def body(x):
            for y, n in self.parts:
                c = self.c[x, pl.ds(y, n), :]
                self.fx[x, pl.ds(y, n), :] = harmonic(c, self.c[x + 1, pl.ds(y, n), :])
                self.fy[x, pl.ds(y, n), :] = harmonic(c, self.c[x, pl.ds(y + 1, n), :])
                fz = harmonic(c, lroll(c, -self.s))
                self.fz[x, pl.ds(y, n), :] = fz
                self.fzm[x, pl.ds(y, n), :] = lroll(fz, self.s)

        rows(lo, hi, body)

    def weights(self, lo, hi, start=None):
        def body(x):
            for y, n in self.parts:
                here = pl.ds(y, n)
                d = self.fx[x, here, :] + self.fx[x - 1, here, :]
                d = d + self.fy[x, here, :] + self.fy[x, pl.ds(y - 1, n), :]
                d = d + self.fz[x, here, :] + self.fzm[x, here, :]
                w = DAMP * recip(self.h + d)
                self.w[x, here, :] = w
                if start is not None:
                    start[x, here, :] = w * self.b[x, here, :]

        rows(lo, hi, body)

    def flux(self, u, x, y, n):
        here = pl.ds(y, n)
        v = u[x, here, :]
        acc = self.fx[x, here, :] * u[x + 1, here, :]
        acc = acc + self.fx[x - 1, here, :] * u[x - 1, here, :]
        acc = acc + self.fy[x, here, :] * u[x, pl.ds(y + 1, n), :]
        acc = acc + self.fy[x, pl.ds(y - 1, n), :] * u[x, pl.ds(y - 1, n), :]
        acc = acc + self.fz[x, here, :] * lroll(v, -self.s)
        acc = acc + self.fzm[x, here, :] * lroll(v, self.s)
        return v, acc

    def sweep(self, u, out, lo, hi):
        def body(x):
            for y, n in self.parts:
                here = pl.ds(y, n)
                v, acc = self.flux(u, x, y, n)
                out[x, here, :] = KEEP * v + self.w[x, here, :] * (self.b[x, here, :] + acc)

        rows(lo, hi, body)

    def residual(self, u, x, y, n):
        here = pl.ds(y, n)
        v = u[x, here, :]
        r = self.b[x, here, :] - self.h * v
        r = r + self.fx[x, here, :] * (u[x + 1, here, :] - v)
        r = r + self.fx[x - 1, here, :] * (u[x - 1, here, :] - v)
        r = r + self.fy[x, here, :] * (u[x, pl.ds(y + 1, n), :] - v)
        r = r + self.fy[x, pl.ds(y - 1, n), :] * (u[x, pl.ds(y - 1, n), :] - v)
        r = r + self.fz[x, here, :] * (lroll(v, -self.s) - v)
        return r + self.fzm[x, here, :] * (lroll(v, self.s) - v)

    def restrict(self, u, tmp, out, count, x_from, x_to, rows_from):
        def body(k):
            x = x_from + 2 * k
            for y, n in self.parts:
                tmp[pl.ds(y, n), :] = self.residual(u, x, y, n) + self.residual(u, x + 1, y, n)
            half = tmp.shape[0] // 2
            t = tmp[pl.ds(0, half, stride=2), :] + tmp[pl.ds(1, half, stride=2), :]
            out[x_to + k, pl.ds(8, half), :] = 0.5 * pair_lanes(t, self.s)

        rows(0, count, body)

    def restrict_c(self, tmp, out, count, x_from, x_to):
        def body(k):
            x = x_from + 2 * k
            tmp[...] = self.c[x] + self.c[x + 1]
            half = tmp.shape[0] // 2
            t = tmp[pl.ds(0, half, stride=2), :] + tmp[pl.ds(1, half, stride=2), :]
            out[x_to + k, pl.ds(8, half), :] = 0.125 * pair_lanes(t, self.s)

        rows(0, count, body)


def odd(axis):
    return lax.axis_index(axis) % 2


def begin_kernel(source, density, drag, porous, cond, ypack0, ypack1):
    o = odd("gy")
    at0 = pl.multiple_of((1 - o) * (NY - 8), 8)
    at1 = pl.multiple_of(o * (NY - 8), 8)

    def body(x):
        c = recip(density[x] * (1.0 + drag[x] * porous[...]))
        cond[x] = c
        ypack0[x] = cond[x, pl.ds(at0, 8), :]
        ypack1[x] = cond[x, pl.ds(at1, 8), :]
        ypack0[NX + x] = source[x, pl.ds(at0, 8), :]
        ypack1[NX + x] = source[x, pl.ds(at1, 8), :]

    rows(0, NX, body)


def edge_kernel(cond, source, y0, y1, xpack0, xpack1):
    ox, oy = odd("gx"), odd("gy")
    at0 = pl.multiple_of((1 - oy) * (NY + 8), 8)
    at1 = pl.multiple_of(oy * (NY + 8), 8)

    def put(pack, row, field, x, base):
        pack[row, pl.ds(8, NY), :] = field[x]
        pack[row, pl.ds(at0, 8), :] = y0[base + x]
        pack[row, pl.ds(at1, 8), :] = y1[base + x]

    def body_c(k):
        put(xpack0, k, cond, k + (1 - ox) * (NX - 11), 0)
        put(xpack1, k, cond, k + ox * (NX - 11), 0)

    def body_b(k):
        put(xpack0, 11 + k, source, k + (1 - ox) * (NX - 10), NX)
        put(xpack1, 11 + k, source, k + ox * (NX - 10), NX)

    rows(0, 11, body_c)
    rows(0, 10, body_b)


X0, Y0 = 12, 16
X1, Y1 = 6, 16
X2, Y2 = 6, 16


def down_kernel(
    cond, source, y0, y1, x0, x1,
    c0_out, b0_out, u0_out, c1, b1, u1, c2, b2, ypack0, ypack1,
    c, b, fx, fy, fz, fzm, w, ua, ub, tmp, gx_, gy_, gz_, gzm_, gw_, ga_, tmp1,
):
    ox, oy = odd("gx"), odd("gy")
    at0 = pl.multiple_of(8 + (1 - oy) * (NY + 8), 8)
    at1 = pl.multiple_of(8 + oy * (NY + 8), 8)

    def own(x):
        c[X0 + x, pl.ds(Y0, NY), :] = cond[x]
        c[X0 + x, pl.ds(at0, 8), :] = y0[x]
        c[X0 + x, pl.ds(at1, 8), :] = y1[x]
        b[X0 + x, pl.ds(Y0, NY), :] = source[x]
        b[X0 + x, pl.ds(at0, 8), :] = y0[NX + x]
        b[X0 + x, pl.ds(at1, 8), :] = y1[NX + x]

    rows(0, NX, own)

    def halo_c(k):
        c[k + 1 + (1 - ox) * (11 + NX), pl.ds(8, 80), :] = x0[k]
        c[k + 1 + ox * (11 + NX), pl.ds(8, 80), :] = x1[k]

    def halo_b(k):
        b[k + 2 + (1 - ox) * (10 + NX), pl.ds(8, 80), :] = x0[11 + k]
        b[k + 2 + ox * (10 + NX), pl.ds(8, 80), :] = x1[11 + k]

    rows(0, 11, halo_c)
    rows(0, 10, halo_b)
    zero = jnp.zeros((8, NZ), F32)

    def pads(x):
        c[x, pl.ds(0, 8), :] = zero
        c[x, pl.ds(88, 8), :] = zero
        fy[x, pl.ds(0, 8), :] = zero

    rows(0, 40, pads)

    top = Level(0, c, b, fx, fy, fz, fzm, w, 8, 88, 40)
    top.faces(1, 39)
    top.weights(2, 38, ua)
    top.sweep(ua, ub, 3, 37)

    def clear1(x):
        for ref in (c1, b1, u1):
            ref[x] = jnp.zeros((64, NZ), F32)
        gy_[x, pl.ds(0, 8), :] = zero

    rows(0, 20, clear1)

    def clear2(x):
        for ref in (c2, b2):
            ref[x] = jnp.zeros((48, NZ), F32)

    rows(0, 16, clear2)
    tmp[pl.ds(0, 8), :] = zero
    tmp[pl.ds(88, 8), :] = zero
    tmp1[pl.ds(0, 8), :] = zero
    tmp1[pl.ds(56, 8), :] = zero
    top.restrict(ub, tmp, b1, 16, 4, 2, None)
    top.restrict_c(tmp, c1, 18, 2, 1)

    def keep(x):
        c0_out[x] = c[X0 - 4 + x]
        b0_out[x] = b[X0 - 4 + x]
        u0_out[x] = ub[X0 - 4 + x]

    rows(0, 24, keep)

    mid = Level(1, c1, b1, gx_, gy_, gz_, gzm_, gw_, 8, 56, 48)
    mid.faces(1, 19)
    mid.weights(2, 18, ga_)
    mid.sweep(ga_, u1, 3, 17)
    mid.restrict(u1, tmp1, b2, 6, 4, 5, None)
    mid.restrict_c(tmp1, c2, 8, 2, 4)

    high, low = 28, 0
    e0 = Y1 + (1 - oy) * high
    e1 = Y1 + oy * high

    def edge1(x):
        ypack0[x, pl.ds(0, 4), :] = u1[X1 + x, pl.ds(e0, 4), :]
        ypack1[x, pl.ds(0, 4), :] = u1[X1 + x, pl.ds(e1, 4), :]
        ypack0[x, pl.ds(4, 4), :] = b1[X1 + x, pl.ds(e0, 4), :]
        ypack1[x, pl.ds(4, 4), :] = b1[X1 + x, pl.ds(e1, 4), :]

    rows(0, 8, edge1)
    f0 = pl.multiple_of(Y2 + (1 - oy) * 8, 8)
    f1 = pl.multiple_of(Y2 + oy * 8, 8)
    for x in range(6):
        ypack0[8 + x] = b2[X2 - 1 + x, pl.ds(f0, 8), :]
        ypack1[8 + x] = b2[X2 - 1 + x, pl.ds(f1, 8), :]
    for x in range(8):
        ypack0[14 + x] = c2[X2 - 2 + x, pl.ds(f0, 8), :]
        ypack1[14 + x] = c2[X2 - 2 + x, pl.ds(f1, 8), :]


def set_y1(u1, b1, y0, y1, oy, lo, hi):
    a0 = Y1 - 4 + (1 - oy) * 36
    a1 = Y1 - 4 + oy * 36

    def body(x):
        u1[X1 + x, pl.ds(a0, 4), :] = y0[x, pl.ds(0, 4), :]
        u1[X1 + x, pl.ds(a1, 4), :] = y1[x, pl.ds(0, 4), :]
        if b1 is not None:
            b1[X1 + x, pl.ds(a0, 4), :] = y0[x, pl.ds(4, 4), :]
            b1[X1 + x, pl.ds(a1, 4), :] = y1[x, pl.ds(4, 4), :]

    rows(lo, hi, body)


def set_y2(c2, b2, y0, y1, oy):
    a0 = pl.multiple_of(Y2 - 8 + (1 - oy) * 24, 8)
    a1 = pl.multiple_of(Y2 - 8 + oy * 24, 8)
    for x in range(6):
        b2[X2 - 1 + x, pl.ds(a0, 8), :] = y0[8 + x]
        b2[X2 - 1 + x, pl.ds(a1, 8), :] = y1[8 + x]
    for x in range(8):
        c2[X2 - 2 + x, pl.ds(a0, 8), :] = y0[14 + x]
        c2[X2 - 2 + x, pl.ds(a1, 8), :] = y1[14 + x]


def edge2_kernel(u1_in, c2_in, b2_in, y0, y1, u1, c2, b2, xpack0, xpack1):
    ox, oy = odd("gx"), odd("gy")

    def copy1(x):
        u1[x] = u1_in[x]

    def copy2(x):
        c2[x] = c2_in[x]
        b2[x] = b2_in[x]

    rows(0, 20, copy1)
    rows(0, 16, copy2)
    set_y1(u1, None, y0, y1, oy, 0, 8)
    set_y2(c2, b2, y0, y1, oy)
    for pack, last in ((xpack0, 1 - ox), (xpack1, ox)):
        for k in range(4):
            pack[pl.ds(k * 48, 48), :] = u1[X1 + k + last * 4, pl.ds(8, 48), :]
        for k in range(5):
            pack[pl.ds(192 + k * 32, 32), :] = b2[X2 + k - last, pl.ds(8, 32), :]
        for k in range(6):
            pack[pl.ds(352 + k * 32, 32), :] = c2[X2 + k - 2 * last, pl.ds(8, 32), :]


def one_hot(shape, f):
    i = lax.broadcasted_iota(jnp.int32, shape, 0)
    j = lax.broadcasted_iota(jnp.int32, shape, 1)
    return jnp.where(f(i, j), 1.0, 0.0).astype(F32)


def exact_dot(a, b):
    return jnp.dot(a, b, precision=lax.Precision.HIGHEST, preferred_element_type=F32)


def level2_kernel(
    u1_in, c2_in, b2_in, x0, x1,
    u1, c2, b2, u2, gather,
    fx, fy, fz, fzm, w, ua, tmp, b3, c3,
):
    ox = odd("gx")
    zero = jnp.zeros((8, NZ), F32)

    def copy1(x):
        u1[x] = u1_in[x]

    def copy2(x):
        c2[x] = c2_in[x]
        b2[x] = b2_in[x]
        u2[x] = jnp.zeros((48, NZ), F32)
        fy[x, pl.ds(0, 8), :] = zero

    rows(0, 20, copy1)
    rows(0, 16, copy2)
    for pack, up in ((x0, 1 - ox), (x1, ox)):
        for k in range(4):
            u1[X1 - 4 + k + up * 12, pl.ds(8, 48), :] = pack[pl.ds(k * 48, 48), :]
        for k in range(5):
            b2[X2 - 5 + k + up * 9, pl.ds(8, 32), :] = pack[pl.ds(192 + k * 32, 32), :]
        for k in range(6):
            c2[X2 - 6 + k + up * 10, pl.ds(8, 32), :] = pack[pl.ds(352 + k * 32, 32), :]

    low = Level(2, c2, b2, fx, fy, fz, fzm, w, 8, 40, 32)
    low.faces(0, 15)
    low.weights(1, 15, ua)
    low.sweep(ua, u2, 2, 14)
    tmp[pl.ds(0, 8), :] = zero
    tmp[pl.ds(40, 8), :] = zero
    low.restrict(u2, tmp, b3, 2, X2, 0, None)
    low.restrict_c(tmp, c3, 2, X2, 0)
    both = jnp.concatenate(
        [b3[0, pl.ds(16, 8), :], b3[1, pl.ds(16, 8), :], c3[0, pl.ds(16, 8), :], c3[1, pl.ds(16, 8), :]], 0
    )
    spread = exact_dot(both, one_hot((NZ, NZ), lambda i, j: i == 8 * (j % 16)))
    shape = (8, NZ)
    mine = lane(shape) // 16 == lax.broadcasted_iota(jnp.int32, shape, 0)
    packed = [
        jnp.sum(jnp.where(mine, spread[8 * k : 8 * k + 8], 0.0), axis=0, keepdims=True) for k in range(4)
    ]
    eight = jnp.concatenate(packed + packed, 0)

    def body(k):
        gather[pl.ds(pl.multiple_of(8 * k, 8), 8), :] = eight

    rows(0, 64, body, 8)


class Whole:
    def __init__(self, depth, b, c):
        self.h = H0 * 4.0**depth
        self.s = 2 ** (depth - 3)
        self.st = 16 * self.s
        self.b = b
        n = c.shape[0]
        sub = lax.broadcasted_iota(jnp.int32, (1,) + c.shape[1:], 2)
        up = self.xp(c)
        end = jnp.where(sub == 7, 0.0, up[n - 1 :])
        up = jnp.concatenate([up[: n - 1], end], 0) if n > 1 else end
        self.fxp = harmonic(c, up)
        up = self.yp(c)
        last = up[:, 3:]
        last = jnp.where(lane(last.shape) >= 128 - self.st, 0.0, last)
        self.fyp = harmonic(c, jnp.concatenate([up[:, :3], last], 1))
        self.fzp = harmonic(c, self.zp(c))
        self.fxm, self.fym, self.fzm = self.xm(self.fxp), self.ym(self.fyp), self.zm(self.fzp)
        d = self.h + self.fxp + self.fxm + self.fyp + self.fym + self.fzp + self.fzm
        self.w = DAMP * recip(d)

    def xp(self, v):
        wrap = pltpu.roll(v[:1], 7, 2)
        return jnp.concatenate([v[1:], wrap], 0) if v.shape[0] > 1 else wrap

    def xm(self, v):
        n = v.shape[0]
        wrap = pltpu.roll(v[n - 1 :], 1, 2)
        return jnp.concatenate([wrap, v[: n - 1]], 0) if n > 1 else wrap

    def yp(self, v):
        w = v if self.st == 128 else lroll(v, -self.st)
        far = jnp.concatenate([w[:, 1:], w[:, :1]], 1)
        return far if self.st == 128 else jnp.where(lane(v.shape) < 128 - self.st, w, far)

    def ym(self, v):
        w = v if self.st == 128 else lroll(v, self.st)
        far = jnp.concatenate([w[:, 3:], w[:, :3]], 1)
        return far if self.st == 128 else jnp.where(lane(v.shape) >= self.st, w, far)

    def zp(self, v):
        s = self.s
        return jnp.where(lane(v.shape) % 16 < 16 - s, lroll(v, -s), lroll(v, 16 - s))

    def zm(self, v):
        s = self.s
        return self.zp(v) if s == 8 else jnp.where(lane(v.shape) % 16 >= s, lroll(v, s), lroll(v, s - 16))

    def flux(self, v):
        acc = self.fxp * self.xp(v) + self.fxm * self.xm(v)
        acc = acc + self.fyp * self.yp(v) + self.fym * self.ym(v)
        return acc + self.fzp * self.zp(v) + self.fzm * self.zm(v)

    def sweep(self, v):
        return KEEP * v + self.w * (self.b + self.flux(v))

    def residual(self, v):
        r = self.b - self.h * v
        r = r + self.fxp * (self.xp(v) - v) + self.fxm * (self.xm(v) - v)
        r = r + self.fyp * (self.yp(v) - v) + self.fym * (self.ym(v) - v)
        return r + self.fzp * (self.zp(v) - v) + self.fzm * (self.zm(v) - v)

    def coarse(self, v, scale):
        v = jnp.concatenate([v[2 * k : 2 * k + 1] + v[2 * k + 1 : 2 * k + 2] for k in range(v.shape[0] // 2)], 0)
        return scale * pair_lanes(pair_lanes(v, self.s), self.st)


def whole_cycle(depth, b, c):
    level = Whole(depth, b, c)
    v = level.w * b
    if depth == 6:
        for _ in range(SWEEPS_COARSE - 1):
            v = level.sweep(v)
        return v
    v = level.sweep(v)
    below = whole_cycle(depth + 1, level.coarse(level.residual(v), 0.5), level.coarse(c, 0.125))
    v = v + jnp.concatenate([below[k // 2 : k // 2 + 1] for k in range(v.shape[0])], 0)
    return level.sweep(level.sweep(v))


def up_kernel(
    gather, c2, b2, u2, c1, b1, u1_in, y0, y1, c0, b0, u0,
    out, res,
    s3, e2, e1, e0, hx, hy, hz, hzm, hw, ha, hb,
    gx_, gy_, gz_, gzm_, gw_, ga_, gb_, gr_,
    fx, fy, fz, fzm, w, ua, ub,
):
    ix, iy = lax.axis_index("gx"), lax.axis_index("gy")
    oy = iy % 2
    zero = jnp.zeros((8, NZ), F32)

    def field(k):
        return jnp.stack(
            [
                jnp.stack([gather[pl.ds(xq * 16 + g * 4 + k + xl, 8, stride=64), :] for g in range(4)], 0)
                for xq in range(4)
                for xl in range(2)
            ],
            0,
        )

    u3 = whole_cycle(3, field(0), field(2))
    s3[...] = jnp.zeros(s3.shape, F32)
    for xlo in range(8):
        for g in range(4):
            s3[g + 1, pl.ds(8 + xlo, 8, stride=8), :] = u3[xlo, g]
    shape = (8, NZ)
    mine = lane(shape) // 16 == lax.broadcasted_iota(jnp.int32, shape, 0)
    tiles = []
    for k in range(6):
        for g in range(3):
            row = s3[iy + g, pl.ds(2 * ix + 6 + k, 1), :]
            tiles.append(jnp.where(mine, jnp.broadcast_to(row, shape), 0.0))
    spread = exact_dot(jnp.concatenate(tiles, 0), one_hot((NZ, NZ), lambda i, j: i % 16 == j // 8))
    for k in range(6):
        t = spread[24 * k : 24 * k + 24]
        e2[k, pl.ds(0, 24, stride=2), :] = t
        e2[k, pl.ds(1, 24, stride=2), :] = t

    for x in range(16):
        hy[x, pl.ds(0, 8), :] = zero
        ha[x] = u2[x] + e2[(x - 2) // 2] if 2 <= x < 14 else jnp.zeros((48, NZ), F32)
    low = Level(2, c2, b2, hx, hy, hz, hzm, hw, 8, 40, 32)
    low.faces(0, 15)
    low.weights(1, 15)
    low.sweep(ha, hb, 3, 13)
    low.sweep(hb, ha, 4, 12)

    def grow1(k):
        t = ha[4 + k, pl.ds(8, 32), :]
        e1[k, pl.ds(0, 32, stride=2), :] = t
        e1[k, pl.ds(1, 32, stride=2), :] = t

    rows(0, 8, grow1)

    def copy1(x):
        ga_[x] = u1_in[x]
        gr_[x] = b1[x]
        gy_[x, pl.ds(0, 8), :] = zero

    rows(0, 20, copy1)
    set_y1(ga_, gr_, y0, y1, oy, 0, 8)

    def add1(x):
        ga_[x] = ga_[x] + e1[(x - 2) // 2]

    rows(2, 18, add1)
    mid = Level(1, c1, gr_, gx_, gy_, gz_, gzm_, gw_, 8, 56, 48)
    mid.faces(1, 19)
    mid.weights(2, 18)
    mid.sweep(ga_, gb_, 3, 17)
    mid.sweep(gb_, ga_, 4, 16)

    def grow0(k):
        t = ga_[4 + k, pl.ds(8, 48), :]
        e0[pl.ds(0, 48, stride=2), :] = t
        e0[pl.ds(1, 48, stride=2), :] = t
        for j in range(2):
            ua[2 * k + j] = u0[2 * k + j] + e0[...]

    rows(0, 12, grow0)

    def clear0(x):
        fy[x, pl.ds(0, 8), :] = zero

    rows(0, 24, clear0)
    top = Level(0, c0, b0, fx, fy, fz, fzm, w, 8, 88, 40)
    top.faces(1, 23)
    top.weights(2, 22)
    top.sweep(ua, ub, 2, 22)
    top.sweep(ub, ua, 3, 21)

    def finish(x):
        out[x] = ua[4 + x, pl.ds(Y0, NY), :]
        res[x, pl.ds(0, 32), :] = top.residual(ua, 4 + x, Y0, 32)
        res[x, pl.ds(32, 32), :] = top.residual(ua, 4 + x, Y0 + 32, 32)

    rows(0, NX, finish)


def swaps(axis, first, second):
    count = lax.axis_size(axis)

    def pairs(start):
        return [p for i in range(start, count - 1, 2) for p in ((i, i + 1), (i + 1, i))]

    late = lax.ppermute(second, axis, pairs(1))
    return lax.ppermute(first, axis, pairs(0)), late


def per_device(source, density, drag, porous_rows):
    porous = jnp.broadcast_to(porous_rows.astype(F32)[:, None], (NY, NZ))
    cond, p0, p1 = call(
        begin_kernel, [(NX, NY, NZ), (32, 8, NZ), (32, 8, NZ)], [], (source, density, drag, porous), "begin", 32
    )
    y0, y1 = swaps("gy", p0, p1)
    p0, p1 = call(edge_kernel, [(21, 80, NZ)] * 2, [], (cond, source, y0, y1), "edges", 32)
    x0, x1 = swaps("gx", p0, p1)
    one, two = (20, 64, NZ), (16, 48, NZ)
    keep = (24, 96, NZ)
    c0, b0, u0, c1, b1, u1, c2, b2, p0, p1 = call(
        down_kernel,
        [keep] * 3 + [one] * 3 + [two] * 2 + [(22, 8, NZ)] * 2,
        [(40, 96, NZ)] * 9 + [(96, NZ)] + [one] * 6 + [(64, NZ)],
        (cond, source, y0, y1, x0, x1),
        "down",
        56,
    )
    y0, y1 = swaps("gy", p0, p1)
    u1, c2, b2, p0, p1 = call(
        edge2_kernel, [one, two, two] + [(544, NZ)] * 2, [], (u1, c2, b2, y0, y1), "edges2", 32
    )
    x0, x1 = swaps("gx", p0, p1)
    u1, c2, b2, u2, packed = call(
        level2_kernel,
        [one, two, two, two, (512, NZ)],
        [two] * 6 + [(48, NZ)] + [(2, 48, NZ)] * 2,
        (u1, c2, b2, x0, x1),
        "level2",
        32,
    )
    whole = lax.all_to_all(packed, ("gx", "gy"), 0, 0, tiled=True)
    out, res = call(
        up_kernel,
        [(NX, NY, NZ)] * 2,
        [(6, 80, NZ), (6, 48, NZ), (8, 64, NZ), (96, NZ)] + [two] * 7 + [one] * 8 + [keep] * 7,
        (whole, c2, b2, u2, c1, b1, u1, y0, y1, c0, b0, u0),
        "up",
        56,
    )
    return out, res


def solution(mesh):
    return jax.shard_map(
        per_device,
        mesh=mesh,
        in_specs=(P("gx", "gy", None), P("gx", "gy", None), P("gx", "gy", None), P("gy")),
        out_specs=(P("gx", "gy", None), P("gx", "gy", None)),
        check_vma=False,
    )
```

time: 721 us -> 136 us (0.19)
  the two profiles are of different devices: /device:TPU:38 before, /device:TPU:1 now
where the time goes in v1:
time: 136 us; the launch traced here: 135 us
  Pallas kernels  61.2 us (45%)
  blocking collectives  26.5 us (19%)
  waiting for transfers between devices  18.4 us (14%)
  starting transfers between devices  17.4 us (13%)
  local copies, waits for them, and re-layouts  10.4 us (8%)
    pallas_call x6, Pallas kernels, call(): pl.pallas_call(body, out_shape=[jax.ShapeDtypeStruct(s, F32) for s in out...  61.2 us
    all_to_all x1, blocking collectives, per_device(): whole = lax.all_to_all(packed, ('gx', 'gy'), 0, 0, tiled=True)  26.5 us
    ppermute x4, waiting for transfers between devices, swaps(): late = lax.ppermute(second, axis, pairs(1))  14.9 us
    unnamed x34, local copies, waits for them, and re-layouts  10.3 us
    ppermute x4, starting transfers between devices, swaps(): late = lax.ppermute(second, axis, pairs(1))  9.42 us
    ppermute x4, starting transfers between devices, swaps(): return (lax.ppermute(first, axis, pairs(0)), late)  8.02 us
    ppermute x4, waiting for transfers between devices, swaps(): return (lax.ppermute(first, axis, pairs(0)), late)  3.5 us
  transfers between devices with their start and end apart: 8, of which 4 were waited for; matrix products, arithmetic and copies ran while one was open for 0% of the time, Pallas kernels for 0%

profile of v1, /device:TPU:1, one launch (start us, length us, event | category | flops | bytes accessed | tf_op | source)
XLA Modules:
  0.0 135.4 jit_solution(7329684905807405776)
XLA Ops:
  0.6 0.7 convert_element_type.3
  1.3 0.1 broadcast_in_dim.2.porous
  1.4 1.0 copy-done
  2.4 1.0 copy-done.4
  3.5 1.0 copy-done.5
  4.5 0.5 begin.1
  5.0 2.1 %collective-permute-start = (f32[32,8,128]{2,1,0:T(8,128)S(1)}, f32[32,8,128]{2,1,0:T(8,128)S(1)}, u32[]{:S(2)}, u32[]{:S(2)}) collective-permute-start(f32[32,8,128]{2,1,0:T(8,128)S(1)} %get-tuple-element.28), channel_id=1, source_target_pairs={{0,1},{1,0},{2,3},{3,2},{4,5},{5,4},{6,7},{7,6},{8,9},{9,8},{10,11... | collective-permute-start | bytes 393224 | tf_op jit(solution)/shard_map/ppermute | solution.py:594
  7.1 0.7 collective-permute-start.1
  7.7 2.0 %collective-permute-done.y0 = f32[32,8,128]{2,1,0:T(8,128)S(1)} collective-permute-done((f32[32,8,128]{2,1,0:T(8,128)S(1)}, f32[32,8,128]{2,1,0:T(8,128)S(1)}, u32[]{:S(2)}, u32[]{:S(2)}) %collective-permute-start) | collective-permute-done | bytes 131104 | tf_op jit(solution)/shard_map/ppermute | solution.py:594
  9.8 0.3 edges.1
  10.0 1.8 %collective-permute-start.2 = (f32[21,80,128]{2,1,0:T(8,128)S(1)}, f32[21,80,128]{2,1,0:T(8,128)S(1)}, u32[]{:S(2)}, u32[]{:S(2)}) collective-permute-start(f32[21,80,128]{2,1,0:T(8,128)S(1)} %get-tuple-element.30), channel_id=1, source_target_pairs={{0,4},{4,0},{8,12},{12,8},{16,20},{20,16},{24,28},{28,24},{32,36},... | collective-permute-start | bytes 2580488 | tf_op jit(solution)/shard_map/ppermute | solution.py:594
  11.9 3.4 %collective-permute-start.3 = (f32[21,80,128]{2,1,0:T(8,128)S(1)}, f32[21,80,128]{2,1,0:T(8,128)S(1)}, u32[]{:S(2)}, u32[]{:S(2)}) collective-permute-start(f32[21,80,128]{2,1,0:T(8,128)S(1)} %get-tuple-element.31), channel_id=1, source_target_pairs={{4,8},{8,4},{12,16},{16,12},{20,24},{24,20},{28,32},{32,28},{36,40... | collective-permute-start | bytes 2580488 | tf_op jit(solution)/shard_map/ppermute | solution.py:593
  15.3 10.7 %collective-permute-done.3.x1 = f32[21,80,128]{2,1,0:T(8,128)S(1)} collective-permute-done((f32[21,80,128]{2,1,0:T(8,128)S(1)}, f32[21,80,128]{2,1,0:T(8,128)S(1)}, u32[]{:S(2)}, u32[]{:S(2)}) %collective-permute-start.3) | collective-permute-done | bytes 860192 | tf_op jit(solution)/shard_map/ppermute | solution.py:593
  26.0 0.9 copy-done.16
  26.9 27.4 %down.1 = (f32[24,96,128]{2,1,0:T(8,128)}, f32[24,96,128]{2,1,0:T(8,128)}, f32[24,96,128]{2,1,0:T(8,128)}, f32[20,64,128]{2,1,0:T(8,128)}, f32[20,64,128]{2,1,0:...) custom-call(f32[16,64,128]{2,1,0:T(8,128)} %copy-done.1, ...), custom_call_target="tpu_custom_call" | custom-call | tf_op jit(solution)/shard_map/down/pallas_call | solution.py:21
  54.3 4.0 %collective-permute-start.4 = (f32[22,8,128]{2,1,0:T(8,128)}, f32[22,8,128]{2,1,0:T(8,128)S(1)}, u32[]{:S(2)}, u32[]{:S(2)}) collective-permute-start(f32[22,8,128]{2,1,0:T(8,128)} %get-tuple-element.35), channel_id=1, source_target_pairs={{0,1},{1,0},{2,3},{3,2},{4,5},{5,4},{6,7},{7,6},{8,9},{9,8},{10,11... | collective-permute-start | bytes 270344 | tf_op jit(solution)/shard_map/ppermute | solution.py:594
  58.3 0.7 collective-permute-start.5
  59.0 1.5 %collective-permute-done.4.y0 = f32[22,8,128]{2,1,0:T(8,128)S(1)} collective-permute-done((f32[22,8,128]{2,1,0:T(8,128)}, f32[22,8,128]{2,1,0:T(8,128)S(1)}, u32[]{:S(2)}, u32[]{:S(2)}) %collective-permute-start.4) | collective-permute-done | bytes 90144 | tf_op jit(solution)/shard_map/ppermute | solution.py:594
  60.4 1.1 copy-done.2
  61.6 1.0 copy-done.11
  62.6 1.0 copy-done.12
  63.6 0.3 edges2.1
  63.9 0.1 collective-permute-start.6
  64.0 4.7 %collective-permute-start.7 = (f32[544,128]{1,0:T(8,128)S(1)}, f32[544,128]{1,0:T(8,128)S(1)}, u32[]{:S(2)}, u32[]{:S(2)}) collective-permute-start(f32[544,128]{1,0:T(8,128)S(1)} %get-tuple-element.41), channel_id=1, source_target_pairs={{4,8},{8,4},{12,16},{16,12},{20,24},{24,20},{28,32},{32,28},{36,40... | collective-permute-start | bytes 835592 | tf_op jit(solution)/shard_map/ppermute | solution.py:593
  68.7 4.2 %collective-permute-done.7.x1 = f32[544,128]{1,0:T(8,128)S(1)} collective-permute-done((f32[544,128]{1,0:T(8,128)S(1)}, f32[544,128]{1,0:T(8,128)S(1)}, u32[]{:S(2)}, u32[]{:S(2)}) %collective-permute-start.7) | collective-permute-done | bytes 278560 | tf_op jit(solution)/shard_map/ppermute | solution.py:593
  73.0 4.7 %level2.1 = (f32[20,64,128]{2,1,0:T(8,128)S(1)}, f32[16,48,128]{2,1,0:T(8,128)S(1)}, f32[16,48,128]{2,1,0:T(8,128)S(1)}, f32[16,48,128]{2,1,0:T(8,128)S(1)}, f32[512,128]{1,0:T(8,128)S(1)}) custom-call(f32[20,64,128]{2,1,0:T(8,128)S(1)} %get-tuple-element.37.u1_in, f32[16,48,128]{2,1,0:T(8,128)S(1)} %get-tuple-element.38.c2_in, ...), custom_call_target="tpu_custom_call" | custom-call | tf_op jit(solution)/shard_map/level2/pallas_call | solution.py:21
  77.7 0.8 copy-done.3
  78.5 0.8 copy-done.8
  79.2 0.7 copy-done.9
  80.0 0.7 copy-done.10
  80.7 26.5 %all_to_all.11 = f32[128,4,128]{2,1,0:T(4,128)} all-to-all(f32[128,4,128]{2,1,0:T(4,128)S(1)} %bitcast.2), channel_id=1, replica_groups=mesh['gx'=32,'gy'=4] {'gx','gy'}, dimensions={0} | all-to-all | bytes 524288 | tf_op jit(solution)/shard_map/all_to_all | solution.py:628
  107.2 28.1 %up.1 = (f32[16,64,128]{2,1,0:T(8,128)}, f32[16,64,128]{2,1,0:T(8,128)}) custom-call(f32[512,128]{1,0:T(8,128)} %bitcast.3, f32[16,48,128]{2,1,0:T(8,128)} %copy-done.8, f32[16,48,128]{2,1,0:T(8,128)} %copy-done.9, f32[16,48,128]{2,1,0:T(8,128)} %copy-done.10, f32[20,64,128]{2,1,0:T(8,128)} %get-tuple-element.46.c1, f32[20,64,128]{2,1,0:T(8,128)} %get-tuple-element.47.b1, ...), custom_call_target="tpu_custom_call" | custom-call | tf_op jit(solution)/shard_map/up/pallas_call | solution.py:21
  (27 shorter events, 0.1 us)
Async XLA Ops:
  1.4 1.0 copy-start
  2.4 1.0 copy-start.4
  3.5 1.0 copy-start.5
  4.9 21.0 %copy-start.1 = (f32[16,64,128]{2,1,0:T(8,128)}, f32[16,64,128]{2,1,0:T(8,128)S(1)}, u32[]{:S(2)}) copy-start(f32[16,64,128]{2,1,0:T(8,128)S(1)} %get-tuple-element.27.cond) | copy-start | bytes 1572868
  5.0 4.8 %collective-permute-start = (f32[32,8,128]{2,1,0:T(8,128)S(1)}, f32[32,8,128]{2,1,0:T(8,128)S(1)}, u32[]{:S(2)}, u32[]{:S(2)}) collective-permute-start(f32[32,8,128]{2,1,0:T(8,128)S(1)} %get-tuple-element.28), channel_id=1, source_target_pairs={{0,1},{1,0},{2,3},{3,2},{4,5},{5,4},{6,7},{7,6},{8,9},{9,8},{10,11... | collective-permute-start | bytes 393224 | tf_op jit(solution)/shard_map/ppermute | solution.py:594
  7.1 2.7 %collective-permute-start.1 = (f32[32,8,128]{2,1,0:T(8,128)S(1)}, f32[32,8,128]{2,1,0:T(8,128)S(1)}, u32[]{:S(2)}, u32[]{:S(2)}) collective-permute-start(f32[32,8,128]{2,1,0:T(8,128)S(1)} %get-tuple-element.29), channel_id=1, source_target_pairs={{1,2},{2,1},{5,6},{6,5},{9,10},{10,9},{13,14},{14,13},{17,18},{18,... | collective-permute-start | bytes 393224 | tf_op jit(solution)/shard_map/ppermute | solution.py:593
  9.8 16.2 %copy-start.6 = (f32[32,8,128]{2,1,0:T(8,128)}, f32[32,8,128]{2,1,0:T(8,128)S(1)}, u32[]{:S(2)}) copy-start(f32[32,8,128]{2,1,0:T(8,128)S(1)} %collective-permute-done.y0) | copy-start | bytes 393220
  9.8 16.2 %copy-start.7 = (f32[32,8,128]{2,1,0:T(8,128)}, f32[32,8,128]{2,1,0:T(8,128)S(1)}, u32[]{:S(2)}) copy-start(f32[32,8,128]{2,1,0:T(8,128)S(1)} %collective-permute-done.1.y1) | copy-start | bytes 393220
  10.0 5.2 %collective-permute-start.2 = (f32[21,80,128]{2,1,0:T(8,128)S(1)}, f32[21,80,128]{2,1,0:T(8,128)S(1)}, u32[]{:S(2)}, u32[]{:S(2)}) collective-permute-start(f32[21,80,128]{2,1,0:T(8,128)S(1)} %get-tuple-element.30), channel_id=1, source_target_pairs={{0,4},{4,0},{8,12},{12,8},{16,20},{20,16},{24,28},{28,24},{32,36},... | collective-permute-start | bytes 2580488 | tf_op jit(solution)/shard_map/ppermute | solution.py:594
  11.9 14.1 %collective-permute-start.3 = (f32[21,80,128]{2,1,0:T(8,128)S(1)}, f32[21,80,128]{2,1,0:T(8,128)S(1)}, u32[]{:S(2)}, u32[]{:S(2)}) collective-permute-start(f32[21,80,128]{2,1,0:T(8,128)S(1)} %get-tuple-element.31), channel_id=1, source_target_pairs={{4,8},{8,4},{12,16},{16,12},{20,24},{24,20},{28,32},{32,28},{36,40... | collective-permute-start | bytes 2580488 | tf_op jit(solution)/shard_map/ppermute | solution.py:593
  15.3 10.7 %copy-start.15 = (f32[21,80,128]{2,1,0:T(8,128)}, f32[21,80,128]{2,1,0:T(8,128)S(1)}, u32[]{:S(2)}) copy-start(f32[21,80,128]{2,1,0:T(8,128)S(1)} %collective-permute-done.2.x0) | copy-start | bytes 2580484
  26.0 0.9 copy-start.16
  54.3 6.1 %collective-permute-start.4 = (f32[22,8,128]{2,1,0:T(8,128)}, f32[22,8,128]{2,1,0:T(8,128)S(1)}, u32[]{:S(2)}, u32[]{:S(2)}) collective-permute-start(f32[22,8,128]{2,1,0:T(8,128)} %get-tuple-element.35), channel_id=1, source_target_pairs={{0,1},{1,0},{2,3},{3,2},{4,5},{5,4},{6,7},{7,6},{8,9},{9,8},{10,11... | collective-permute-start | bytes 270344 | tf_op jit(solution)/shard_map/ppermute | solution.py:594
  58.3 2.1 %collective-permute-start.5 = (f32[22,8,128]{2,1,0:T(8,128)}, f32[22,8,128]{2,1,0:T(8,128)S(1)}, u32[]{:S(2)}, u32[]{:S(2)}) collective-permute-start(f32[22,8,128]{2,1,0:T(8,128)} %get-tuple-element.36), channel_id=1, source_target_pairs={{1,2},{2,1},{5,6},{6,5},{9,10},{10,9},{13,14},{14,13},{17,18},{18,... | collective-permute-start | bytes 270344 | tf_op jit(solution)/shard_map/ppermute | solution.py:593
  60.4 17.2 %copy-start.13 = (f32[22,8,128]{2,1,0:T(8,128)}, f32[22,8,128]{2,1,0:T(8,128)S(1)}, u32[]{:S(2)}) copy-start(f32[22,8,128]{2,1,0:T(8,128)S(1)} %collective-permute-done.4.y0) | copy-start | bytes 270340
  60.4 17.2 %copy-start.14 = (f32[22,8,128]{2,1,0:T(8,128)}, f32[22,8,128]{2,1,0:T(8,128)S(1)}, u32[]{:S(2)}) copy-start(f32[22,8,128]{2,1,0:T(8,128)S(1)} %collective-permute-done.5.y1) | copy-start | bytes 270340
  60.4 1.2 copy-start.2
  61.6 1.0 copy-start.11
  62.6 1.0 copy-start.12
  63.9 4.8 %collective-permute-start.6 = (f32[544,128]{1,0:T(8,128)S(1)}, f32[544,128]{1,0:T(8,128)S(1)}, u32[]{:S(2)}, u32[]{:S(2)}) collective-permute-start(f32[544,128]{1,0:T(8,128)S(1)} %get-tuple-element.40), channel_id=1, source_target_pairs={{0,4},{4,0},{8,12},{12,8},{16,20},{20,16},{24,28},{28,24},{32,36},... | collective-permute-start | bytes 835592 | tf_op jit(solution)/shard_map/ppermute | solution.py:594
  64.0 9.0 %collective-permute-start.7 = (f32[544,128]{1,0:T(8,128)S(1)}, f32[544,128]{1,0:T(8,128)S(1)}, u32[]{:S(2)}, u32[]{:S(2)}) collective-permute-start(f32[544,128]{1,0:T(8,128)S(1)} %get-tuple-element.41), channel_id=1, source_target_pairs={{4,8},{8,4},{12,16},{16,12},{20,24},{24,20},{28,32},{32,28},{36,40... | collective-permute-start | bytes 835592 | tf_op jit(solution)/shard_map/ppermute | solution.py:593
  77.6 0.8 copy-start.3
  78.5 0.8 copy-start.8
  79.2 0.7 copy-start.9
  80.0 0.8 copy-start.10

commit v2 on v1

--- a/solution.py
+++ b/solution.py
@@ -15,28 +15,28 @@
 NX, NY, NZ = 16, 64, 128
 F32 = jnp.float32
 VMEM = pl.BlockSpec(memory_space=pltpu.VMEM)
-
-
-def call(body, outs, scratch, args, name, vmem):
+HBM = pl.BlockSpec(memory_space=pltpu.HBM)
+
+
+def call(body, outs, scratch, args, name, vmem, hbm=0):
+    args = [pltpu.with_memory_space_constraint(a, pltpu.HBM) for a in args[:hbm]] + list(args[hbm:])
     return pl.pallas_call(
         body,
         out_shape=[jax.ShapeDtypeStruct(s, F32) for s in outs],
-        in_specs=[VMEM] * len(args),
+        in_specs=[HBM] * hbm + [VMEM] * (len(args) - hbm),
         out_specs=[VMEM] * len(outs),
-        scratch_shapes=[pltpu.VMEM(s, F32) for s in scratch],
+        scratch_shapes=[pltpu.VMEM(s, F32) if isinstance(s, tuple) else s for s in scratch],
         compiler_params=pltpu.CompilerParams(vmem_limit_bytes=vmem * 2**20),
         name=name,
     )(*args)
 
 
 def recip(t):
-    r = pl.reciprocal(t, approx=True)
-    r = r * (2.0 - t * r)
-    return r * (2.0 - t * r)
+    return 1.0 / t
 
 
 def harmonic(a, b):
-    return (2.0 * a) * b * recip(jnp.maximum(a + b, 1e-30))
+    return (2.0 * a) * b / jnp.maximum(a + b, 1e-30)
 
 
 def lane(shape):
@@ -52,12 +52,39 @@
     return v + jnp.where(first, lroll(v, -s), lroll(v, s))
 
 
-def rows(lo, hi, body, unroll=1):
-    def step(x, carry):
+def pack_lanes(tiles):
+    n = len(tiles)
+    out = tiles[0]
+    for k in range(1, n):
+        out = jnp.where(lane(out.shape) % n == k, tiles[k], out)
+    return out
+
+
+def unpack_lanes(p, n):
+    at = lane(p.shape) % n
+    moved = {d: p if d == 0 else lroll(p, -d) for d in range(1 - n, n)}
+    tiles = []
+    for k in range(n):
+        out = moved[k]
+        for m in range(1, n):
+            out = jnp.where(at == m, moved[k - m], out)
+        tiles.append(out)
+    return tiles
+
+
+def rows(lo, hi, body, unroll=8):
+    whole = (hi - lo) // unroll
+
+    def step(k, carry):
+        for j in range(unroll):
+            body(lo + k * unroll + j)
+        return carry
+
+    if whole > 1:
+        lax.fori_loop(0, whole, step, 0)
+        lo = lo + whole * unroll
+    for x in range(lo, hi):
         body(x)
-        return carry
-
-    lax.fori_loop(lo, hi, step, 0, unroll=unroll)
 
 
 def chunks(ys, ye, size):
@@ -128,46 +155,73 @@
         r = r + self.fz[x, here, :] * (lroll(v, -self.s) - v)
         return r + self.fzm[x, here, :] * (lroll(v, self.s) - v)
 
-    def restrict(self, u, tmp, out, count, x_from, x_to, rows_from):
+    def halve(self, tmp, out, count, x_to, scale):
+        half = tmp.shape[1] // 2
+
+        def body(k):
+            t = tmp[k, pl.ds(0, half, stride=2), :] + tmp[k, pl.ds(1, half, stride=2), :]
+            out[x_to + k, pl.ds(8, half), :] = scale * pair_lanes(t, self.s)
+
+        rows(0, count, body)
+
+    def restrict(self, u, tmp, out, count, x_from, x_to):
         def body(k):
             x = x_from + 2 * k
             for y, n in self.parts:
-                tmp[pl.ds(y, n), :] = self.residual(u, x, y, n) + self.residual(u, x + 1, y, n)
-            half = tmp.shape[0] // 2
-            t = tmp[pl.ds(0, half, stride=2), :] + tmp[pl.ds(1, half, stride=2), :]
-            out[x_to + k, pl.ds(8, half), :] = 0.5 * pair_lanes(t, self.s)
-
-        rows(0, count, body)
+                tmp[k, pl.ds(y, n), :] = self.residual(u, x, y, n) + self.residual(u, x + 1, y, n)
+
+        rows(0, count, body, 4)
+        self.halve(tmp, out, count, x_to, 0.5)
 
     def restrict_c(self, tmp, out, count, x_from, x_to):
         def body(k):
             x = x_from + 2 * k
-            tmp[...] = self.c[x] + self.c[x + 1]
-            half = tmp.shape[0] // 2
-            t = tmp[pl.ds(0, half, stride=2), :] + tmp[pl.ds(1, half, stride=2), :]
-            out[x_to + k, pl.ds(8, half), :] = 0.125 * pair_lanes(t, self.s)
+            tmp[k] = self.c[x] + self.c[x + 1]
 
         rows(0, count, body)
+        self.halve(tmp, out, count, x_to, 0.125)
 
 
 def odd(axis):
     return lax.axis_index(axis) % 2
 
 
-def begin_kernel(source, density, drag, porous, cond, ypack0, ypack1):
+PARTS = 4
+
+
+def begin_kernel(source, density, drag, porous, cond, rhs, ypack0, ypack1, dens, dra, por, sem, esem):
     o = odd("gy")
     at0 = pl.multiple_of((1 - o) * (NY - 8), 8)
     at1 = pl.multiple_of(o * (NY - 8), 8)
-
-    def body(x):
-        c = recip(density[x] * (1.0 + drag[x] * porous[...]))
-        cond[x] = c
-        ypack0[x] = cond[x, pl.ds(at0, 8), :]
-        ypack1[x] = cond[x, pl.ds(at1, 8), :]
-        ypack0[NX + x] = source[x, pl.ds(at0, 8), :]
-        ypack1[NX + x] = source[x, pl.ds(at1, 8), :]
-
-    rows(0, NX, body)
+    part = NX // PARTS
+    loads = []
+    first = pltpu.make_async_copy(porous, por, esem.at[3])
+    first.start()
+    for k in range(PARTS):
+        here = pl.ds(k * part, part)
+        for j, (src, dst) in enumerate(((density, dens), (drag, dra))):
+            loads.append(pltpu.make_async_copy(src.at[here], dst.at[here], sem.at[j, k]))
+            loads[-1].start()
+    edges = []
+    for j, (at, pack) in enumerate(((at0, ypack0), (at1, ypack1))):
+        edges.append(pltpu.make_async_copy(source.at[:, pl.ds(at, 8), :], pack.at[pl.ds(NX, NX)], esem.at[j]))
+        edges[-1].start()
+    edges.append(pltpu.make_async_copy(source, rhs, esem.at[2]))
+    edges[-1].start()
+    first.wait()
+    shape = (NY, NZ)
+    line = jnp.broadcast_to(por[...].astype(F32)[None], (NY, NY))
+    same = lax.broadcasted_iota(jnp.int32, (NY, NY), 0) == lax.broadcasted_iota(jnp.int32, (NY, NY), 1)
+    mask = jnp.broadcast_to(jnp.sum(jnp.where(same, line, 0.0), axis=1, keepdims=True), shape)
+    for k in range(PARTS):
+        loads[2 * k].wait()
+        loads[2 * k + 1].wait()
+        for x in range(k * part, k * part + part):
+            cond[x] = recip(dens[x] * (1.0 + dra[x] * mask))
+            ypack0[x] = cond[x, pl.ds(at0, 8), :]
+            ypack1[x] = cond[x, pl.ds(at1, 8), :]
+    for edge in edges:
+        edge.wait()
 
 
 def edge_kernel(cond, source, y0, y1, xpack0, xpack1):
@@ -199,8 +253,8 @@
 
 def down_kernel(
     cond, source, y0, y1, x0, x1,
-    c0_out, b0_out, u0_out, c1, b1, u1, c2, b2, ypack0, ypack1,
-    c, b, fx, fy, fz, fzm, w, ua, ub, tmp, gx_, gy_, gz_, gzm_, gw_, ga_, tmp1,
+    fx, fy, fz, fzm, w, b, ub, gx_, gy_, gz_, gzm_, gw_, b1, u1, c2, b2, ypack0, ypack1,
+    c, ua, tmp, c1, ga_, tmp1,
 ):
     ox, oy = odd("gx"), odd("gy")
     at0 = pl.multiple_of(8 + (1 - oy) * (NY + 8), 8)
@@ -252,94 +306,82 @@
             ref[x] = jnp.zeros((48, NZ), F32)
 
     rows(0, 16, clear2)
-    tmp[pl.ds(0, 8), :] = zero
-    tmp[pl.ds(88, 8), :] = zero
-    tmp1[pl.ds(0, 8), :] = zero
-    tmp1[pl.ds(56, 8), :] = zero
-    top.restrict(ub, tmp, b1, 16, 4, 2, None)
+
+    def clear_tmp(x):
+        tmp[x, pl.ds(0, 8), :] = zero
+        tmp[x, pl.ds(88, 8), :] = zero
+
+    rows(0, 18, clear_tmp)
+    for x in range(8):
+        tmp1[x, pl.ds(0, 8), :] = zero
+        tmp1[x, pl.ds(56, 8), :] = zero
+    top.restrict(ub, tmp, b1, 16, 4, 2)
     top.restrict_c(tmp, c1, 18, 2, 1)
-
-    def keep(x):
-        c0_out[x] = c[X0 - 4 + x]
-        b0_out[x] = b[X0 - 4 + x]
-        u0_out[x] = ub[X0 - 4 + x]
-
-    rows(0, 24, keep)
 
     mid = Level(1, c1, b1, gx_, gy_, gz_, gzm_, gw_, 8, 56, 48)
     mid.faces(1, 19)
     mid.weights(2, 18, ga_)
     mid.sweep(ga_, u1, 3, 17)
-    mid.restrict(u1, tmp1, b2, 6, 4, 5, None)
+    mid.restrict(u1, tmp1, b2, 6, 4, 5)
     mid.restrict_c(tmp1, c2, 8, 2, 4)
 
-    high, low = 28, 0
-    e0 = Y1 + (1 - oy) * high
-    e1 = Y1 + oy * high
-
-    def edge1(x):
-        ypack0[x, pl.ds(0, 4), :] = u1[X1 + x, pl.ds(e0, 4), :]
-        ypack1[x, pl.ds(0, 4), :] = u1[X1 + x, pl.ds(e1, 4), :]
-        ypack0[x, pl.ds(4, 4), :] = b1[X1 + x, pl.ds(e0, 4), :]
-        ypack1[x, pl.ds(4, 4), :] = b1[X1 + x, pl.ds(e1, 4), :]
-
-    rows(0, 8, edge1)
+    e0 = Y1 + (1 - oy) * 28
+    e1 = Y1 + oy * 28
     f0 = pl.multiple_of(Y2 + (1 - oy) * 8, 8)
     f1 = pl.multiple_of(Y2 + oy * 8, 8)
-    for x in range(6):
-        ypack0[8 + x] = b2[X2 - 1 + x, pl.ds(f0, 8), :]
-        ypack1[8 + x] = b2[X2 - 1 + x, pl.ds(f1, 8), :]
-    for x in range(8):
-        ypack0[14 + x] = c2[X2 - 2 + x, pl.ds(f0, 8), :]
-        ypack1[14 + x] = c2[X2 - 2 + x, pl.ds(f1, 8), :]
-
-
-def set_y1(u1, b1, y0, y1, oy, lo, hi):
+    for pack, e, f in ((ypack0, e0, f0), (ypack1, e1, f1)):
+        for k in range(4):
+            x = X1 + 2 * k
+            pack[k, pl.ds(0, 4), :] = pack_lanes([u1[x + j, pl.ds(e, 4), :] for j in range(2)])
+            pack[k, pl.ds(4, 4), :] = pack_lanes([b1[x + j, pl.ds(e, 4), :] for j in range(2)])
+        for k in range(2):
+            pack[4 + k] = pack_lanes([b2[X2 - 1 + 4 * k + j, pl.ds(f, 8), :] for j in range(4)])
+            pack[6 + k] = pack_lanes([c2[X2 - 2 + 4 * k + j, pl.ds(f, 8), :] for j in range(4)])
+
+
+def set_y1(ref, y0, y1, oy, part):
     a0 = Y1 - 4 + (1 - oy) * 36
     a1 = Y1 - 4 + oy * 36
-
-    def body(x):
-        u1[X1 + x, pl.ds(a0, 4), :] = y0[x, pl.ds(0, 4), :]
-        u1[X1 + x, pl.ds(a1, 4), :] = y1[x, pl.ds(0, 4), :]
-        if b1 is not None:
-            b1[X1 + x, pl.ds(a0, 4), :] = y0[x, pl.ds(4, 4), :]
-            b1[X1 + x, pl.ds(a1, 4), :] = y1[x, pl.ds(4, 4), :]
-
-    rows(lo, hi, body)
+    for y, a in ((y0, a0), (y1, a1)):
+        for k in range(4):
+            for j, v in enumerate(unpack_lanes(y[k], 2)):
+                ref[X1 + 2 * k + j, pl.ds(a, 4), :] = v[4 * part : 4 * part + 4]
 
 
 def set_y2(c2, b2, y0, y1, oy):
     a0 = pl.multiple_of(Y2 - 8 + (1 - oy) * 24, 8)
     a1 = pl.multiple_of(Y2 - 8 + oy * 24, 8)
-    for x in range(6):
-        b2[X2 - 1 + x, pl.ds(a0, 8), :] = y0[8 + x]
-        b2[X2 - 1 + x, pl.ds(a1, 8), :] = y1[8 + x]
-    for x in range(8):
-        c2[X2 - 2 + x, pl.ds(a0, 8), :] = y0[14 + x]
-        c2[X2 - 2 + x, pl.ds(a1, 8), :] = y1[14 + x]
-
-
-def edge2_kernel(u1_in, c2_in, b2_in, y0, y1, u1, c2, b2, xpack0, xpack1):
+    for y, a in ((y0, a0), (y1, a1)):
+        for k in range(2):
+            for j, v in enumerate(unpack_lanes(y[4 + k], 4)):
+                if 4 * k + j < 6:
+                    b2[X2 - 1 + 4 * k + j, pl.ds(a, 8), :] = v
+            for j, v in enumerate(unpack_lanes(y[6 + k], 4)):
+                c2[X2 - 2 + 4 * k + j, pl.ds(a, 8), :] = v
+
+
+def copy_rows(pairs, lo, hi):
+    def body(x):
+        for src, dst in pairs:
+            dst[x] = src[x]
+
+    rows(lo, hi, body)
+
+
+def edge2_kernel(u1_in, c2_in, b2_in, y0, y1, xpack0, xpack1, u1, c2, b2):
     ox, oy = odd("gx"), odd("gy")
-
-    def copy1(x):
-        u1[x] = u1_in[x]
-
-    def copy2(x):
-        c2[x] = c2_in[x]
-        b2[x] = b2_in[x]
-
-    rows(0, 20, copy1)
-    rows(0, 16, copy2)
-    set_y1(u1, None, y0, y1, oy, 0, 8)
+    copy_rows([(u1_in, u1)], X1, X1 + 8)
+    copy_rows([(c2_in, c2), (b2_in, b2)], X2 - 2, X2 + 6)
+    set_y1(u1, y0, y1, oy, 0)
     set_y2(c2, b2, y0, y1, oy)
     for pack, last in ((xpack0, 1 - ox), (xpack1, ox)):
-        for k in range(4):
-            pack[pl.ds(k * 48, 48), :] = u1[X1 + k + last * 4, pl.ds(8, 48), :]
-        for k in range(5):
-            pack[pl.ds(192 + k * 32, 32), :] = b2[X2 + k - last, pl.ds(8, 32), :]
-        for k in range(6):
-            pack[pl.ds(352 + k * 32, 32), :] = c2[X2 + k - 2 * last, pl.ds(8, 32), :]
+        for k in range(2):
+            x = X1 + 2 * k + last * 4
+            pack[pl.ds(k * 48, 48), :] = pack_lanes([u1[x + j, pl.ds(8, 48), :] for j in range(2)])
+        t = [c2[X2 + k - 2 * last, pl.ds(8, 32), :] for k in range(6)]
+        t += [b2[X2 + k - last, pl.ds(8, 32), :] for k in range(5)]
+        for k in range(3):
+            pack[pl.ds(96 + k * 32, 32), :] = pack_lanes((t + t[:1])[4 * k : 4 * k + 4])
 
 
 def one_hot(shape, f):
@@ -353,39 +395,39 @@
 
 
 def level2_kernel(
-    u1_in, c2_in, b2_in, x0, x1,
-    u1, c2, b2, u2, gather,
-    fx, fy, fz, fzm, w, ua, tmp, b3, c3,
+    u1_in, c2_in, b2_in, y0, y1, x0, x1,
+    fx, fy, fz, fzm, w, b2, u2, u1, gather,
+    c2, ua, tmp, b3, c3,
 ):
-    ox = odd("gx")
+    ox, oy = odd("gx"), odd("gy")
     zero = jnp.zeros((8, NZ), F32)
-
-    def copy1(x):
-        u1[x] = u1_in[x]
-
-    def copy2(x):
-        c2[x] = c2_in[x]
-        b2[x] = b2_in[x]
+    copy_rows([(u1_in, u1)], 0, 20)
+    copy_rows([(c2_in, c2), (b2_in, b2)], 0, 16)
+    for x in range(16):
         u2[x] = jnp.zeros((48, NZ), F32)
         fy[x, pl.ds(0, 8), :] = zero
-
-    rows(0, 20, copy1)
-    rows(0, 16, copy2)
+    set_y1(u1, y0, y1, oy, 0)
+    set_y2(c2, b2, y0, y1, oy)
     for pack, up in ((x0, 1 - ox), (x1, ox)):
-        for k in range(4):
-            u1[X1 - 4 + k + up * 12, pl.ds(8, 48), :] = pack[pl.ds(k * 48, 48), :]
+        for k in range(2):
+            for j, v in enumerate(unpack_lanes(pack[pl.ds(k * 48, 48), :], 2)):
+                u1[X1 - 4 + 2 * k + j + up * 12, pl.ds(8, 48), :] = v
+        t = []
+        for k in range(3):
+            t += unpack_lanes(pack[pl.ds(96 + k * 32, 32), :], 4)
+        for k in range(6):
+            c2[X2 - 6 + k + up * 10, pl.ds(8, 32), :] = t[k]
         for k in range(5):
-            b2[X2 - 5 + k + up * 9, pl.ds(8, 32), :] = pack[pl.ds(192 + k * 32, 32), :]
-        for k in range(6):
-            c2[X2 - 6 + k + up * 10, pl.ds(8, 32), :] = pack[pl.ds(352 + k * 32, 32), :]
+            b2[X2 - 5 + k + up * 9, pl.ds(8, 32), :] = t[6 + k]
 
     low = Level(2, c2, b2, fx, fy, fz, fzm, w, 8, 40, 32)
     low.faces(0, 15)
     low.weights(1, 15, ua)
     low.sweep(ua, u2, 2, 14)
-    tmp[pl.ds(0, 8), :] = zero
-    tmp[pl.ds(40, 8), :] = zero
-    low.restrict(u2, tmp, b3, 2, X2, 0, None)
+    for x in range(2):
+        tmp[x, pl.ds(0, 8), :] = zero
+        tmp[x, pl.ds(40, 8), :] = zero
+    low.restrict(u2, tmp, b3, 2, X2, 0)
     low.restrict_c(tmp, c3, 2, X2, 0)
     both = jnp.concatenate(
         [b3[0, pl.ds(16, 8), :], b3[1, pl.ds(16, 8), :], c3[0, pl.ds(16, 8), :], c3[1, pl.ds(16, 8), :]], 0
@@ -485,11 +527,12 @@
 
 
 def up_kernel(
-    gather, c2, b2, u2, c1, b1, u1_in, y0, y1, c0, b0, u0,
+    gather, y0, y1,
+    hx, hy, hz, hzm, hw, b2, u2,
+    gx_, gy_, gz_, gzm_, gw_, b1_in, u1,
+    fx, fy, fz, fzm, w, b, u0,
     out, res,
-    s3, e2, e1, e0, hx, hy, hz, hzm, hw, ha, hb,
-    gx_, gy_, gz_, gzm_, gw_, ga_, gb_, gr_,
-    fx, fy, fz, fzm, w, ua, ub,
+    s3, e2, e1, e0, ha, hb, b1, ga_, gb_, ua, ub,
 ):
     ix, iy = lax.axis_index("gx"), lax.axis_index("gy")
     oy = iy % 2
@@ -524,11 +567,8 @@
         e2[k, pl.ds(1, 24, stride=2), :] = t
 
     for x in range(16):
-        hy[x, pl.ds(0, 8), :] = zero
         ha[x] = u2[x] + e2[(x - 2) // 2] if 2 <= x < 14 else jnp.zeros((48, NZ), F32)
-    low = Level(2, c2, b2, hx, hy, hz, hzm, hw, 8, 40, 32)
-    low.faces(0, 15)
-    low.weights(1, 15)
+    low = Level(2, None, b2, hx, hy, hz, hzm, hw, 8, 40, 32)
     low.sweep(ha, hb, 3, 13)
     low.sweep(hb, ha, 4, 12)
 
@@ -539,47 +579,36 @@
 
     rows(0, 8, grow1)
 
-    def copy1(x):
-        ga_[x] = u1_in[x]
-        gr_[x] = b1[x]
-        gy_[x, pl.ds(0, 8), :] = zero
-
-    rows(0, 20, copy1)
-    set_y1(ga_, gr_, y0, y1, oy, 0, 8)
-
-    def add1(x):
-        ga_[x] = ga_[x] + e1[(x - 2) // 2]
-
-    rows(2, 18, add1)
-    mid = Level(1, c1, gr_, gx_, gy_, gz_, gzm_, gw_, 8, 56, 48)
-    mid.faces(1, 19)
-    mid.weights(2, 18)
+    copy_rows([(b1_in, b1)], 2, 18)
+    set_y1(b1, y0, y1, oy, 1)
+
+    def add1(k):
+        for j in range(2):
+            ga_[2 + 2 * k + j] = u1[2 + 2 * k + j] + e1[k]
+
+    rows(0, 8, add1)
+    mid = Level(1, None, b1, gx_, gy_, gz_, gzm_, gw_, 8, 56, 48)
     mid.sweep(ga_, gb_, 3, 17)
     mid.sweep(gb_, ga_, 4, 16)
 
     def grow0(k):
         t = ga_[4 + k, pl.ds(8, 48), :]
-        e0[pl.ds(0, 48, stride=2), :] = t
-        e0[pl.ds(1, 48, stride=2), :] = t
+        e0[k, pl.ds(0, 48, stride=2), :] = t
+        e0[k, pl.ds(1, 48, stride=2), :] = t
+
+    def add0(k):
         for j in range(2):
-            ua[2 * k + j] = u0[2 * k + j] + e0[...]
-
-    rows(0, 12, grow0)
-
-    def clear0(x):
-        fy[x, pl.ds(0, 8), :] = zero
-
-    rows(0, 24, clear0)
-    top = Level(0, c0, b0, fx, fy, fz, fzm, w, 8, 88, 40)
-    top.faces(1, 23)
-    top.weights(2, 22)
-    top.sweep(ua, ub, 2, 22)
-    top.sweep(ub, ua, 3, 21)
+            ua[8 + 2 * k + j] = u0[8 + 2 * k + j] + e0[k]
+
+    rows(0, 12, grow0, 4)
+    rows(0, 12, add0, 4)
+    top = Level(0, None, b, fx, fy, fz, fzm, w, 8, 88, 40)
+    top.sweep(ua, ub, 10, 30)
+    top.sweep(ub, ua, 11, 29)
 
     def finish(x):
-        out[x] = ua[4 + x, pl.ds(Y0, NY), :]
-        res[x, pl.ds(0, 32), :] = top.residual(ua, 4 + x, Y0, 32)
-        res[x, pl.ds(32, 32), :] = top.residual(ua, 4 + x, Y0 + 32, 32)
+        out[x] = ua[X0 + x, pl.ds(Y0, NY), :]
+        res[x] = top.residual(ua, X0 + x, Y0, NY)
 
     rows(0, NX, finish)
 
@@ -595,44 +624,50 @@
 
 
 def per_device(source, density, drag, porous_rows):
-    porous = jnp.broadcast_to(porous_rows.astype(F32)[:, None], (NY, NZ))
-    cond, p0, p1 = call(
-        begin_kernel, [(NX, NY, NZ), (32, 8, NZ), (32, 8, NZ)], [], (source, density, drag, porous), "begin", 32
+    sems = [pltpu.SemaphoreType.DMA((2, PARTS)), pltpu.SemaphoreType.DMA((4,))]
+    block = (NX, NY, NZ)
+    cond, source, p0, p1 = call(
+        begin_kernel,
+        [block, block, (32, 8, NZ), (32, 8, NZ)],
+        [block, block, pltpu.VMEM((NY,), jnp.int32)] + sems,
+        (source, density, drag, porous_rows),
+        "begin",
+        16,
+        4,
     )
     y0, y1 = swaps("gy", p0, p1)
-    p0, p1 = call(edge_kernel, [(21, 80, NZ)] * 2, [], (cond, source, y0, y1), "edges", 32)
+    p0, p1 = call(edge_kernel, [(21, 80, NZ)] * 2, [], (cond, source, y0, y1), "edges", 16)
     x0, x1 = swaps("gx", p0, p1)
-    one, two = (20, 64, NZ), (16, 48, NZ)
-    keep = (24, 96, NZ)
-    c0, b0, u0, c1, b1, u1, c2, b2, p0, p1 = call(
+    zero, one, two = (40, 96, NZ), (20, 64, NZ), (16, 48, NZ)
+    down = call(
         down_kernel,
-        [keep] * 3 + [one] * 3 + [two] * 2 + [(22, 8, NZ)] * 2,
-        [(40, 96, NZ)] * 9 + [(96, NZ)] + [one] * 6 + [(64, NZ)],
+        [zero] * 7 + [one] * 7 + [two] * 2 + [(8, 8, NZ)] * 2,
+        [zero] * 2 + [(18, 96, NZ)] + [one] * 2 + [(8, 64, NZ)],
         (cond, source, y0, y1, x0, x1),
         "down",
-        56,
+        36,
     )
+    level0, level1 = down[:7], down[7:14]
+    u1, c2, b2, p0, p1 = down[13:]
     y0, y1 = swaps("gy", p0, p1)
-    u1, c2, b2, p0, p1 = call(
-        edge2_kernel, [one, two, two] + [(544, NZ)] * 2, [], (u1, c2, b2, y0, y1), "edges2", 32
-    )
+    p0, p1 = call(edge2_kernel, [(192, NZ)] * 2, [one, two, two], (u1, c2, b2, y0, y1), "edges2", 16)
     x0, x1 = swaps("gx", p0, p1)
-    u1, c2, b2, u2, packed = call(
+    *level2, u1, packed = call(
         level2_kernel,
-        [one, two, two, two, (512, NZ)],
-        [two] * 6 + [(48, NZ)] + [(2, 48, NZ)] * 2,
-        (u1, c2, b2, x0, x1),
+        [two] * 7 + [one, (512, NZ)],
+        [two] * 2 + [(2, 48, NZ)] * 3,
+        (u1, c2, b2, y0, y1, x0, x1),
         "level2",
-        32,
+        16,
     )
     whole = lax.all_to_all(packed, ("gx", "gy"), 0, 0, tiled=True)
     out, res = call(
         up_kernel,
-        [(NX, NY, NZ)] * 2,
-        [(6, 80, NZ), (6, 48, NZ), (8, 64, NZ), (96, NZ)] + [two] * 7 + [one] * 8 + [keep] * 7,
-        (whole, c2, b2, u2, c1, b1, u1, y0, y1, c0, b0, u0),
+        [block] * 2,
+        [(6, 80, NZ), (6, 48, NZ), (8, 64, NZ), (12, 96, NZ)] + [two] * 2 + [one] * 3 + [zero] * 2,
+        (whole, y0, y1, *level2, *level1[:6], u1, *level0),
         "up",
-        56,
+        36,
     )
     return out, res
 

time: 136 us -> 83.1 us (0.61)
  Pallas kernels: 61.2 us -> 22.6 us
  local copies, waits for them, and re-layouts: 10.4 us -> 0 us
  waiting for transfers between devices: 18.4 us -> 15.7 us
    pallas_call x6, Pallas kernels: 61.2 us -> 22.6 us  [call(): pl.pallas_call(body, out_shape=[jax.ShapeDtypeStruct(s, F32) for s in out...]
    unnamed x34 -> x0, local copies, waits for them, and re-layouts: 10.3 us -> none
    ppermute x4, waiting for transfers between devices: 14.9 us -> 13 us  [swaps(): late = lax.ppermute(second, axis, pairs(1))]
where the time goes in v2:
time: 83.1 us; the launch traced here: 82.9 us
  blocking collectives  27.1 us (33%)
  Pallas kernels  22.6 us (27%)
  starting transfers between devices  16.8 us (20%)
  waiting for transfers between devices  15.7 us (19%)
    all_to_all x1, blocking collectives, per_device(): whole = lax.all_to_all(packed, ('gx', 'gy'), 0, 0, tiled=True)  27.1 us
    pallas_call x6, Pallas kernels, call(): pl.pallas_call(body, out_shape=[jax.ShapeDtypeStruct(s, F32) for s in out...  22.6 us
    ppermute x4, waiting for transfers between devices, swaps(): late = lax.ppermute(second, axis, pairs(1))  13 us
    ppermute x4, starting transfers between devices, swaps(): late = lax.ppermute(second, axis, pairs(1))  8.79 us
    ppermute x4, starting transfers between devices, swaps(): return (lax.ppermute(first, axis, pairs(0)), late)  8.03 us
    ppermute x4, waiting for transfers between devices, swaps(): return (lax.ppermute(first, axis, pairs(0)), late)  2.7 us
  transfers between devices with their start and end apart: 8, of which 4 were waited for; matrix products, arithmetic and copies ran while one was open for 0% of the time, Pallas kernels for 0%

profile of v2, /device:TPU:1, one launch (start us, length us, event | category | flops | bytes accessed | tf_op | source)
XLA Modules:
  0.0 82.9 jit_solution(1893865103446022248)
XLA Ops:
  0.6 1.6 %begin.1 = (f32[16,64,128]{2,1,0:T(8,128)S(1)}, f32[16,64,128]{2,1,0:T(8,128)S(1)}, f32[32,8,128]{2,1,0:T(8,128)S(1)}, f32[32,8,128]{2,1,0:T(8,128)S(1)}) custom-call(f32[16,64,128]{2,1,0:T(8,128)} %source.1, f32[16,64,128]{2,1,0:T(8,128)} %density.1, f32[16,64,128]{2,1,0:T(8,128)} %drag.1, s32[64]{0:T(128)} %porous.1), custom_call_target="tpu_custom_call" | custom-call | tf_op jit(solution)/shard_map/begin/pallas_call | solution.py:23
  2.3 2.1 %collective-permute-start = (f32[32,8,128]{2,1,0:T(8,128)S(1)}, f32[32,8,128]{2,1,0:T(8,128)S(1)}, u32[]{:S(2)}, u32[]{:S(2)}) collective-permute-start(f32[32,8,128]{2,1,0:T(8,128)S(1)} %get-tuple-element.39), channel_id=1, source_target_pairs={{0,1},{1,0},{2,3},{3,2},{4,5},{5,4},{6,7},{7,6},{8,9},{9,8},{10,11... | collective-permute-start | bytes 393224 | tf_op jit(solution)/shard_map/ppermute | solution.py:623
  4.4 0.7 collective-permute-start.1
  5.1 2.0 %collective-permute-done.y0 = f32[32,8,128]{2,1,0:T(8,128)S(1)} collective-permute-done((f32[32,8,128]{2,1,0:T(8,128)S(1)}, f32[32,8,128]{2,1,0:T(8,128)S(1)}, u32[]{:S(2)}, u32[]{:S(2)}) %collective-permute-start) | collective-permute-done | bytes 131104 | tf_op jit(solution)/shard_map/ppermute | solution.py:623
  7.1 0.0 collective-permute-done.1.y1
  7.1 0.1 edges.1
  7.2 1.8 %collective-permute-start.2 = (f32[21,80,128]{2,1,0:T(8,128)S(1)}, f32[21,80,128]{2,1,0:T(8,128)S(1)}, u32[]{:S(2)}, u32[]{:S(2)}) collective-permute-start(f32[21,80,128]{2,1,0:T(8,128)S(1)} %get-tuple-element.41), channel_id=1, source_target_pairs={{0,4},{4,0},{8,12},{12,8},{16,20},{20,16},{24,28},{28,24},{32,36},... | collective-permute-start | bytes 2580488 | tf_op jit(solution)/shard_map/ppermute | solution.py:623
  9.0 3.4 %collective-permute-start.3 = (f32[21,80,128]{2,1,0:T(8,128)S(1)}, f32[21,80,128]{2,1,0:T(8,128)S(1)}, u32[]{:S(2)}, u32[]{:S(2)}) collective-permute-start(f32[21,80,128]{2,1,0:T(8,128)S(1)} %get-tuple-element.42), channel_id=1, source_target_pairs={{4,8},{8,4},{12,16},{16,12},{20,24},{24,20},{28,32},{32,28},{36,40... | collective-permute-start | bytes 2580488 | tf_op jit(solution)/shard_map/ppermute | solution.py:622
  12.4 0.0 collective-permute-done.2.x0
  12.4 10.7 %collective-permute-done.3.x1 = f32[21,80,128]{2,1,0:T(8,128)S(1)} collective-permute-done((f32[21,80,128]{2,1,0:T(8,128)S(1)}, f32[21,80,128]{2,1,0:T(8,128)S(1)}, u32[]{:S(2)}, u32[]{:S(2)}) %collective-permute-start.3) | collective-permute-done | bytes 860192 | tf_op jit(solution)/shard_map/ppermute | solution.py:622
  23.1 9.0 %down.1 = (f32[40,96,128]{2,1,0:T(8,128)S(1)}, f32[40,96,128]{2,1,0:T(8,128)S(1)}, f32[40,96,128]{2,1,0:T(8,128)S(1)}, f32[40,96,128]{2,1,0:T(8,128)S(1)}, f32[4...) custom-call(f32[16,64,128]{2,1,0:T(8,128)S(1)} %get-tuple-element.37, ...), custom_call_target="tpu_custom_call" | custom-call | tf_op jit(solution)/shard_map/down/pallas_call | solution.py:23
  32.2 4.0 %collective-permute-start.4 = (f32[8,8,128]{2,1,0:T(8,128)S(1)}, f32[8,8,128]{2,1,0:T(8,128)S(1)}, u32[]{:S(2)}, u32[]{:S(2)}) collective-permute-start(f32[8,8,128]{2,1,0:T(8,128)S(1)} %get-tuple-element.46), channel_id=1, source_target_pairs={{0,1},{1,0},{2,3},{3,2},{4,5},{5,4},{6,7},{7,6},{8,9},{9,8},{10,11... | collective-permute-start | bytes 98312 | tf_op jit(solution)/shard_map/ppermute | solution.py:623
  36.2 0.7 collective-permute-start.5
  36.8 0.6 collective-permute-done.4.y0
  37.5 0.0 collective-permute-done.5.y1
  37.5 0.2 edges2.1
  37.7 0.1 collective-permute-start.6
  37.7 4.1 %collective-permute-start.7 = (f32[192,128]{1,0:T(8,128)S(1)}, f32[192,128]{1,0:T(8,128)S(1)}, u32[]{:S(2)}, u32[]{:S(2)}) collective-permute-start(f32[192,128]{1,0:T(8,128)S(1)} %get-tuple-element.49), channel_id=1, source_target_pairs={{4,8},{8,4},{12,16},{16,12},{20,24},{24,20},{28,32},{32,28},{36,40... | collective-permute-start | bytes 294920 | tf_op jit(solution)/shard_map/ppermute | solution.py:622
  41.9 0.0 collective-permute-done.6.x0
  41.9 2.3 %collective-permute-done.7.x1 = f32[192,128]{1,0:T(8,128)S(1)} collective-permute-done((f32[192,128]{1,0:T(8,128)S(1)}, f32[192,128]{1,0:T(8,128)S(1)}, u32[]{:S(2)}, u32[]{:S(2)}) %collective-permute-start.7) | collective-permute-done | bytes 98336 | tf_op jit(solution)/shard_map/ppermute | solution.py:622
  44.2 1.2 %level2.1 = (f32[16,48,128]{2,1,0:T(8,128)S(1)}, f32[16,48,128]{2,1,0:T(8,128)S(1)}, f32[16,48,128]{2,1,0:T(8,128)S(1)}, f32[16,48,128]{2,1,0:T(8,128)S(1)}, f32...) custom-call(f32[20,64,128]{2,1,0:T(8,128)S(1)} %get-tuple-element.43, ...), custom_call_target="tpu_custom_call" | custom-call | tf_op jit(solution)/shard_map/level2/pallas_call | solution.py:23
  45.3 27.1 %all_to_all.11 = f32[128,4,128]{2,1,0:T(4,128)S(1)} all-to-all(f32[128,4,128]{2,1,0:T(4,128)S(1)} %bitcast.3), channel_id=1, replica_groups=mesh['gx'=32,'gy'=4] {'gx','gy'}, dimensions={0} | all-to-all | bytes 524288 | tf_op jit(solution)/shard_map/all_to_all | solution.py:663
  72.4 10.5 %up.1 = (f32[16,64,128]{2,1,0:T(8,128)}, f32[16,64,128]{2,1,0:T(8,128)}) custom-call(f32[512,128]{1,0:T(8,128)S(1)} %bitcast.2, f32[8,8,128]{2,1,0:T(8,128)S(1)} %collective-permute-done.4.y0, f32[8,8,128]{2,1,0:T(8,128)S(1)} %collective-permute-done.5.y1, f32[16,48,128]{2,1,0:T(8,128)S(1)} %get-tuple-element.51.hx, ...), custom_call_target="tpu_custom_call" | custom-call | tf_op jit(solution)/shard_map/up/pallas_call | solution.py:23
Async XLA Ops:
  2.3 4.8 %collective-permute-start = (f32[32,8,128]{2,1,0:T(8,128)S(1)}, f32[32,8,128]{2,1,0:T(8,128)S(1)}, u32[]{:S(2)}, u32[]{:S(2)}) collective-permute-start(f32[32,8,128]{2,1,0:T(8,128)S(1)} %get-tuple-element.39), channel_id=1, source_target_pairs={{0,1},{1,0},{2,3},{3,2},{4,5},{5,4},{6,7},{7,6},{8,9},{9,8},{10,11... | collective-permute-start | bytes 393224 | tf_op jit(solution)/shard_map/ppermute | solution.py:623
  4.4 2.7 %collective-permute-start.1 = (f32[32,8,128]{2,1,0:T(8,128)S(1)}, f32[32,8,128]{2,1,0:T(8,128)S(1)}, u32[]{:S(2)}, u32[]{:S(2)}) collective-permute-start(f32[32,8,128]{2,1,0:T(8,128)S(1)} %get-tuple-element.40), channel_id=1, source_target_pairs={{1,2},{2,1},{5,6},{6,5},{9,10},{10,9},{13,14},{14,13},{17,18},{18,... | collective-permute-start | bytes 393224 | tf_op jit(solution)/shard_map/ppermute | solution.py:622
  7.2 5.2 %collective-permute-start.2 = (f32[21,80,128]{2,1,0:T(8,128)S(1)}, f32[21,80,128]{2,1,0:T(8,128)S(1)}, u32[]{:S(2)}, u32[]{:S(2)}) collective-permute-start(f32[21,80,128]{2,1,0:T(8,128)S(1)} %get-tuple-element.41), channel_id=1, source_target_pairs={{0,4},{4,0},{8,12},{12,8},{16,20},{20,16},{24,28},{28,24},{32,36},... | collective-permute-start | bytes 2580488 | tf_op jit(solution)/shard_map/ppermute | solution.py:623
  9.0 14.1 %collective-permute-start.3 = (f32[21,80,128]{2,1,0:T(8,128)S(1)}, f32[21,80,128]{2,1,0:T(8,128)S(1)}, u32[]{:S(2)}, u32[]{:S(2)}) collective-permute-start(f32[21,80,128]{2,1,0:T(8,128)S(1)} %get-tuple-element.42), channel_id=1, source_target_pairs={{4,8},{8,4},{12,16},{16,12},{20,24},{24,20},{28,32},{32,28},{36,40... | collective-permute-start | bytes 2580488 | tf_op jit(solution)/shard_map/ppermute | solution.py:622
  32.2 5.3 %collective-permute-start.4 = (f32[8,8,128]{2,1,0:T(8,128)S(1)}, f32[8,8,128]{2,1,0:T(8,128)S(1)}, u32[]{:S(2)}, u32[]{:S(2)}) collective-permute-start(f32[8,8,128]{2,1,0:T(8,128)S(1)} %get-tuple-element.46), channel_id=1, source_target_pairs={{0,1},{1,0},{2,3},{3,2},{4,5},{5,4},{6,7},{7,6},{8,9},{9,8},{10,11... | collective-permute-start | bytes 98312 | tf_op jit(solution)/shard_map/ppermute | solution.py:623
  36.2 1.3 %collective-permute-start.5 = (f32[8,8,128]{2,1,0:T(8,128)S(1)}, f32[8,8,128]{2,1,0:T(8,128)S(1)}, u32[]{:S(2)}, u32[]{:S(2)}) collective-permute-start(f32[8,8,128]{2,1,0:T(8,128)S(1)} %get-tuple-element.47), channel_id=1, source_target_pairs={{1,2},{2,1},{5,6},{6,5},{9,10},{10,9},{13,14},{14,13},{17,18},{18,... | collective-permute-start | bytes 98312 | tf_op jit(solution)/shard_map/ppermute | solution.py:622
  37.7 4.2 %collective-permute-start.6 = (f32[192,128]{1,0:T(8,128)S(1)}, f32[192,128]{1,0:T(8,128)S(1)}, u32[]{:S(2)}, u32[]{:S(2)}) collective-permute-start(f32[192,128]{1,0:T(8,128)S(1)} %get-tuple-element.48), channel_id=1, source_target_pairs={{0,4},{4,0},{8,12},{12,8},{16,20},{20,16},{24,28},{28,24},{32,36},... | collective-permute-start | bytes 294920 | tf_op jit(solution)/shard_map/ppermute | solution.py:623
  37.7 6.4 %collective-permute-start.7 = (f32[192,128]{1,0:T(8,128)S(1)}, f32[192,128]{1,0:T(8,128)S(1)}, u32[]{:S(2)}, u32[]{:S(2)}) collective-permute-start(f32[192,128]{1,0:T(8,128)S(1)} %get-tuple-element.49), channel_id=1, source_target_pairs={{4,8},{8,4},{12,16},{16,12},{20,24},{24,20},{28,32},{32,28},{36,40... | collective-permute-start | bytes 294920 | tf_op jit(solution)/shard_map/ppermute | solution.py:622

commit v3 on v2

--- a/solution.py
+++ b/solution.py
@@ -18,7 +18,7 @@
 HBM = pl.BlockSpec(memory_space=pltpu.HBM)
 
 
-def call(body, outs, scratch, args, name, vmem, hbm=0):
+def call(body, outs, scratch, args, name, vmem, hbm=0, cost=0):
     args = [pltpu.with_memory_space_constraint(a, pltpu.HBM) for a in args[:hbm]] + list(args[hbm:])
     return pl.pallas_call(
         body,
@@ -28,6 +28,7 @@
         scratch_shapes=[pltpu.VMEM(s, F32) if isinstance(s, tuple) else s for s in scratch],
         compiler_params=pltpu.CompilerParams(vmem_limit_bytes=vmem * 2**20),
         name=name,
+        cost_estimate=pl.CostEstimate(flops=cost, bytes_accessed=0, transcendentals=0) if cost else None,
     )(*args)
 
 
@@ -87,99 +88,102 @@
         body(x)
 
 
-def chunks(ys, ye, size):
-    return [(y, min(size, ye - y)) for y in range(ys, ye, size)]
-
-
 class Level:
-    def __init__(self, depth, c, b, fx, fy, fz, fzm, w, ys, ye, size):
+    def __init__(self, depth, c, b, fx, fy, fz, w, ys, ye):
         self.h = H0 * 4.0**depth
         self.s = 2**depth
-        self.c, self.b, self.fx, self.fy, self.fz, self.fzm, self.w = c, b, fx, fy, fz, fzm, w
-        self.parts = chunks(ys, ye, size)
+        self.c, self.b, self.fx, self.fy, self.fz, self.w = c, b, fx, fy, fz, w
+        self.ys, self.n = ys, ye - ys
 
     def faces(self, lo, hi):
+        here, above = pl.ds(self.ys, self.n), pl.ds(self.ys + 1, self.n)
+
         def body(x):
-            for y, n in self.parts:
-                c = self.c[x, pl.ds(y, n), :]
-                self.fx[x, pl.ds(y, n), :] = harmonic(c, self.c[x + 1, pl.ds(y, n), :])
-                self.fy[x, pl.ds(y, n), :] = harmonic(c, self.c[x, pl.ds(y + 1, n), :])
-                fz = harmonic(c, lroll(c, -self.s))
-                self.fz[x, pl.ds(y, n), :] = fz
-                self.fzm[x, pl.ds(y, n), :] = lroll(fz, self.s)
+            c = self.c[x, here, :]
+            twice, safe = c + c, c + 1e-30
+
+            def face(other):
+                return twice * other / (safe + other)
+
+            self.fx[x, here, :] = face(self.c[x + 1, here, :])
+            self.fy[x, here, :] = face(self.c[x, above, :])
+            self.fz[x, here, :] = face(lroll(c, -self.s))
 
         rows(lo, hi, body)
 
     def weights(self, lo, hi, start=None):
+        here, below = pl.ds(self.ys, self.n), pl.ds(self.ys - 1, self.n)
+
         def body(x):
-            for y, n in self.parts:
-                here = pl.ds(y, n)
-                d = self.fx[x, here, :] + self.fx[x - 1, here, :]
-                d = d + self.fy[x, here, :] + self.fy[x, pl.ds(y - 1, n), :]
-                d = d + self.fz[x, here, :] + self.fzm[x, here, :]
-                w = DAMP * recip(self.h + d)
-                self.w[x, here, :] = w
-                if start is not None:
-                    start[x, here, :] = w * self.b[x, here, :]
+            fz = self.fz[x, here, :]
+            d = self.fx[x, here, :] + self.fx[x - 1, here, :]
+            d = d + (self.fy[x, here, :] + self.fy[x, below, :])
+            d = d + (fz + lroll(fz, self.s))
+            w = DAMP * recip(self.h + d)
+            self.w[x, here, :] = w
+            if start is not None:
+                start[x, here, :] = w * self.b[x, here, :]
 
         rows(lo, hi, body)
 
-    def flux(self, u, x, y, n):
-        here = pl.ds(y, n)
+    def start(self, out, lo, hi):
+        here = pl.ds(self.ys, self.n)
+
+        def body(x):
+            out[x, here, :] = self.w[x, here, :] * self.b[x, here, :]
+
+        rows(lo, hi, body)
+
+    def sweep(self, u, out, lo, hi):
+        here = pl.ds(self.ys, self.n)
+        above, below = pl.ds(self.ys + 1, self.n), pl.ds(self.ys - 1, self.n)
+
+        def body(x):
+            v = u[x, here, :]
+            fz = self.fz[x, here, :]
+            acc = fz * lroll(v, -self.s) + lroll(fz * v, self.s)
+            acc = acc + (self.fx[x, here, :] * u[x + 1, here, :] + self.fx[x - 1, here, :] * u[x - 1, here, :])
+            acc = acc + (self.fy[x, here, :] * u[x, above, :] + self.fy[x, below, :] * u[x, below, :])
+            out[x, here, :] = KEEP * v + self.w[x, here, :] * (self.b[x, here, :] + acc)
+
+        rows(lo, hi, body)
+
+    def residual(self, u, x, y, n):
+        here, above, below = pl.ds(y, n), pl.ds(y + 1, n), pl.ds(y - 1, n)
         v = u[x, here, :]
-        acc = self.fx[x, here, :] * u[x + 1, here, :]
-        acc = acc + self.fx[x - 1, here, :] * u[x - 1, here, :]
-        acc = acc + self.fy[x, here, :] * u[x, pl.ds(y + 1, n), :]
-        acc = acc + self.fy[x, pl.ds(y - 1, n), :] * u[x, pl.ds(y - 1, n), :]
-        acc = acc + self.fz[x, here, :] * lroll(v, -self.s)
-        acc = acc + self.fzm[x, here, :] * lroll(v, self.s)
-        return v, acc
-
-    def sweep(self, u, out, lo, hi):
-        def body(x):
-            for y, n in self.parts:
-                here = pl.ds(y, n)
-                v, acc = self.flux(u, x, y, n)
-                out[x, here, :] = KEEP * v + self.w[x, here, :] * (self.b[x, here, :] + acc)
-
-        rows(lo, hi, body)
-
-    def residual(self, u, x, y, n):
-        here = pl.ds(y, n)
-        v = u[x, here, :]
+        flow = self.fz[x, here, :] * (lroll(v, -self.s) - v)
         r = self.b[x, here, :] - self.h * v
+        r = r + (flow - lroll(flow, self.s))
         r = r + self.fx[x, here, :] * (u[x + 1, here, :] - v)
         r = r + self.fx[x - 1, here, :] * (u[x - 1, here, :] - v)
-        r = r + self.fy[x, here, :] * (u[x, pl.ds(y + 1, n), :] - v)
-        r = r + self.fy[x, pl.ds(y - 1, n), :] * (u[x, pl.ds(y - 1, n), :] - v)
-        r = r + self.fz[x, here, :] * (lroll(v, -self.s) - v)
-        return r + self.fzm[x, here, :] * (lroll(v, self.s) - v)
-
-    def halve(self, tmp, out, count, x_to, scale):
+        r = r + self.fy[x, here, :] * (u[x, above, :] - v)
+        return r + self.fy[x, below, :] * (u[x, below, :] - v)
+
+    def halve(self, tmp, out, lo, hi, x_to, scale):
         half = tmp.shape[1] // 2
 
         def body(k):
             t = tmp[k, pl.ds(0, half, stride=2), :] + tmp[k, pl.ds(1, half, stride=2), :]
             out[x_to + k, pl.ds(8, half), :] = scale * pair_lanes(t, self.s)
 
-        rows(0, count, body)
-
-    def restrict(self, u, tmp, out, count, x_from, x_to):
+        rows(lo, hi, body)
+
+    def restrict(self, u, tmp, out, lo, hi, x_from, x_to):
         def body(k):
             x = x_from + 2 * k
-            for y, n in self.parts:
-                tmp[k, pl.ds(y, n), :] = self.residual(u, x, y, n) + self.residual(u, x + 1, y, n)
-
-        rows(0, count, body, 4)
-        self.halve(tmp, out, count, x_to, 0.5)
-
-    def restrict_c(self, tmp, out, count, x_from, x_to):
+            both = self.residual(u, x, self.ys, self.n) + self.residual(u, x + 1, self.ys, self.n)
+            tmp[k, pl.ds(self.ys, self.n), :] = both
+
+        rows(lo, hi, body, 4)
+        self.halve(tmp, out, lo, hi, x_to, 0.5)
+
+    def restrict_c(self, tmp, out, lo, hi, x_from, x_to):
         def body(k):
             x = x_from + 2 * k
             tmp[k] = self.c[x] + self.c[x + 1]
 
-        rows(0, count, body)
-        self.halve(tmp, out, count, x_to, 0.125)
+        rows(lo, hi, body)
+        self.halve(tmp, out, lo, hi, x_to, 0.125)
 
 
 def odd(axis):
@@ -189,7 +193,7 @@
 PARTS = 4
 
 
-def begin_kernel(source, density, drag, porous, cond, rhs, ypack0, ypack1, dens, dra, por, sem, esem):
+def begin_kernel(source, density, drag, porous, cond, rhs, ypack0, ypack1, xpack0, xpack1, dens, dra, por, sem, esem):
     o = odd("gy")
     at0 = pl.multiple_of((1 - o) * (NY - 8), 8)
     at1 = pl.multiple_of(o * (NY - 8), 8)
@@ -208,6 +212,11 @@
         edges[-1].start()
     edges.append(pltpu.make_async_copy(source, rhs, esem.at[2]))
     edges[-1].start()
+    ox = odd("gx")
+    for j, (last, pack) in enumerate(((1 - ox, xpack0), (ox, xpack1))):
+        rhs_rows = source.at[pl.ds(last * (NX - 10), 10)]
+        edges.append(pltpu.make_async_copy(rhs_rows, pack.at[pl.ds(11, 10)], esem.at[4 + j]))
+        edges[-1].start()
     first.wait()
     shape = (NY, NZ)
     line = jnp.broadcast_to(por[...].astype(F32)[None], (NY, NY))
@@ -220,30 +229,22 @@
             cond[x] = recip(dens[x] * (1.0 + dra[x] * mask))
             ypack0[x] = cond[x, pl.ds(at0, 8), :]
             ypack1[x] = cond[x, pl.ds(at1, 8), :]
+    for last, pack in ((1 - ox, xpack0), (ox, xpack1)):
+        for k in range(11):
+            pack[k] = cond[k + last * (NX - 11)]
     for edge in edges:
         edge.wait()
 
 
-def edge_kernel(cond, source, y0, y1, xpack0, xpack1):
+def corner_kernel(y0, y1, xpack0, xpack1):
     ox, oy = odd("gx"), odd("gy")
-    at0 = pl.multiple_of((1 - oy) * (NY + 8), 8)
-    at1 = pl.multiple_of(oy * (NY + 8), 8)
-
-    def put(pack, row, field, x, base):
-        pack[row, pl.ds(8, NY), :] = field[x]
-        pack[row, pl.ds(at0, 8), :] = y0[base + x]
-        pack[row, pl.ds(at1, 8), :] = y1[base + x]
-
-    def body_c(k):
-        put(xpack0, k, cond, k + (1 - ox) * (NX - 11), 0)
-        put(xpack1, k, cond, k + ox * (NX - 11), 0)
-
-    def body_b(k):
-        put(xpack0, 11 + k, source, k + (1 - ox) * (NX - 10), NX)
-        put(xpack1, 11 + k, source, k + ox * (NX - 10), NX)
-
-    rows(0, 11, body_c)
-    rows(0, 10, body_b)
+    at0 = pl.multiple_of((1 - oy) * 8, 8)
+    at1 = pl.multiple_of(oy * 8, 8)
+    for pack, last in ((xpack0, 1 - ox), (xpack1, ox)):
+        for k in range(21):
+            x = k + last * (NX - 11) if k < 11 else NX + k - 11 + last * (NX - 10)
+            pack[k, pl.ds(at0, 8), :] = y0[x]
+            pack[k, pl.ds(at1, 8), :] = y1[x]
 
 
 X0, Y0 = 12, 16
@@ -251,79 +252,88 @@
 X2, Y2 = 6, 16
 
 
+def levels_down(c, b, fx, fy, fz, w, c1, b1, gx_, gy_, gz_, gw_):
+    top = Level(0, c, b, fx, fy, fz, w, 8, 88)
+    return top, Level(1, c1, b1, gx_, gy_, gz_, gw_, 8, 56)
+
+
+def inner_kernel(cond, source, y0, y1, c, b, fx, fy, fz, w, ua, ub, c1, b1, gx_, gy_, gz_, gw_, tmp):
+    oy = odd("gy")
+    at0 = pl.multiple_of(8 + (1 - oy) * (NY + 8), 8)
+    at1 = pl.multiple_of(8 + oy * (NY + 8), 8)
+
+    def own(x):
+        c[1 + x, pl.ds(Y0, NY), :] = cond[x]
+        c[1 + x, pl.ds(at0, 8), :] = y0[x]
+        c[1 + x, pl.ds(at1, 8), :] = y1[x]
+        b[1 + x, pl.ds(Y0, NY), :] = source[x]
+        b[1 + x, pl.ds(at0, 8), :] = y0[NX + x]
+        b[1 + x, pl.ds(at1, 8), :] = y1[NX + x]
+
+    rows(0, NX, own)
+    top, mid = levels_down(c, b, fx, fy, fz, w, c1, b1, gx_, gy_, gz_, gw_)
+    top.faces(1, 17)
+    top.weights(2, 16, ua)
+    top.sweep(ua, ub, 3, 15)
+    top.restrict_c(tmp, c1, 0, 8, 1, 1)
+    top.restrict(ub, tmp, b1, 2, 6, 1, 1)
+    mid.faces(1, 9)
+    mid.weights(2, 8)
+
+
 def down_kernel(
-    cond, source, y0, y1, x0, x1,
-    fx, fy, fz, fzm, w, b, ub, gx_, gy_, gz_, gzm_, gw_, b1, u1, c2, b2, ypack0, ypack1,
-    c, ua, tmp, c1, ga_, tmp1,
+    x0, x1, k0, k1, c_in, b_in, fx_in, fy_in, fz_in, w_in, ua_in, ub_in, c1_in, b1_in, gx_in, gy_in, gz_in, gw_in,
+    fx, fy, fz, w, b, ub, gx_, gy_, gz_, gw_, b1, u1, c2, b2, ypack0, ypack1,
+    c, ua, c1, ga_, tmp, ctmp, tmp1,
 ):
     ox, oy = odd("gx"), odd("gy")
-    at0 = pl.multiple_of(8 + (1 - oy) * (NY + 8), 8)
-    at1 = pl.multiple_of(8 + oy * (NY + 8), 8)
-
-    def own(x):
-        c[X0 + x, pl.ds(Y0, NY), :] = cond[x]
-        c[X0 + x, pl.ds(at0, 8), :] = y0[x]
-        c[X0 + x, pl.ds(at1, 8), :] = y1[x]
-        b[X0 + x, pl.ds(Y0, NY), :] = source[x]
-        b[X0 + x, pl.ds(at0, 8), :] = y0[NX + x]
-        b[X0 + x, pl.ds(at1, 8), :] = y1[NX + x]
-
-    rows(0, NX, own)
-
-    def halo_c(k):
-        c[k + 1 + (1 - ox) * (11 + NX), pl.ds(8, 80), :] = x0[k]
-        c[k + 1 + ox * (11 + NX), pl.ds(8, 80), :] = x1[k]
-
-    def halo_b(k):
-        b[k + 2 + (1 - ox) * (10 + NX), pl.ds(8, 80), :] = x0[11 + k]
-        b[k + 2 + ox * (10 + NX), pl.ds(8, 80), :] = x1[11 + k]
-
-    rows(0, 11, halo_c)
-    rows(0, 10, halo_b)
-    zero = jnp.zeros((8, NZ), F32)
-
-    def pads(x):
-        c[x, pl.ds(0, 8), :] = zero
-        c[x, pl.ds(88, 8), :] = zero
-        fy[x, pl.ds(0, 8), :] = zero
-
-    rows(0, 40, pads)
-
-    top = Level(0, c, b, fx, fy, fz, fzm, w, 8, 88, 40)
-    top.faces(1, 39)
-    top.weights(2, 38, ua)
-    top.sweep(ua, ub, 3, 37)
-
-    def clear1(x):
-        for ref in (c1, b1, u1):
-            ref[x] = jnp.zeros((64, NZ), F32)
-        gy_[x, pl.ds(0, 8), :] = zero
-
-    rows(0, 20, clear1)
-
-    def clear2(x):
-        for ref in (c2, b2):
-            ref[x] = jnp.zeros((48, NZ), F32)
-
-    rows(0, 16, clear2)
-
-    def clear_tmp(x):
-        tmp[x, pl.ds(0, 8), :] = zero
-        tmp[x, pl.ds(88, 8), :] = zero
-
-    rows(0, 18, clear_tmp)
-    for x in range(8):
-        tmp1[x, pl.ds(0, 8), :] = zero
-        tmp1[x, pl.ds(56, 8), :] = zero
-    top.restrict(ub, tmp, b1, 16, 4, 2)
-    top.restrict_c(tmp, c1, 18, 2, 1)
-
-    mid = Level(1, c1, b1, gx_, gy_, gz_, gzm_, gw_, 8, 56, 48)
-    mid.faces(1, 19)
-    mid.weights(2, 18, ga_)
+    here, here1 = pl.ds(8, 80), pl.ds(8, 48)
+
+    def halo(ref, row, x, k, pack):
+        ref[row, pl.ds(Y0, NY), :] = x[k]
+        ref[row, pl.ds(8, 8), :] = pack[k, pl.ds(0, 8), :]
+        ref[row, pl.ds(88 - 8, 8), :] = pack[k, pl.ds(8, 8), :]
+
+    for x, pack, up in ((x0, k0, 1 - ox), (x1, k1, ox)):
+        for k in range(11):
+            halo(c, k + 1 + up * (11 + NX), x, k, pack)
+        for k in range(10):
+            halo(b, k + 2 + up * (10 + NX), x, 11 + k, pack)
+    for x in (1, 16):
+        c[x + 11, here, :] = c_in[x, here, :]
+    for x in (2, 3, 14, 15):
+        ua[x + 11, here, :] = ua_in[x, here, :]
+
+    def fill(x):
+        for ref, src in ((fx, fx_in), (fy, fy_in), (fz, fz_in), (w, w_in), (b, b_in), (ub, ub_in)):
+            ref[x + 11, here, :] = src[x, here, :]
+
+    rows(1, 17, fill)
+    for x in range(1, 9):
+        c1[x + 5, here1, :] = c1_in[x, here1, :]
+        for ref, src in ((gx_, gx_in), (gy_, gy_in), (gz_, gz_in), (gw_, gw_in), (b1, b1_in)):
+            ref[x + 5, here1, :] = src[x, here1, :]
+
+    top, mid = levels_down(c, b, fx, fy, fz, w, c1, b1, gx_, gy_, gz_, gw_)
+    top.faces(1, 12)
+    top.faces(27, 39)
+    top.weights(2, 13, ua)
+    top.weights(27, 38, ua)
+    top.sweep(ua, ub, 3, 14)
+    top.sweep(ua, ub, 26, 37)
+    top.restrict_c(ctmp, c1, 0, 5, 2, 1)
+    top.restrict_c(ctmp, c1, 13, 18, 2, 1)
+    top.restrict(ub, tmp, b1, 0, 6, 4, 2)
+    top.restrict(ub, tmp, b1, 10, 16, 4, 2)
+
+    mid.faces(1, 6)
+    mid.faces(13, 19)
+    mid.weights(2, 7)
+    mid.weights(13, 18)
+    mid.start(ga_, 2, 18)
     mid.sweep(ga_, u1, 3, 17)
-    mid.restrict(u1, tmp1, b2, 6, 4, 5)
-    mid.restrict_c(tmp1, c2, 8, 2, 4)
+    mid.restrict(u1, tmp1, b2, 0, 6, 4, 5)
+    mid.restrict_c(tmp1, c2, 0, 8, 2, 4)
 
     e0 = Y1 + (1 - oy) * 28
     e1 = Y1 + oy * 28
@@ -396,16 +406,12 @@
 
 def level2_kernel(
     u1_in, c2_in, b2_in, y0, y1, x0, x1,
-    fx, fy, fz, fzm, w, b2, u2, u1, gather,
+    fx, fy, fz, w, b2, u2, u1, gather,
     c2, ua, tmp, b3, c3,
 ):
     ox, oy = odd("gx"), odd("gy")
-    zero = jnp.zeros((8, NZ), F32)
-    copy_rows([(u1_in, u1)], 0, 20)
-    copy_rows([(c2_in, c2), (b2_in, b2)], 0, 16)
-    for x in range(16):
-        u2[x] = jnp.zeros((48, NZ), F32)
-        fy[x, pl.ds(0, 8), :] = zero
+    copy_rows([(u1_in, u1)], X1, X1 + 8)
+    copy_rows([(c2_in, c2), (b2_in, b2)], X2 - 2, X2 + 6)
     set_y1(u1, y0, y1, oy, 0)
     set_y2(c2, b2, y0, y1, oy)
     for pack, up in ((x0, 1 - ox), (x1, ox)):
@@ -420,15 +426,12 @@
         for k in range(5):
             b2[X2 - 5 + k + up * 9, pl.ds(8, 32), :] = t[6 + k]
 
-    low = Level(2, c2, b2, fx, fy, fz, fzm, w, 8, 40, 32)
+    low = Level(2, c2, b2, fx, fy, fz, w, 8, 40)
     low.faces(0, 15)
     low.weights(1, 15, ua)
     low.sweep(ua, u2, 2, 14)
-    for x in range(2):
-        tmp[x, pl.ds(0, 8), :] = zero
-        tmp[x, pl.ds(40, 8), :] = zero
-    low.restrict(u2, tmp, b3, 2, X2, 0)
-    low.restrict_c(tmp, c3, 2, X2, 0)
+    low.restrict(u2, tmp, b3, 0, 2, X2, 0)
+    low.restrict_c(tmp, c3, 0, 2, X2, 0)
     both = jnp.concatenate(
         [b3[0, pl.ds(16, 8), :], b3[1, pl.ds(16, 8), :], c3[0, pl.ds(16, 8), :], c3[1, pl.ds(16, 8), :]], 0
     )
@@ -528,15 +531,14 @@
 
 def up_kernel(
     gather, y0, y1,
-    hx, hy, hz, hzm, hw, b2, u2,
-    gx_, gy_, gz_, gzm_, gw_, b1_in, u1,
-    fx, fy, fz, fzm, w, b, u0,
+    hx, hy, hz, hw, b2, u2,
+    gx_, gy_, gz_, gw_, b1_in, u1,
+    fx, fy, fz, w, b, u0,
     out, res,
     s3, e2, e1, e0, ha, hb, b1, ga_, gb_, ua, ub,
 ):
     ix, iy = lax.axis_index("gx"), lax.axis_index("gy")
     oy = iy % 2
-    zero = jnp.zeros((8, NZ), F32)
 
     def field(k):
         return jnp.stack(
@@ -566,9 +568,9 @@
         e2[k, pl.ds(0, 24, stride=2), :] = t
         e2[k, pl.ds(1, 24, stride=2), :] = t
 
-    for x in range(16):
-        ha[x] = u2[x] + e2[(x - 2) // 2] if 2 <= x < 14 else jnp.zeros((48, NZ), F32)
-    low = Level(2, None, b2, hx, hy, hz, hzm, hw, 8, 40, 32)
+    for x in range(2, 14):
+        ha[x] = u2[x] + e2[(x - 2) // 2]
+    low = Level(2, None, b2, hx, hy, hz, hw, 8, 40)
     low.sweep(ha, hb, 3, 13)
     low.sweep(hb, ha, 4, 12)
 
@@ -587,7 +589,7 @@
             ga_[2 + 2 * k + j] = u1[2 + 2 * k + j] + e1[k]
 
     rows(0, 8, add1)
-    mid = Level(1, None, b1, gx_, gy_, gz_, gzm_, gw_, 8, 56, 48)
+    mid = Level(1, None, b1, gx_, gy_, gz_, gw_, 8, 56)
     mid.sweep(ga_, gb_, 3, 17)
     mid.sweep(gb_, ga_, 4, 16)
 
@@ -602,7 +604,7 @@
 
     rows(0, 12, grow0, 4)
     rows(0, 12, add0, 4)
-    top = Level(0, None, b, fx, fy, fz, fzm, w, 8, 88, 40)
+    top = Level(0, None, b, fx, fy, fz, w, 8, 88)
     top.sweep(ua, ub, 10, 30)
     top.sweep(ub, ua, 11, 29)
 
@@ -624,37 +626,42 @@
 
 
 def per_device(source, density, drag, porous_rows):
-    sems = [pltpu.SemaphoreType.DMA((2, PARTS)), pltpu.SemaphoreType.DMA((4,))]
+    sems = [pltpu.SemaphoreType.DMA((2, PARTS)), pltpu.SemaphoreType.DMA((6,))]
     block = (NX, NY, NZ)
-    cond, source, p0, p1 = call(
+    cond, source, p0, p1, q0, q1 = call(
         begin_kernel,
-        [block, block, (32, 8, NZ), (32, 8, NZ)],
+        [block, block, (32, 8, NZ), (32, 8, NZ)] + [(21, NY, NZ)] * 2,
         [block, block, pltpu.VMEM((NY,), jnp.int32)] + sems,
         (source, density, drag, porous_rows),
         "begin",
         16,
         4,
     )
+    x0, x1 = swaps("gx", q0, q1)
     y0, y1 = swaps("gy", p0, p1)
-    p0, p1 = call(edge_kernel, [(21, 80, NZ)] * 2, [], (cond, source, y0, y1), "edges", 16)
-    x0, x1 = swaps("gx", p0, p1)
+    p0, p1 = call(corner_kernel, [(21, 16, NZ)] * 2, [], (y0, y1), "corners", 16)
+    k0, k1 = swaps("gx", p0, p1)
     zero, one, two = (40, 96, NZ), (20, 64, NZ), (16, 48, NZ)
+    small, small1 = (18, 96, NZ), (10, 64, NZ)
+    inner = call(
+        inner_kernel, [small] * 8 + [small1] * 6, [(8, 96, NZ)], (cond, source, y0, y1), "inner", 16, 0, 10**7
+    )
     down = call(
         down_kernel,
-        [zero] * 7 + [one] * 7 + [two] * 2 + [(8, 8, NZ)] * 2,
-        [zero] * 2 + [(18, 96, NZ)] + [one] * 2 + [(8, 64, NZ)],
-        (cond, source, y0, y1, x0, x1),
+        [zero] * 6 + [one] * 6 + [two] * 2 + [(8, 8, NZ)] * 2,
+        [zero] * 2 + [one] * 2 + [(16, 96, NZ), (18, 96, NZ), (8, 64, NZ)],
+        (x0, x1, k0, k1, *inner),
         "down",
-        36,
+        24,
     )
-    level0, level1 = down[:7], down[7:14]
-    u1, c2, b2, p0, p1 = down[13:]
+    level0, level1 = down[:6], down[6:12]
+    u1, c2, b2, p0, p1 = down[11:]
     y0, y1 = swaps("gy", p0, p1)
     p0, p1 = call(edge2_kernel, [(192, NZ)] * 2, [one, two, two], (u1, c2, b2, y0, y1), "edges2", 16)
     x0, x1 = swaps("gx", p0, p1)
     *level2, u1, packed = call(
         level2_kernel,
-        [two] * 7 + [one, (512, NZ)],
+        [two] * 6 + [one, (512, NZ)],
         [two] * 2 + [(2, 48, NZ)] * 3,
         (u1, c2, b2, y0, y1, x0, x1),
         "level2",
@@ -665,9 +672,9 @@
         up_kernel,
         [block] * 2,
         [(6, 80, NZ), (6, 48, NZ), (8, 64, NZ), (12, 96, NZ)] + [two] * 2 + [one] * 3 + [zero] * 2,
-        (whole, y0, y1, *level2, *level1[:6], u1, *level0),
+        (whole, y0, y1, *level2, *level1[:5], u1, *level0),
         "up",
-        36,
+        24,
     )
     return out, res
 

time: 83.1 us -> 74.1 us (0.89)
  waiting for transfers between devices: 15.7 us -> 5.91 us
  starting transfers between devices: 16.8 us -> 20.9 us
  Pallas kernels: 22.6 us -> 19.1 us
    ppermute x4 -> x5, waiting for transfers between devices: 13 us -> 3.31 us  [swaps(): late = lax.ppermute(second, axis, pairs(1))]
    ppermute x4 -> x5, starting transfers between devices: 8.79 us -> 14 us  [swaps(): late = lax.ppermute(second, axis, pairs(1))]
    pallas_call x6 -> x7, Pallas kernels: 22.6 us -> 19.1 us  [call(): pl.pallas_call(body, out_shape=[jax.ShapeDtypeStruct(s, F32) for s in out...]
    ppermute x4 -> x5, starting transfers between devices: 8.03 us -> 6.87 us  [swaps(): return (lax.ppermute(first, axis, pairs(0)), late)]
    ppermute x4 -> x5, waiting for transfers between devices: 2.7 us -> 2.6 us  [swaps(): return (lax.ppermute(first, axis, pairs(0)), late)]
  transfers between devices with their start and end apart: 8 -> 10, of which waited for: 4 -> 4; matrix products, arithmetic and copies ran while one was open for 0% -> 0% of each run, Pallas kernels for 0% -> 3%
where the time goes in v3:
time: 74.1 us; the launch traced here: 73.8 us
  blocking collectives  27.2 us (37%)
  starting transfers between devices  20.9 us (28%)
  Pallas kernels  19.1 us (26%)
  waiting for transfers between devices  5.91 us (8%)
  between operations  0.75 us (1%)
    all_to_all x1, blocking collectives, per_device(): whole = lax.all_to_all(packed, ('gx', 'gy'), 0, 0, tiled=True)  27.2 us
    pallas_call x7, Pallas kernels, call(): pl.pallas_call(body, out_shape=[jax.ShapeDtypeStruct(s, F32) for s in out...  19.1 us
    ppermute x5, starting transfers between devices, swaps(): late = lax.ppermute(second, axis, pairs(1))  14 us
    ppermute x5, starting transfers between devices, swaps(): return (lax.ppermute(first, axis, pairs(0)), late)  6.87 us
    ppermute x5, waiting for transfers between devices, swaps(): late = lax.ppermute(second, axis, pairs(1))  3.31 us
    ppermute x5, waiting for transfers between devices, swaps(): return (lax.ppermute(first, axis, pairs(0)), late)  2.6 us
  transfers between devices with their start and end apart: 10, of which 4 were waited for; matrix products, arithmetic and copies ran while one was open for 0% of the time, Pallas kernels for 3%

profile of v3, /device:TPU:1, one launch (start us, length us, event | category | flops | bytes accessed | tf_op | source)
XLA Modules:
  0.0 73.8 jit_solution(6767393939650288714)
XLA Ops:
  0.6 1.9 %begin.1 = (f32[16,64,128]{2,1,0:T(8,128)S(1)}, f32[16,64,128]{2,1,0:T(8,128)S(1)}, f32[32,8,128]{2,1,0:T(8,128)S(1)}, f32[32,8,128]{2,1,0:T(8,128)S(1)}, f32[21...) custom-call(f32[16,64,128]{2,1,0:T(8,128)} %source.1, f32[16,64,128]{2,1,0:T(8,128)} %density.1, f32[16,64,128]{2,1,0:T(8,128)} %drag.1, ...), custom_call_target="tpu_custom_call" | custom-call | tf_op jit(solution)/shard_map/begin/pallas_call | solution.py:23
  2.5 1.5 %collective-permute-start = (f32[21,64,128]{2,1,0:T(8,128)S(1)}, f32[21,64,128]{2,1,0:T(8,128)S(1)}, u32[]{:S(2)}, u32[]{:S(2)}) collective-permute-start(f32[21,64,128]{2,1,0:T(8,128)S(1)} %get-tuple-element.50), channel_id=1, source_target_pairs={{0,4},{4,0},{8,12},{12,8},{16,20},{20,16},{24,28},{28,24},{32,36},... | collective-permute-start | bytes 2064392 | tf_op jit(solution)/shard_map/ppermute | solution.py:625
  4.0 3.2 %collective-permute-start.1 = (f32[21,64,128]{2,1,0:T(8,128)S(1)}, f32[21,64,128]{2,1,0:T(8,128)S(1)}, u32[]{:S(2)}, u32[]{:S(2)}) collective-permute-start(f32[21,64,128]{2,1,0:T(8,128)S(1)} %get-tuple-element.51), channel_id=1, source_target_pairs={{4,8},{8,4},{12,16},{16,12},{20,24},{24,20},{28,32},{32,28},{36,40... | collective-permute-start | bytes 2064392 | tf_op jit(solution)/shard_map/ppermute | solution.py:624
  7.2 1.3 %collective-permute-start.2 = (f32[32,8,128]{2,1,0:T(8,128)S(1)}, f32[32,8,128]{2,1,0:T(8,128)S(1)}, u32[]{:S(2)}, u32[]{:S(2)}) collective-permute-start(f32[32,8,128]{2,1,0:T(8,128)S(1)} %get-tuple-element.52), channel_id=1, source_target_pairs={{0,1},{1,0},{2,3},{3,2},{4,5},{5,4},{6,7},{7,6},{8,9},{9,8},{10,11... | collective-permute-start | bytes 393224 | tf_op jit(solution)/shard_map/ppermute | solution.py:625
  8.5 0.7 collective-permute-start.3
  9.1 1.9 %collective-permute-done.2.y0 = f32[32,8,128]{2,1,0:T(8,128)S(1)} collective-permute-done((f32[32,8,128]{2,1,0:T(8,128)S(1)}, f32[32,8,128]{2,1,0:T(8,128)S(1)}, u32[]{:S(2)}, u32[]{:S(2)}) %collective-permute-start.2) | collective-permute-done | bytes 131104 | tf_op jit(solution)/shard_map/ppermute | solution.py:625
  11.1 0.0 collective-permute-done.3.y1
  11.1 0.1 collective-permute-start.4
  11.2 5.0 %collective-permute-start.5 = (f32[21,16,128]{2,1,0:T(8,128)S(1)}, f32[21,16,128]{2,1,0:T(8,128)S(1)}, u32[]{:S(2)}, u32[]{:S(2)}) collective-permute-start(f32[21,16,128]{2,1,0:T(8,128)S(1)} %get-tuple-element.55), channel_id=1, source_target_pairs={{4,8},{8,4},{12,16},{16,12},{20,24},{24,20},{28,32},{32,28},{36,40... | collective-permute-start | bytes 516104 | tf_op jit(solution)/shard_map/ppermute | solution.py:624
  16.2 2.0 %inner.1 = (f32[18,96,128]{2,1,0:T(8,128)S(1)}, f32[18,96,128]{2,1,0:T(8,128)S(1)}, f32[18,96,128]{2,1,0:T(8,128)S(1)}, f32[18,96,128]{2,1,0:T(8,128)S(1)}, f32[...) custom-call(f32[16,64,128]{2,1,0:T(8,128)S(1)} %get-tuple-element.56, ...), custom_call_target="tpu_custom_call" | custom-call | flops 10000000 | tf_op jit(solution)/shard_map/inner/pallas_call | solution.py:23
  18.3 0.0 collective-permute-done.4.k0
  18.3 1.0 %collective-permute-done.5.k1 = f32[21,16,128]{2,1,0:T(8,128)S(1)} collective-permute-done((f32[21,16,128]{2,1,0:T(8,128)S(1)}, f32[21,16,128]{2,1,0:T(8,128)S(1)}, u32[]{:S(2)}, u32[]{:S(2)}) %collective-permute-start.5) | collective-permute-done | bytes 172064 | tf_op jit(solution)/shard_map/ppermute | solution.py:624
  19.3 0.0 collective-permute-done.x0
  19.3 0.0 collective-permute-done.1.x1
  19.3 5.7 %down.1 = (f32[40,96,128]{2,1,0:T(8,128)S(1)}, f32[40,96,128]{2,1,0:T(8,128)S(1)}, f32[40,96,128]{2,1,0:T(8,128)S(1)}, f32[40,96,128]{2,1,0:T(8,128)S(1)}, f32[4...) custom-call(f32[21,64,128]{2,1,0:T(8,128)S(1)} %collective-permute-d, ...), custom_call_target="tpu_custom_call" | custom-call | tf_op jit(solution)/shard_map/down/pallas_call | solution.py:23
  25.0 3.9 %collective-permute-start.6 = (f32[8,8,128]{2,1,0:T(8,128)S(1)}, f32[8,8,128]{2,1,0:T(8,128)S(1)}, u32[]{:S(2)}, u32[]{:S(2)}) collective-permute-start(f32[8,8,128]{2,1,0:T(8,128)S(1)} %get-tuple-element.75), channel_id=1, source_target_pairs={{0,1},{1,0},{2,3},{3,2},{4,5},{5,4},{6,7},{7,6},{8,9},{9,8},{10,11... | collective-permute-start | bytes 98312 | tf_op jit(solution)/shard_map/ppermute | solution.py:625
  28.9 0.7 collective-permute-start.7
  29.5 0.6 collective-permute-done.6.y0
  30.2 0.0 collective-permute-done.7.y1
  30.2 0.1 edges2.1
  30.3 0.1 collective-permute-start.8
  30.4 4.5 %collective-permute-start.9 = (f32[192,128]{1,0:T(8,128)S(1)}, f32[192,128]{1,0:T(8,128)S(1)}, u32[]{:S(2)}, u32[]{:S(2)}) collective-permute-start(f32[192,128]{1,0:T(8,128)S(1)} %get-tuple-element.78), channel_id=1, source_target_pairs={{4,8},{8,4},{12,16},{16,12},{20,24},{24,20},{28,32},{32,28},{36,40... | collective-permute-start | bytes 294920 | tf_op jit(solution)/shard_map/ppermute | solution.py:624
  35.0 0.0 collective-permute-done.8.x0
  35.0 2.3 %collective-permute-done.9.x1 = f32[192,128]{1,0:T(8,128)S(1)} collective-permute-done((f32[192,128]{1,0:T(8,128)S(1)}, f32[192,128]{1,0:T(8,128)S(1)}, u32[]{:S(2)}, u32[]{:S(2)}) %collective-permute-start.9) | collective-permute-done | bytes 98336 | tf_op jit(solution)/shard_map/ppermute | solution.py:624
  37.2 1.0 %level2.1 = (f32[16,48,128]{2,1,0:T(8,128)S(1)}, f32[16,48,128]{2,1,0:T(8,128)S(1)}, f32[16,48,128]{2,1,0:T(8,128)S(1)}, f32[16,48,128]{2,1,0:T(8,128)S(1)}, f32...) custom-call(f32[20,64,128]{2,1,0:T(8,128)S(1)} %get-tuple-element.72., ...), custom_call_target="tpu_custom_call" | custom-call | tf_op jit(solution)/shard_map/level2/pallas_call | solution.py:23
  38.3 27.2 %all_to_all.11 = f32[128,4,128]{2,1,0:T(4,128)S(1)} all-to-all(f32[128,4,128]{2,1,0:T(4,128)S(1)} %bitcast.3), channel_id=1, replica_groups=mesh['gx'=32,'gy'=4] {'gx','gy'}, dimensions={0} | all-to-all | bytes 524288 | tf_op jit(solution)/shard_map/all_to_all | solution.py:670
  65.4 8.4 %up.1 = (f32[16,64,128]{2,1,0:T(8,128)}, f32[16,64,128]{2,1,0:T(8,128)}) custom-call(f32[512,128]{1,0:T(8,128)S(1)} %bitcast.2, f32[8,8,128]{2,1,0:T(8,128)S(1)} %collective-permute-done.6.y0, f32[8,8,128]{2,1,0:T(8,128)S(1)} %collective-permute-done.7.y1, f32[16,48,128]{2,1,0:T(8,128)S(1)} %get-tuple-element.80.hx, ...), custom_call_target="tpu_custom_call" | custom-call | tf_op jit(solution)/shard_map/up/pallas_call | solution.py:23
  (1 shorter events, 0.0 us)
Async XLA Ops:
  2.5 16.8 %collective-permute-start = (f32[21,64,128]{2,1,0:T(8,128)S(1)}, f32[21,64,128]{2,1,0:T(8,128)S(1)}, u32[]{:S(2)}, u32[]{:S(2)}) collective-permute-start(f32[21,64,128]{2,1,0:T(8,128)S(1)} %get-tuple-element.50), channel_id=1, source_target_pairs={{0,4},{4,0},{8,12},{12,8},{16,20},{20,16},{24,28},{28,24},{32,36},... | collective-permute-start | bytes 2064392 | tf_op jit(solution)/shard_map/ppermute | solution.py:625
  4.0 15.3 %collective-permute-start.1 = (f32[21,64,128]{2,1,0:T(8,128)S(1)}, f32[21,64,128]{2,1,0:T(8,128)S(1)}, u32[]{:S(2)}, u32[]{:S(2)}) collective-permute-start(f32[21,64,128]{2,1,0:T(8,128)S(1)} %get-tuple-element.51), channel_id=1, source_target_pairs={{4,8},{8,4},{12,16},{16,12},{20,24},{24,20},{28,32},{32,28},{36,40... | collective-permute-start | bytes 2064392 | tf_op jit(solution)/shard_map/ppermute | solution.py:624
  7.2 3.9 %collective-permute-start.2 = (f32[32,8,128]{2,1,0:T(8,128)S(1)}, f32[32,8,128]{2,1,0:T(8,128)S(1)}, u32[]{:S(2)}, u32[]{:S(2)}) collective-permute-start(f32[32,8,128]{2,1,0:T(8,128)S(1)} %get-tuple-element.52), channel_id=1, source_target_pairs={{0,1},{1,0},{2,3},{3,2},{4,5},{5,4},{6,7},{7,6},{8,9},{9,8},{10,11... | collective-permute-start | bytes 393224 | tf_op jit(solution)/shard_map/ppermute | solution.py:625
  8.5 2.6 %collective-permute-start.3 = (f32[32,8,128]{2,1,0:T(8,128)S(1)}, f32[32,8,128]{2,1,0:T(8,128)S(1)}, u32[]{:S(2)}, u32[]{:S(2)}) collective-permute-start(f32[32,8,128]{2,1,0:T(8,128)S(1)} %get-tuple-element.53), channel_id=1, source_target_pairs={{1,2},{2,1},{5,6},{6,5},{9,10},{10,9},{13,14},{14,13},{17,18},{18,... | collective-permute-start | bytes 393224 | tf_op jit(solution)/shard_map/ppermute | solution.py:624
  11.1 7.2 %collective-permute-start.4 = (f32[21,16,128]{2,1,0:T(8,128)S(1)}, f32[21,16,128]{2,1,0:T(8,128)S(1)}, u32[]{:S(2)}, u32[]{:S(2)}) collective-permute-start(f32[21,16,128]{2,1,0:T(8,128)S(1)} %get-tuple-element.54), channel_id=1, source_target_pairs={{0,4},{4,0},{8,12},{12,8},{16,20},{20,16},{24,28},{28,24},{32,36},... | collective-permute-start | bytes 516104 | tf_op jit(solution)/shard_map/ppermute | solution.py:625
  11.2 8.1 %collective-permute-start.5 = (f32[21,16,128]{2,1,0:T(8,128)S(1)}, f32[21,16,128]{2,1,0:T(8,128)S(1)}, u32[]{:S(2)}, u32[]{:S(2)}) collective-permute-start(f32[21,16,128]{2,1,0:T(8,128)S(1)} %get-tuple-element.55), channel_id=1, source_target_pairs={{4,8},{8,4},{12,16},{16,12},{20,24},{24,20},{28,32},{32,28},{36,40... | collective-permute-start | bytes 516104 | tf_op jit(solution)/shard_map/ppermute | solution.py:624
  25.0 5.2 %collective-permute-start.6 = (f32[8,8,128]{2,1,0:T(8,128)S(1)}, f32[8,8,128]{2,1,0:T(8,128)S(1)}, u32[]{:S(2)}, u32[]{:S(2)}) collective-permute-start(f32[8,8,128]{2,1,0:T(8,128)S(1)} %get-tuple-element.75), channel_id=1, source_target_pairs={{0,1},{1,0},{2,3},{3,2},{4,5},{5,4},{6,7},{7,6},{8,9},{9,8},{10,11... | collective-permute-start | bytes 98312 | tf_op jit(solution)/shard_map/ppermute | solution.py:625
  28.9 1.3 %collective-permute-start.7 = (f32[8,8,128]{2,1,0:T(8,128)S(1)}, f32[8,8,128]{2,1,0:T(8,128)S(1)}, u32[]{:S(2)}, u32[]{:S(2)}) collective-permute-start(f32[8,8,128]{2,1,0:T(8,128)S(1)} %get-tuple-element.76), channel_id=1, source_target_pairs={{1,2},{2,1},{5,6},{6,5},{9,10},{10,9},{13,14},{14,13},{17,18},{18,... | collective-permute-start | bytes 98312 | tf_op jit(solution)/shard_map/ppermute | solution.py:624
  30.3 4.6 %collective-permute-start.8 = (f32[192,128]{1,0:T(8,128)S(1)}, f32[192,128]{1,0:T(8,128)S(1)}, u32[]{:S(2)}, u32[]{:S(2)}) collective-permute-start(f32[192,128]{1,0:T(8,128)S(1)} %get-tuple-element.77), channel_id=1, source_target_pairs={{0,4},{4,0},{8,12},{12,8},{16,20},{20,16},{24,28},{28,24},{32,36},... | collective-permute-start | bytes 294920 | tf_op jit(solution)/shard_map/ppermute | solution.py:625
  30.4 6.8 %collective-permute-start.9 = (f32[192,128]{1,0:T(8,128)S(1)}, f32[192,128]{1,0:T(8,128)S(1)}, u32[]{:S(2)}, u32[]{:S(2)}) collective-permute-start(f32[192,128]{1,0:T(8,128)S(1)} %get-tuple-element.78), channel_id=1, source_target_pairs={{4,8},{8,4},{12,16},{16,12},{20,24},{24,20},{28,32},{32,28},{36,40... | collective-permute-start | bytes 294920 | tf_op jit(solution)/shard_map/ppermute | solution.py:624

commit v4 on v3

--- a/solution.py
+++ b/solution.py
@@ -193,7 +193,7 @@
 PARTS = 4
 
 
-def begin_kernel(source, density, drag, porous, cond, rhs, ypack0, ypack1, xpack0, xpack1, dens, dra, por, sem, esem):
+def begin_kernel(source, density, drag, porous, cond, rhs, ypack0, ypack1, dens, dra, por, sem, esem):
     o = odd("gy")
     at0 = pl.multiple_of((1 - o) * (NY - 8), 8)
     at1 = pl.multiple_of(o * (NY - 8), 8)
@@ -212,11 +212,6 @@
         edges[-1].start()
     edges.append(pltpu.make_async_copy(source, rhs, esem.at[2]))
     edges[-1].start()
-    ox = odd("gx")
-    for j, (last, pack) in enumerate(((1 - ox, xpack0), (ox, xpack1))):
-        rhs_rows = source.at[pl.ds(last * (NX - 10), 10)]
-        edges.append(pltpu.make_async_copy(rhs_rows, pack.at[pl.ds(11, 10)], esem.at[4 + j]))
-        edges[-1].start()
     first.wait()
     shape = (NY, NZ)
     line = jnp.broadcast_to(por[...].astype(F32)[None], (NY, NY))
@@ -229,22 +224,50 @@
             cond[x] = recip(dens[x] * (1.0 + dra[x] * mask))
             ypack0[x] = cond[x, pl.ds(at0, 8), :]
             ypack1[x] = cond[x, pl.ds(at1, 8), :]
+    for edge in edges:
+        edge.wait()
+
+
+def edge_kernel(cond, source, xpack0, xpack1):
+    ox = odd("gx")
     for last, pack in ((1 - ox, xpack0), (ox, xpack1)):
         for k in range(11):
             pack[k] = cond[k + last * (NX - 11)]
-    for edge in edges:
-        edge.wait()
+        for k in range(10):
+            pack[11 + k] = source[k + last * (NX - 10)]
+
+
+CORNERS = (
+    [(0, d, d - 1, 0) for d in (1, 2, 3, 4, 5, 6, 7)]
+    + [(0, 9, 4, 2), (0, 8, 5, 3), (0, 10, 6, 1)]
+    + [(1, d, d + 6, 0) for d in (1, 2, 3, 4, 5, 6)]
+    + [(1, 7, 11, 3), (1, 8, 12, 2), (1, 9, 10, 1)]
+)
+TILES = 13
+
+
+def turn(v, by):
+    return v if by == 0 else pltpu.roll(v, by % 8, 0)
 
 
 def corner_kernel(y0, y1, xpack0, xpack1):
     ox, oy = odd("gx"), odd("gy")
     at0 = pl.multiple_of((1 - oy) * 8, 8)
     at1 = pl.multiple_of(oy * 8, 8)
+    row = lax.broadcasted_iota(jnp.int32, (8, NZ), 0)
     for pack, last in ((xpack0, 1 - ox), (xpack1, ox)):
-        for k in range(21):
-            x = k + last * (NX - 11) if k < 11 else NX + k - 11 + last * (NX - 10)
-            pack[k, pl.ds(at0, 8), :] = y0[x]
-            pack[k, pl.ds(at1, 8), :] = y1[x]
+        for y, at, high in ((y0, at0, 1 - oy), (y1, at1, oy)):
+            tiles = {}
+            for field, d, t, by in CORNERS:
+                v = y[field * NX + d - 1 + last * (NX + 1 - 2 * d)]
+                if by == 0:
+                    tiles[t] = v
+                else:
+                    low = jnp.where(row < by, turn(v, by), tiles[t])
+                    top = jnp.where(row >= 8 - by, turn(v, -by), tiles[t])
+                    tiles[t] = jnp.where(high == 1, top, low)
+            for t in range(TILES):
+                pack[t, pl.ds(at, 8), :] = tiles[t]
 
 
 X0, Y0 = 12, 16
@@ -289,16 +312,16 @@
     ox, oy = odd("gx"), odd("gy")
     here, here1 = pl.ds(8, 80), pl.ds(8, 48)
 
-    def halo(ref, row, x, k, pack):
-        ref[row, pl.ds(Y0, NY), :] = x[k]
-        ref[row, pl.ds(8, 8), :] = pack[k, pl.ds(0, 8), :]
-        ref[row, pl.ds(88 - 8, 8), :] = pack[k, pl.ds(8, 8), :]
-
     for x, pack, up in ((x0, k0, 1 - ox), (x1, k1, ox)):
         for k in range(11):
-            halo(c, k + 1 + up * (11 + NX), x, k, pack)
+            c[k + 1 + up * (11 + NX), pl.ds(Y0, NY), :] = x[k]
         for k in range(10):
-            halo(b, k + 2 + up * (10 + NX), x, 11 + k, pack)
+            b[k + 2 + up * (10 + NX), pl.ds(Y0, NY), :] = x[11 + k]
+        for field, d, t, by in CORNERS:
+            ref = (c, b)[field]
+            at = X0 - d + up * (NX - 1 + 2 * d)
+            ref[at, pl.ds(8, 8), :] = turn(pack[t, pl.ds(0, 8), :], -by)
+            ref[at, pl.ds(80, 8), :] = turn(pack[t, pl.ds(8, 8), :], by)
     for x in (1, 16):
         c[x + 11, here, :] = c_in[x, here, :]
     for x in (2, 3, 14, 15):
@@ -626,25 +649,26 @@
 
 
 def per_device(source, density, drag, porous_rows):
-    sems = [pltpu.SemaphoreType.DMA((2, PARTS)), pltpu.SemaphoreType.DMA((6,))]
+    sems = [pltpu.SemaphoreType.DMA((2, PARTS)), pltpu.SemaphoreType.DMA((4,))]
     block = (NX, NY, NZ)
-    cond, source, p0, p1, q0, q1 = call(
+    cond, source, p0, p1 = call(
         begin_kernel,
-        [block, block, (32, 8, NZ), (32, 8, NZ)] + [(21, NY, NZ)] * 2,
+        [block, block, (32, 8, NZ), (32, 8, NZ)],
         [block, block, pltpu.VMEM((NY,), jnp.int32)] + sems,
         (source, density, drag, porous_rows),
         "begin",
         16,
         4,
     )
+    y0, y1 = swaps("gy", p0, p1)
+    q0, q1 = call(edge_kernel, [(21, NY, NZ)] * 2, [], (cond, source), "edges", 16, 0, 10**9)
     x0, x1 = swaps("gx", q0, q1)
-    y0, y1 = swaps("gy", p0, p1)
-    p0, p1 = call(corner_kernel, [(21, 16, NZ)] * 2, [], (y0, y1), "corners", 16)
+    p0, p1 = call(corner_kernel, [(TILES, 16, NZ)] * 2, [], (y0, y1), "corners", 16)
     k0, k1 = swaps("gx", p0, p1)
     zero, one, two = (40, 96, NZ), (20, 64, NZ), (16, 48, NZ)
     small, small1 = (18, 96, NZ), (10, 64, NZ)
     inner = call(
-        inner_kernel, [small] * 8 + [small1] * 6, [(8, 96, NZ)], (cond, source, y0, y1), "inner", 16, 0, 10**7
+        inner_kernel, [small] * 8 + [small1] * 6, [(8, 96, NZ)], (cond, source, y0, y1), "inner", 16, 0, 10**10
     )
     down = call(
         down_kernel,

time: 74.1 us -> 72.2 us (0.974)
  starting transfers between devices: 20.9 us -> 19.2 us
  blocking collectives: 27.2 us -> 25.6 us
  waiting for transfers between devices: 5.91 us -> 7.41 us
    ppermute x5, waiting for transfers between devices: 3.31 us -> 6.75 us  [swaps(): late = lax.ppermute(second, axis, pairs(1))]
    ppermute x5, waiting for transfers between devices: 2.6 us -> 0.66 us  [swaps(): return (lax.ppermute(first, axis, pairs(0)), late)]
    ppermute x5, starting transfers between devices: 14 us -> 12.1 us  [swaps(): late = lax.ppermute(second, axis, pairs(1))]
    all_to_all x1, blocking collectives: 27.2 us -> 25.6 us  [per_device(): whole = lax.all_to_all(packed, ('gx', 'gy'), 0, 0, tiled=True)]
    pallas_call x7 -> x8, Pallas kernels: 19.1 us -> 19 us  [call(): pl.pallas_call(body, out_shape=[jax.ShapeDtypeStruct(s, F32) for s in out...]
  transfers between devices with their start and end apart: 10 -> 10, of which waited for: 4 -> 3; matrix products, arithmetic and copies ran while one was open for 0% -> 0% of each run, Pallas kernels for 3% -> 3%
where the time goes in v4:
time: 72.2 us; the launch traced here: 72 us
  blocking collectives  25.6 us (35%)
  starting transfers between devices  19.2 us (27%)
  Pallas kernels  19 us (26%)
  waiting for transfers between devices  7.41 us (10%)
  between operations  0.78 us (1%)
    all_to_all x1, blocking collectives, per_device(): whole = lax.all_to_all(packed, ('gx', 'gy'), 0, 0, tiled=True)  25.6 us
    pallas_call x8, Pallas kernels, call(): pl.pallas_call(body, out_shape=[jax.ShapeDtypeStruct(s, F32) for s in out...  19 us
    ppermute x5, starting transfers between devices, swaps(): late = lax.ppermute(second, axis, pairs(1))  12.1 us
    ppermute x5, starting transfers between devices, swaps(): return (lax.ppermute(first, axis, pairs(0)), late)  7.05 us
    ppermute x5, waiting for transfers between devices, swaps(): late = lax.ppermute(second, axis, pairs(1))  6.75 us
  transfers between devices with their start and end apart: 10, of which 3 were waited for; matrix products, arithmetic and copies ran while one was open for 0% of the time, Pallas kernels for 3%

profile of v4, /device:TPU:1, one launch (start us, length us, event | category | flops | bytes accessed | tf_op | source)
XLA Modules:
  0.0 72.0 jit_solution(3097052770521039445)
XLA Ops:
  0.6 1.6 %begin.1 = (f32[16,64,128]{2,1,0:T(8,128)S(1)}, f32[16,64,128]{2,1,0:T(8,128)S(1)}, f32[32,8,128]{2,1,0:T(8,128)S(1)}, f32[32,8,128]{2,1,0:T(8,128)S(1)}) custom-call(f32[16,64,128]{2,1,0:T(8,128)} %source.1, f32[16,64,128]{2,1,0:T(8,128)} %density.1, f32[16,64,128]{2,1,0:T(8,128)} %drag.1, s32[64]{0:T(128)} %porous.1), custom_call_target="tpu_custom_call" | custom-call | tf_op jit(solution)/shard_map/begin/pallas_call | solution.py:23
  2.3 2.1 %collective-permute-start.2 = (f32[32,8,128]{2,1,0:T(8,128)S(1)}, f32[32,8,128]{2,1,0:T(8,128)S(1)}, u32[]{:S(2)}, u32[]{:S(2)}) collective-permute-start(f32[32,8,128]{2,1,0:T(8,128)S(1)} %get-tuple-element.54), channel_id=1, source_target_pairs={{0,1},{1,0},{2,3},{3,2},{4,5},{5,4},{6,7},{7,6},{8,9},{9,8},{10,11... | collective-permute-start | bytes 393224 | tf_op jit(solution)/shard_map/ppermute | solution.py:648
  4.4 0.7 collective-permute-start.3
  5.1 0.1 edges.1
  5.2 1.0 %collective-permute-start = (f32[21,64,128]{2,1,0:T(8,128)S(1)}, f32[21,64,128]{2,1,0:T(8,128)S(1)}, u32[]{:S(2)}, u32[]{:S(2)}) collective-permute-start(f32[21,64,128]{2,1,0:T(8,128)S(1)} %get-tuple-element.52), channel_id=1, source_target_pairs={{0,4},{4,0},{8,12},{12,8},{16,20},{20,16},{24,28},{28,24},{32,36},... | collective-permute-start | bytes 2064392 | tf_op jit(solution)/shard_map/ppermute | solution.py:648
  6.2 3.1 %collective-permute-start.1 = (f32[21,64,128]{2,1,0:T(8,128)S(1)}, f32[21,64,128]{2,1,0:T(8,128)S(1)}, u32[]{:S(2)}, u32[]{:S(2)}) collective-permute-start(f32[21,64,128]{2,1,0:T(8,128)S(1)} %get-tuple-element.53), channel_id=1, source_target_pairs={{4,8},{8,4},{12,16},{16,12},{20,24},{24,20},{28,32},{32,28},{36,40... | collective-permute-start | bytes 2064392 | tf_op jit(solution)/shard_map/ppermute | solution.py:647
  9.3 0.0 collective-permute-done.2.y0
  9.3 0.0 collective-permute-done.3.y1
  9.3 0.1 corners.1
  9.4 0.1 collective-permute-start.4
  9.5 3.6 %collective-permute-start.5 = (f32[13,16,128]{2,1,0:T(8,128)S(1)}, f32[13,16,128]{2,1,0:T(8,128)S(1)}, u32[]{:S(2)}, u32[]{:S(2)}) collective-permute-start(f32[13,16,128]{2,1,0:T(8,128)S(1)} %get-tuple-element.57), channel_id=1, source_target_pairs={{4,8},{8,4},{12,16},{16,12},{20,24},{24,20},{28,32},{32,28},{36,40... | collective-permute-start | bytes 319496 | tf_op jit(solution)/shard_map/ppermute | solution.py:647
  13.1 2.0 %inner.1 = (f32[18,96,128]{2,1,0:T(8,128)S(1)}, f32[18,96,128]{2,1,0:T(8,128)S(1)}, f32[18,96,128]{2,1,0:T(8,128)S(1)}, f32[18,96,128]{2,1,0:T(8,128)S(1)}, f32[...) custom-call(f32[16,64,128]{2,1,0:T(8,128)S(1)} %get-tuple-element.50, ...), custom_call_target="tpu_custom_call" | custom-call | flops 10000000000 | tf_op jit(solution)/shard_map/inner/pallas_call | solution.py:23
  15.1 0.0 collective-permute-done.4.k0
  15.1 4.5 %collective-permute-done.5.k1 = f32[13,16,128]{2,1,0:T(8,128)S(1)} collective-permute-done((f32[13,16,128]{2,1,0:T(8,128)S(1)}, f32[13,16,128]{2,1,0:T(8,128)S(1)}, u32[]{:S(2)}, u32[]{:S(2)}) %collective-permute-start.5) | collective-permute-done | bytes 106528 | tf_op jit(solution)/shard_map/ppermute | solution.py:647
  19.6 0.0 collective-permute-done.x0
  19.6 0.0 collective-permute-done.1.x1
  19.6 5.6 %down.1 = (f32[40,96,128]{2,1,0:T(8,128)S(1)}, f32[40,96,128]{2,1,0:T(8,128)S(1)}, f32[40,96,128]{2,1,0:T(8,128)S(1)}, f32[40,96,128]{2,1,0:T(8,128)S(1)}, f32[4...) custom-call(f32[21,64,128]{2,1,0:T(8,128)S(1)} %collective-permute-d, ...), custom_call_target="tpu_custom_call" | custom-call | tf_op jit(solution)/shard_map/down/pallas_call | solution.py:23
  25.2 3.7 %collective-permute-start.6 = (f32[8,8,128]{2,1,0:T(8,128)S(1)}, f32[8,8,128]{2,1,0:T(8,128)S(1)}, u32[]{:S(2)}, u32[]{:S(2)}) collective-permute-start(f32[8,8,128]{2,1,0:T(8,128)S(1)} %get-tuple-element.75), channel_id=1, source_target_pairs={{0,1},{1,0},{2,3},{3,2},{4,5},{5,4},{6,7},{7,6},{8,9},{9,8},{10,11... | collective-permute-start | bytes 98312 | tf_op jit(solution)/shard_map/ppermute | solution.py:648
  29.0 0.7 collective-permute-start.7
  29.6 0.6 collective-permute-done.6.y0
  30.3 0.0 collective-permute-done.7.y1
  30.3 0.1 edges2.1
  30.4 0.1 collective-permute-start.8
  30.5 4.1 %collective-permute-start.9 = (f32[192,128]{1,0:T(8,128)S(1)}, f32[192,128]{1,0:T(8,128)S(1)}, u32[]{:S(2)}, u32[]{:S(2)}) collective-permute-start(f32[192,128]{1,0:T(8,128)S(1)} %get-tuple-element.78), channel_id=1, source_target_pairs={{4,8},{8,4},{12,16},{16,12},{20,24},{24,20},{28,32},{32,28},{36,40... | collective-permute-start | bytes 294920 | tf_op jit(solution)/shard_map/ppermute | solution.py:647
  34.7 0.0 collective-permute-done.8.x0
  34.7 2.3 %collective-permute-done.9.x1 = f32[192,128]{1,0:T(8,128)S(1)} collective-permute-done((f32[192,128]{1,0:T(8,128)S(1)}, f32[192,128]{1,0:T(8,128)S(1)}, u32[]{:S(2)}, u32[]{:S(2)}) %collective-permute-start.9) | collective-permute-done | bytes 98336 | tf_op jit(solution)/shard_map/ppermute | solution.py:647
  37.0 1.0 %level2.1 = (f32[16,48,128]{2,1,0:T(8,128)S(1)}, f32[16,48,128]{2,1,0:T(8,128)S(1)}, f32[16,48,128]{2,1,0:T(8,128)S(1)}, f32[16,48,128]{2,1,0:T(8,128)S(1)}, f32...) custom-call(f32[20,64,128]{2,1,0:T(8,128)S(1)} %get-tuple-element.72., ...), custom_call_target="tpu_custom_call" | custom-call | tf_op jit(solution)/shard_map/level2/pallas_call | solution.py:23
  38.0 25.6 %all_to_all.11 = f32[128,4,128]{2,1,0:T(4,128)S(1)} all-to-all(f32[128,4,128]{2,1,0:T(4,128)S(1)} %bitcast.3), channel_id=1, replica_groups=mesh['gx'=32,'gy'=4] {'gx','gy'}, dimensions={0} | all-to-all | bytes 524288 | tf_op jit(solution)/shard_map/all_to_all | solution.py:694
  63.6 8.4 %up.1 = (f32[16,64,128]{2,1,0:T(8,128)}, f32[16,64,128]{2,1,0:T(8,128)}) custom-call(f32[512,128]{1,0:T(8,128)S(1)} %bitcast.2, f32[8,8,128]{2,1,0:T(8,128)S(1)} %collective-permute-done.6.y0, f32[8,8,128]{2,1,0:T(8,128)S(1)} %collective-permute-done.7.y1, f32[16,48,128]{2,1,0:T(8,128)S(1)} %get-tuple-element.80.hx, ...), custom_call_target="tpu_custom_call" | custom-call | tf_op jit(solution)/shard_map/up/pallas_call | solution.py:23
Async XLA Ops:
  2.3 7.0 %collective-permute-start.2 = (f32[32,8,128]{2,1,0:T(8,128)S(1)}, f32[32,8,128]{2,1,0:T(8,128)S(1)}, u32[]{:S(2)}, u32[]{:S(2)}) collective-permute-start(f32[32,8,128]{2,1,0:T(8,128)S(1)} %get-tuple-element.54), channel_id=1, source_target_pairs={{0,1},{1,0},{2,3},{3,2},{4,5},{5,4},{6,7},{7,6},{8,9},{9,8},{10,11... | collective-permute-start | bytes 393224 | tf_op jit(solution)/shard_map/ppermute | solution.py:648
  4.4 4.9 %collective-permute-start.3 = (f32[32,8,128]{2,1,0:T(8,128)S(1)}, f32[32,8,128]{2,1,0:T(8,128)S(1)}, u32[]{:S(2)}, u32[]{:S(2)}) collective-permute-start(f32[32,8,128]{2,1,0:T(8,128)S(1)} %get-tuple-element.55), channel_id=1, source_target_pairs={{1,2},{2,1},{5,6},{6,5},{9,10},{10,9},{13,14},{14,13},{17,18},{18,... | collective-permute-start | bytes 393224 | tf_op jit(solution)/shard_map/ppermute | solution.py:647
  5.2 14.4 %collective-permute-start = (f32[21,64,128]{2,1,0:T(8,128)S(1)}, f32[21,64,128]{2,1,0:T(8,128)S(1)}, u32[]{:S(2)}, u32[]{:S(2)}) collective-permute-start(f32[21,64,128]{2,1,0:T(8,128)S(1)} %get-tuple-element.52), channel_id=1, source_target_pairs={{0,4},{4,0},{8,12},{12,8},{16,20},{20,16},{24,28},{28,24},{32,36},... | collective-permute-start | bytes 2064392 | tf_op jit(solution)/shard_map/ppermute | solution.py:648
  6.2 13.4 %collective-permute-start.1 = (f32[21,64,128]{2,1,0:T(8,128)S(1)}, f32[21,64,128]{2,1,0:T(8,128)S(1)}, u32[]{:S(2)}, u32[]{:S(2)}) collective-permute-start(f32[21,64,128]{2,1,0:T(8,128)S(1)} %get-tuple-element.53), channel_id=1, source_target_pairs={{4,8},{8,4},{12,16},{16,12},{20,24},{24,20},{28,32},{32,28},{36,40... | collective-permute-start | bytes 2064392 | tf_op jit(solution)/shard_map/ppermute | solution.py:647
  9.4 5.7 %collective-permute-start.4 = (f32[13,16,128]{2,1,0:T(8,128)S(1)}, f32[13,16,128]{2,1,0:T(8,128)S(1)}, u32[]{:S(2)}, u32[]{:S(2)}) collective-permute-start(f32[13,16,128]{2,1,0:T(8,128)S(1)} %get-tuple-element.56), channel_id=1, source_target_pairs={{0,4},{4,0},{8,12},{12,8},{16,20},{20,16},{24,28},{28,24},{32,36},... | collective-permute-start | bytes 319496 | tf_op jit(solution)/shard_map/ppermute | solution.py:648
  9.5 10.1 %collective-permute-start.5 = (f32[13,16,128]{2,1,0:T(8,128)S(1)}, f32[13,16,128]{2,1,0:T(8,128)S(1)}, u32[]{:S(2)}, u32[]{:S(2)}) collective-permute-start(f32[13,16,128]{2,1,0:T(8,128)S(1)} %get-tuple-element.57), channel_id=1, source_target_pairs={{4,8},{8,4},{12,16},{16,12},{20,24},{24,20},{28,32},{32,28},{36,40... | collective-permute-start | bytes 319496 | tf_op jit(solution)/shard_map/ppermute | solution.py:647
  25.2 5.0 %collective-permute-start.6 = (f32[8,8,128]{2,1,0:T(8,128)S(1)}, f32[8,8,128]{2,1,0:T(8,128)S(1)}, u32[]{:S(2)}, u32[]{:S(2)}) collective-permute-start(f32[8,8,128]{2,1,0:T(8,128)S(1)} %get-tuple-element.75), channel_id=1, source_target_pairs={{0,1},{1,0},{2,3},{3,2},{4,5},{5,4},{6,7},{7,6},{8,9},{9,8},{10,11... | collective-permute-start | bytes 98312 | tf_op jit(solution)/shard_map/ppermute | solution.py:648
  29.0 1.3 %collective-permute-start.7 = (f32[8,8,128]{2,1,0:T(8,128)S(1)}, f32[8,8,128]{2,1,0:T(8,128)S(1)}, u32[]{:S(2)}, u32[]{:S(2)}) collective-permute-start(f32[8,8,128]{2,1,0:T(8,128)S(1)} %get-tuple-element.76), channel_id=1, source_target_pairs={{1,2},{2,1},{5,6},{6,5},{9,10},{10,9},{13,14},{14,13},{17,18},{18,... | collective-permute-start | bytes 98312 | tf_op jit(solution)/shard_map/ppermute | solution.py:647
  30.4 4.2 %collective-permute-start.8 = (f32[192,128]{1,0:T(8,128)S(1)}, f32[192,128]{1,0:T(8,128)S(1)}, u32[]{:S(2)}, u32[]{:S(2)}) collective-permute-start(f32[192,128]{1,0:T(8,128)S(1)} %get-tuple-element.77), channel_id=1, source_target_pairs={{0,4},{4,0},{8,12},{12,8},{16,20},{20,16},{24,28},{28,24},{32,36},... | collective-permute-start | bytes 294920 | tf_op jit(solution)/shard_map/ppermute | solution.py:648
  30.5 6.4 %collective-permute-start.9 = (f32[192,128]{1,0:T(8,128)S(1)}, f32[192,128]{1,0:T(8,128)S(1)}, u32[]{:S(2)}, u32[]{:S(2)}) collective-permute-start(f32[192,128]{1,0:T(8,128)S(1)} %get-tuple-element.78), channel_id=1, source_target_pairs={{4,8},{8,4},{12,16},{16,12},{20,24},{24,20},{28,32},{32,28},{36,40... | collective-permute-start | bytes 294920 | tf_op jit(solution)/shard_map/ppermute | solution.py:647

commit v5 on v4

--- a/solution.py
+++ b/solution.py
@@ -193,85 +193,91 @@
 PARTS = 4
 
 
-def begin_kernel(source, density, drag, porous, cond, rhs, ypack0, ypack1, dens, dra, por, sem, esem):
+def stored(x):
+    o = odd("gx")
+    return o * (NX - 1) + (1 - 2 * o) * x
+
+
+def begin_kernel(source, density, drag, porous, cond, rhs, ypack0, ypack1, dens, dra, src, por, sem, psem):
     o = odd("gy")
     at0 = pl.multiple_of((1 - o) * (NY - 8), 8)
     at1 = pl.multiple_of(o * (NY - 8), 8)
     part = NX // PARTS
     loads = []
-    first = pltpu.make_async_copy(porous, por, esem.at[3])
+    first = pltpu.make_async_copy(porous, por, psem)
     first.start()
     for k in range(PARTS):
         here = pl.ds(k * part, part)
-        for j, (src, dst) in enumerate(((density, dens), (drag, dra))):
-            loads.append(pltpu.make_async_copy(src.at[here], dst.at[here], sem.at[j, k]))
+        for j, (ref, dst) in enumerate(((density, dens), (drag, dra), (source, src))):
+            loads.append(pltpu.make_async_copy(ref.at[here], dst.at[here], sem.at[j, k]))
             loads[-1].start()
-    edges = []
-    for j, (at, pack) in enumerate(((at0, ypack0), (at1, ypack1))):
-        edges.append(pltpu.make_async_copy(source.at[:, pl.ds(at, 8), :], pack.at[pl.ds(NX, NX)], esem.at[j]))
-        edges[-1].start()
-    edges.append(pltpu.make_async_copy(source, rhs, esem.at[2]))
-    edges[-1].start()
     first.wait()
-    shape = (NY, NZ)
     line = jnp.broadcast_to(por[...].astype(F32)[None], (NY, NY))
     same = lax.broadcasted_iota(jnp.int32, (NY, NY), 0) == lax.broadcasted_iota(jnp.int32, (NY, NY), 1)
-    mask = jnp.broadcast_to(jnp.sum(jnp.where(same, line, 0.0), axis=1, keepdims=True), shape)
+    mask = jnp.broadcast_to(jnp.sum(jnp.where(same, line, 0.0), axis=1, keepdims=True), (NY, NZ))
     for k in range(PARTS):
-        loads[2 * k].wait()
-        loads[2 * k + 1].wait()
+        for load in loads[3 * k : 3 * k + 3]:
+            load.wait()
         for x in range(k * part, k * part + part):
-            cond[x] = recip(dens[x] * (1.0 + dra[x] * mask))
-            ypack0[x] = cond[x, pl.ds(at0, 8), :]
-            ypack1[x] = cond[x, pl.ds(at1, 8), :]
-    for edge in edges:
-        edge.wait()
-
-
-def edge_kernel(cond, source, xpack0, xpack1):
-    ox = odd("gx")
-    for last, pack in ((1 - ox, xpack0), (ox, xpack1)):
-        for k in range(11):
-            pack[k] = cond[k + last * (NX - 11)]
-        for k in range(10):
-            pack[11 + k] = source[k + last * (NX - 10)]
-
-
-CORNERS = (
+            to = stored(x)
+            cond[to] = recip(dens[x] * (1.0 + dra[x] * mask))
+            rhs[to] = src[x]
+            for pack, at in ((ypack0, at0), (ypack1, at1)):
+                pack[to] = cond[to, pl.ds(at, 8), :]
+                pack[NX + to] = src[x, pl.ds(at, 8), :]
+
+
+HIGH_C, HIGH_B, LOW_C, LOW_B = 11, 10, 8, 6
+
+
+def edge_kernel(cond, source, high, low):
+    for d in range(HIGH_C):
+        high[d] = cond[NX - 1 - d]
+    for d in range(HIGH_B):
+        high[HIGH_C + d] = source[NX - 1 - d]
+    for d in range(LOW_C):
+        low[d] = cond[d]
+    for d in range(LOW_B):
+        low[LOW_C + d] = source[d]
+
+
+HIGH = (
     [(0, d, d - 1, 0) for d in (1, 2, 3, 4, 5, 6, 7)]
     + [(0, 9, 4, 2), (0, 8, 5, 3), (0, 10, 6, 1)]
     + [(1, d, d + 6, 0) for d in (1, 2, 3, 4, 5, 6)]
     + [(1, 7, 11, 3), (1, 8, 12, 2), (1, 9, 10, 1)]
 )
-TILES = 13
+LOW = [(0, 1, 0, 0), (0, 7, 0, 1), (0, 2, 1, 0), (0, 6, 1, 2), (0, 3, 2, 0), (0, 5, 2, 3), (0, 4, 3, 0)]
+LOW += [(1, 5, 3, 1), (1, 1, 4, 0), (1, 3, 4, 3), (1, 2, 5, 0), (1, 4, 5, 2)]
+HIGH_TILES, LOW_TILES = 13, 6
 
 
 def turn(v, by):
     return v if by == 0 else pltpu.roll(v, by % 8, 0)
 
 
-def corner_kernel(y0, y1, xpack0, xpack1):
-    ox, oy = odd("gx"), odd("gy")
+def corner_kernel(y0, y1, high, low):
+    oy = odd("gy")
     at0 = pl.multiple_of((1 - oy) * 8, 8)
     at1 = pl.multiple_of(oy * 8, 8)
     row = lax.broadcasted_iota(jnp.int32, (8, NZ), 0)
-    for pack, last in ((xpack0, 1 - ox), (xpack1, ox)):
-        for y, at, high in ((y0, at0, 1 - oy), (y1, at1, oy)):
+    for pack, corners, count, side in ((high, HIGH, HIGH_TILES, 1), (low, LOW, LOW_TILES, 0)):
+        for y, at, above in ((y0, at0, 1 - oy), (y1, at1, oy)):
             tiles = {}
-            for field, d, t, by in CORNERS:
-                v = y[field * NX + d - 1 + last * (NX + 1 - 2 * d)]
+            for field, d, t, by in corners:
+                v = y[field * NX + (NX - d if side else d - 1)]
                 if by == 0:
                     tiles[t] = v
                 else:
-                    low = jnp.where(row < by, turn(v, by), tiles[t])
-                    top = jnp.where(row >= 8 - by, turn(v, -by), tiles[t])
-                    tiles[t] = jnp.where(high == 1, top, low)
-            for t in range(TILES):
+                    under = jnp.where(row < by, turn(v, by), tiles[t])
+                    over = jnp.where(row >= 8 - by, turn(v, -by), tiles[t])
+                    tiles[t] = jnp.where(above == 1, over, under)
+            for t in range(count):
                 pack[t, pl.ds(at, 8), :] = tiles[t]
 
 
-X0, Y0 = 12, 16
-X1, Y1 = 6, 16
+X0, Y0 = 9, 16
+X1, Y1 = 5, 16
 X2, Y2 = 6, 16
 
 
@@ -309,54 +315,53 @@
     fx, fy, fz, w, b, ub, gx_, gy_, gz_, gw_, b1, u1, c2, b2, ypack0, ypack1,
     c, ua, c1, ga_, tmp, ctmp, tmp1,
 ):
-    ox, oy = odd("gx"), odd("gy")
+    oy = odd("gy")
     here, here1 = pl.ds(8, 80), pl.ds(8, 48)
-
-    for x, pack, up in ((x0, k0, 1 - ox), (x1, k1, ox)):
-        for k in range(11):
-            c[k + 1 + up * (11 + NX), pl.ds(Y0, NY), :] = x[k]
-        for k in range(10):
-            b[k + 2 + up * (10 + NX), pl.ds(Y0, NY), :] = x[11 + k]
-        for field, d, t, by in CORNERS:
+    sides = ((x0, k0, HIGH, HIGH_C, HIGH_B, X0 + NX - 1, 1), (x1, k1, LOW, LOW_C, LOW_B, X0, -1))
+    for x, pack, corners, nc, nb, edge, sign in sides:
+        for d in range(1, nc + 1):
+            c[edge + sign * d, pl.ds(Y0, NY), :] = x[d - 1]
+        for d in range(1, nb + 1):
+            b[edge + sign * d, pl.ds(Y0, NY), :] = x[nc + d - 1]
+        for field, d, t, by in corners:
             ref = (c, b)[field]
-            at = X0 - d + up * (NX - 1 + 2 * d)
-            ref[at, pl.ds(8, 8), :] = turn(pack[t, pl.ds(0, 8), :], -by)
-            ref[at, pl.ds(80, 8), :] = turn(pack[t, pl.ds(8, 8), :], by)
+            ref[edge + sign * d, pl.ds(8, 8), :] = turn(pack[t, pl.ds(0, 8), :], -by)
+            ref[edge + sign * d, pl.ds(80, 8), :] = turn(pack[t, pl.ds(8, 8), :], by)
     for x in (1, 16):
-        c[x + 11, here, :] = c_in[x, here, :]
+        c[x + 8, here, :] = c_in[x, here, :]
     for x in (2, 3, 14, 15):
-        ua[x + 11, here, :] = ua_in[x, here, :]
+        ua[x + 8, here, :] = ua_in[x, here, :]
 
     def fill(x):
         for ref, src in ((fx, fx_in), (fy, fy_in), (fz, fz_in), (w, w_in), (b, b_in), (ub, ub_in)):
-            ref[x + 11, here, :] = src[x, here, :]
+            ref[x + 8, here, :] = src[x, here, :]
 
     rows(1, 17, fill)
     for x in range(1, 9):
-        c1[x + 5, here1, :] = c1_in[x, here1, :]
+        c1[x + 4, here1, :] = c1_in[x, here1, :]
         for ref, src in ((gx_, gx_in), (gy_, gy_in), (gz_, gz_in), (gw_, gw_in), (b1, b1_in)):
-            ref[x + 5, here1, :] = src[x, here1, :]
+            ref[x + 4, here1, :] = src[x, here1, :]
 
     top, mid = levels_down(c, b, fx, fy, fz, w, c1, b1, gx_, gy_, gz_, gw_)
-    top.faces(1, 12)
-    top.faces(27, 39)
-    top.weights(2, 13, ua)
-    top.weights(27, 38, ua)
-    top.sweep(ua, ub, 3, 14)
-    top.sweep(ua, ub, 26, 37)
-    top.restrict_c(ctmp, c1, 0, 5, 2, 1)
-    top.restrict_c(ctmp, c1, 13, 18, 2, 1)
-    top.restrict(ub, tmp, b1, 0, 6, 4, 2)
-    top.restrict(ub, tmp, b1, 10, 16, 4, 2)
-
-    mid.faces(1, 6)
-    mid.faces(13, 19)
-    mid.weights(2, 7)
-    mid.weights(13, 18)
-    mid.start(ga_, 2, 18)
-    mid.sweep(ga_, u1, 3, 17)
-    mid.restrict(u1, tmp1, b2, 0, 6, 4, 5)
-    mid.restrict_c(tmp1, c2, 0, 8, 2, 4)
+    top.faces(2, 9)
+    top.faces(24, 35)
+    top.weights(3, 10, ua)
+    top.weights(24, 35, ua)
+    top.sweep(ua, ub, 4, 11)
+    top.sweep(ua, ub, 23, 34)
+    top.restrict_c(ctmp, c1, 0, 4, 1, 1)
+    top.restrict_c(ctmp, c1, 12, 17, 1, 1)
+    top.restrict(ub, tmp, b1, 0, 4, 5, 3)
+    top.restrict(ub, tmp, b1, 8, 14, 5, 3)
+
+    mid.faces(1, 5)
+    mid.faces(12, 17)
+    mid.weights(2, 6)
+    mid.weights(12, 17)
+    mid.start(ga_, 3, 17)
+    mid.sweep(ga_, u1, 4, 16)
+    mid.restrict(u1, tmp1, b2, 0, 5, 5, X2)
+    mid.restrict_c(tmp1, c2, 0, 8, 1, X2 - 2)
 
     e0 = Y1 + (1 - oy) * 28
     e1 = Y1 + oy * 28
@@ -368,7 +373,7 @@
             pack[k, pl.ds(0, 4), :] = pack_lanes([u1[x + j, pl.ds(e, 4), :] for j in range(2)])
             pack[k, pl.ds(4, 4), :] = pack_lanes([b1[x + j, pl.ds(e, 4), :] for j in range(2)])
         for k in range(2):
-            pack[4 + k] = pack_lanes([b2[X2 - 1 + 4 * k + j, pl.ds(f, 8), :] for j in range(4)])
+            pack[4 + k] = pack_lanes([b2[X2 + min(4 * k + j, 4), pl.ds(f, 8), :] for j in range(4)])
             pack[6 + k] = pack_lanes([c2[X2 - 2 + 4 * k + j, pl.ds(f, 8), :] for j in range(4)])
 
 
@@ -387,8 +392,8 @@
     for y, a in ((y0, a0), (y1, a1)):
         for k in range(2):
             for j, v in enumerate(unpack_lanes(y[4 + k], 4)):
-                if 4 * k + j < 6:
-                    b2[X2 - 1 + 4 * k + j, pl.ds(a, 8), :] = v
+                if 4 * k + j < 5:
+                    b2[X2 + 4 * k + j, pl.ds(a, 8), :] = v
             for j, v in enumerate(unpack_lanes(y[6 + k], 4)):
                 c2[X2 - 2 + 4 * k + j, pl.ds(a, 8), :] = v
 
@@ -401,20 +406,27 @@
     rows(lo, hi, body)
 
 
-def edge2_kernel(u1_in, c2_in, b2_in, y0, y1, xpack0, xpack1, u1, c2, b2):
-    ox, oy = odd("gx"), odd("gy")
-    copy_rows([(u1_in, u1)], X1, X1 + 8)
-    copy_rows([(c2_in, c2), (b2_in, b2)], X2 - 2, X2 + 6)
+def edge2_kernel(u1_in, b1_in, c2_in, b2_in, y0, y1, high, low, u1, b1, c2, b2):
+    oy = odd("gy")
+    copy_rows([(u1_in, u1), (b1_in, b1)], X1, X1 + 8)
+    copy_rows([(c2_in, c2)], X2 - 2, X2 + 6)
+    copy_rows([(b2_in, b2)], X2, X2 + 5)
     set_y1(u1, y0, y1, oy, 0)
+    set_y1(b1, y0, y1, oy, 1)
     set_y2(c2, b2, y0, y1, oy)
-    for pack, last in ((xpack0, 1 - ox), (xpack1, ox)):
+    for pack, edge1, edge2, sign in ((high, X1 + 7, X2 + 3, -1), (low, X1, X2, 1)):
         for k in range(2):
-            x = X1 + 2 * k + last * 4
-            pack[pl.ds(k * 48, 48), :] = pack_lanes([u1[x + j, pl.ds(8, 48), :] for j in range(2)])
-        t = [c2[X2 + k - 2 * last, pl.ds(8, 32), :] for k in range(6)]
-        t += [b2[X2 + k - last, pl.ds(8, 32), :] for k in range(5)]
+            t = [u1[edge1 + sign * (2 * k + j), pl.ds(12, 40), :] for j in range(2)]
+            pack[pl.ds(k * 40, 40), :] = pack_lanes(t)
+        t = [c2[edge2 + sign * d, pl.ds(8, 32), :] for d in range(6)]
+        t += [b2[edge2 + sign * d, pl.ds(8, 32), :] for d in range(5 if sign == 1 else 4)]
+        t += t[:1] * (12 - len(t))
         for k in range(3):
-            pack[pl.ds(96 + k * 32, 32), :] = pack_lanes((t + t[:1])[4 * k : 4 * k + 4])
+            pack[pl.ds(80 + k * 32, 32), :] = pack_lanes(t[4 * k : 4 * k + 4])
+        t = [b1[edge1 + sign * j, pl.ds(12, 40), :] for j in range(2)]
+        pack[pl.ds(176, 40), :] = pack_lanes(t)
+        t = [b1[edge1 + sign * 2, pl.ds(16 + 16 * j, 16), :] for j in range(2)]
+        pack[pl.ds(216, 16), :] = pack_lanes(t)
 
 
 def one_hot(shape, f):
@@ -428,26 +440,28 @@
 
 
 def level2_kernel(
-    u1_in, c2_in, b2_in, y0, y1, x0, x1,
+    u1_in, c2_in, b2_in, y0, y1, x0, x1, far,
     fx, fy, fz, w, b2, u2, u1, gather,
     c2, ua, tmp, b3, c3,
 ):
     ox, oy = odd("gx"), odd("gy")
     copy_rows([(u1_in, u1)], X1, X1 + 8)
-    copy_rows([(c2_in, c2), (b2_in, b2)], X2 - 2, X2 + 6)
+    copy_rows([(c2_in, c2)], X2 - 2, X2 + 6)
+    copy_rows([(b2_in, b2)], X2, X2 + 5)
     set_y1(u1, y0, y1, oy, 0)
     set_y2(c2, b2, y0, y1, oy)
-    for pack, up in ((x0, 1 - ox), (x1, ox)):
+    for pack, edge1, edge2, sign in ((x0, X1 + 7, X2 + 3, 1), (x1, X1, X2, -1)):
         for k in range(2):
-            for j, v in enumerate(unpack_lanes(pack[pl.ds(k * 48, 48), :], 2)):
-                u1[X1 - 4 + 2 * k + j + up * 12, pl.ds(8, 48), :] = v
+            for j, v in enumerate(unpack_lanes(pack[pl.ds(k * 40, 40), :], 2)):
+                u1[edge1 + sign * (2 * k + j + 1), pl.ds(12, 40), :] = v
         t = []
         for k in range(3):
-            t += unpack_lanes(pack[pl.ds(96 + k * 32, 32), :], 4)
-        for k in range(6):
-            c2[X2 - 6 + k + up * 10, pl.ds(8, 32), :] = t[k]
-        for k in range(5):
-            b2[X2 - 5 + k + up * 9, pl.ds(8, 32), :] = t[6 + k]
+            t += unpack_lanes(pack[pl.ds(80 + k * 32, 32), :], 4)
+        for d in range(6):
+            c2[edge2 + sign * (d + 1), pl.ds(8, 32), :] = t[d]
+        for d in range(5 if sign == -1 else 4):
+            b2[edge2 + sign * (d + 1), pl.ds(8, 32), :] = t[6 + d]
+    b2[X2 + 8, pl.ds(8, 32), :] = unpack_lanes(far[pl.ds(112, 32), :], 4)[2]
 
     low = Level(2, c2, b2, fx, fy, fz, w, 8, 40)
     low.faces(0, 15)
@@ -464,6 +478,7 @@
     packed = [
         jnp.sum(jnp.where(mine, spread[8 * k : 8 * k + 8], 0.0), axis=0, keepdims=True) for k in range(4)
     ]
+    packed = [jnp.where(ox == 1, packed[k ^ 1], packed[k]) for k in range(4)]
     eight = jnp.concatenate(packed + packed, 0)
 
     def body(k):
@@ -553,7 +568,7 @@
 
 
 def up_kernel(
-    gather, y0, y1,
+    gather, y0, y1, x1,
     hx, hy, hz, hw, b2, u2,
     gx_, gy_, gz_, gw_, b1_in, u1,
     fx, fy, fz, w, b, u0,
@@ -561,7 +576,7 @@
     s3, e2, e1, e0, ha, hb, b1, ga_, gb_, ua, ub,
 ):
     ix, iy = lax.axis_index("gx"), lax.axis_index("gy")
-    oy = iy % 2
+    ox, oy = ix % 2, iy % 2
 
     def field(k):
         return jnp.stack(
@@ -583,7 +598,7 @@
     tiles = []
     for k in range(6):
         for g in range(3):
-            row = s3[iy + g, pl.ds(2 * ix + 6 + k, 1), :]
+            row = s3[iy + g, pl.ds(2 * ix + 6 + 5 * ox + (1 - 2 * ox) * k, 1), :]
             tiles.append(jnp.where(mine, jnp.broadcast_to(row, shape), 0.0))
     spread = exact_dot(jnp.concatenate(tiles, 0), one_hot((NZ, NZ), lambda i, j: i % 16 == j // 8))
     for k in range(6):
@@ -604,68 +619,75 @@
 
     rows(0, 8, grow1)
 
-    copy_rows([(b1_in, b1)], 2, 18)
+    copy_rows([(b1_in, b1)], 3, 17)
     set_y1(b1, y0, y1, oy, 1)
+    for j, v in enumerate(unpack_lanes(x1[pl.ds(176, 40), :], 2)):
+        b1[X1 - 1 - j, pl.ds(12, 40), :] = v
+    for j, v in enumerate(unpack_lanes(x1[pl.ds(216, 16), :], 2)):
+        b1[X1 - 3, pl.ds(16 + 16 * j, 16), :] = v
 
     def add1(k):
         for j in range(2):
-            ga_[2 + 2 * k + j] = u1[2 + 2 * k + j] + e1[k]
+            ga_[1 + 2 * k + j] = u1[1 + 2 * k + j] + e1[k]
 
     rows(0, 8, add1)
     mid = Level(1, None, b1, gx_, gy_, gz_, gw_, 8, 56)
-    mid.sweep(ga_, gb_, 3, 17)
-    mid.sweep(gb_, ga_, 4, 16)
+    mid.sweep(ga_, gb_, 2, 16)
+    mid.sweep(gb_, ga_, 3, 15)
 
     def grow0(k):
-        t = ga_[4 + k, pl.ds(8, 48), :]
+        t = ga_[3 + k, pl.ds(8, 48), :]
         e0[k, pl.ds(0, 48, stride=2), :] = t
         e0[k, pl.ds(1, 48, stride=2), :] = t
 
     def add0(k):
         for j in range(2):
-            ua[8 + 2 * k + j] = u0[8 + 2 * k + j] + e0[k]
+            ua[5 + 2 * k + j] = u0[5 + 2 * k + j] + e0[k]
 
     rows(0, 12, grow0, 4)
     rows(0, 12, add0, 4)
     top = Level(0, None, b, fx, fy, fz, w, 8, 88)
-    top.sweep(ua, ub, 10, 30)
-    top.sweep(ub, ua, 11, 29)
+    top.sweep(ua, ub, 7, 27)
+    top.sweep(ub, ua, 8, 26)
 
     def finish(x):
-        out[x] = ua[X0 + x, pl.ds(Y0, NY), :]
-        res[x] = top.residual(ua, X0 + x, Y0, NY)
+        to = stored(x)
+        out[to] = ua[X0 + x, pl.ds(Y0, NY), :]
+        res[to] = top.residual(ua, X0 + x, Y0, NY)
 
     rows(0, NX, finish)
 
 
-def swaps(axis, first, second):
+def swaps(axis, first, second=None):
     count = lax.axis_size(axis)
 
     def pairs(start):
         return [p for i in range(start, count - 1, 2) for p in ((i, i + 1), (i + 1, i))]
 
+    if second is None:
+        return lax.ppermute(first, axis, pairs(0))
     late = lax.ppermute(second, axis, pairs(1))
     return lax.ppermute(first, axis, pairs(0)), late
 
 
 def per_device(source, density, drag, porous_rows):
-    sems = [pltpu.SemaphoreType.DMA((2, PARTS)), pltpu.SemaphoreType.DMA((4,))]
+    sems = [pltpu.SemaphoreType.DMA((3, PARTS)), pltpu.SemaphoreType.DMA]
     block = (NX, NY, NZ)
     cond, source, p0, p1 = call(
         begin_kernel,
         [block, block, (32, 8, NZ), (32, 8, NZ)],
-        [block, block, pltpu.VMEM((NY,), jnp.int32)] + sems,
+        [block] * 3 + [pltpu.VMEM((NY,), jnp.int32)] + sems,
         (source, density, drag, porous_rows),
         "begin",
         16,
         4,
     )
     y0, y1 = swaps("gy", p0, p1)
-    q0, q1 = call(edge_kernel, [(21, NY, NZ)] * 2, [], (cond, source), "edges", 16, 0, 10**9)
+    q0, q1 = call(edge_kernel, [(HIGH_C + HIGH_B, NY, NZ), (LOW_C + LOW_B, NY, NZ)], [], (cond, source), "edges", 16, 0, 10**9)
     x0, x1 = swaps("gx", q0, q1)
-    p0, p1 = call(corner_kernel, [(TILES, 16, NZ)] * 2, [], (y0, y1), "corners", 16)
+    p0, p1 = call(corner_kernel, [(HIGH_TILES, 16, NZ), (LOW_TILES, 16, NZ)], [], (y0, y1), "corners", 16)
     k0, k1 = swaps("gx", p0, p1)
-    zero, one, two = (40, 96, NZ), (20, 64, NZ), (16, 48, NZ)
+    zero, one, two = (36, 96, NZ), (18, 64, NZ), (16, 48, NZ)
     small, small1 = (18, 96, NZ), (10, 64, NZ)
     inner = call(
         inner_kernel, [small] * 8 + [small1] * 6, [(8, 96, NZ)], (cond, source, y0, y1), "inner", 16, 0, 10**10
@@ -673,7 +695,7 @@
     down = call(
         down_kernel,
         [zero] * 6 + [one] * 6 + [two] * 2 + [(8, 8, NZ)] * 2,
-        [zero] * 2 + [one] * 2 + [(16, 96, NZ), (18, 96, NZ), (8, 64, NZ)],
+        [zero] * 2 + [one] * 2 + [(14, 96, NZ), (17, 96, NZ), (8, 64, NZ)],
         (x0, x1, k0, k1, *inner),
         "down",
         24,
@@ -681,13 +703,14 @@
     level0, level1 = down[:6], down[6:12]
     u1, c2, b2, p0, p1 = down[11:]
     y0, y1 = swaps("gy", p0, p1)
-    p0, p1 = call(edge2_kernel, [(192, NZ)] * 2, [one, two, two], (u1, c2, b2, y0, y1), "edges2", 16)
+    p0, p1 = call(edge2_kernel, [(232, NZ)] * 2, [one, one, two, two], (u1, level1[4], c2, b2, y0, y1), "edges2", 16)
     x0, x1 = swaps("gx", p0, p1)
+    far = swaps("gx", x1)
     *level2, u1, packed = call(
         level2_kernel,
         [two] * 6 + [one, (512, NZ)],
         [two] * 2 + [(2, 48, NZ)] * 3,
-        (u1, c2, b2, y0, y1, x0, x1),
+        (u1, c2, b2, y0, y1, x0, x1, far),
         "level2",
         16,
     )
@@ -696,7 +719,7 @@
         up_kernel,
         [block] * 2,
         [(6, 80, NZ), (6, 48, NZ), (8, 64, NZ), (12, 96, NZ)] + [two] * 2 + [one] * 3 + [zero] * 2,
-        (whole, y0, y1, *level2, *level1[:5], u1, *level0),
+        (whole, y0, y1, x1, *level2, *level1[:5], u1, *level0),
         "up",
         24,
     )

time: 72.2 us -> 70.1 us (0.971)
  waiting for transfers between devices: 7.41 us -> 5.62 us
  blocking collectives: 25.6 us -> 24.6 us
  Pallas kernels: 19 us -> 19.9 us
    ppermute x5, waiting for transfers between devices: 6.75 us -> 3.05 us  [swaps(): late = lax.ppermute(second, axis, pairs(1))]
    ppermute x0 -> x1, waiting for transfers between devices: none -> 1.32 us  [swaps(): return lax.ppermute(first, axis, pairs(0))]
    all_to_all x1, blocking collectives: 25.6 us -> 24.6 us  [per_device(): whole = lax.all_to_all(packed, ('gx', 'gy'), 0, 0, tiled=True)]
    ppermute x5, starting transfers between devices: 7.05 us -> 6.1 us  [swaps(): return (lax.ppermute(first, axis, pairs(0)), late)]
    pallas_call x8, Pallas kernels: 19 us -> 19.9 us  [call(): pl.pallas_call(body, out_shape=[jax.ShapeDtypeStruct(s, F32) for s in out...]
    ppermute x5, starting transfers between devices: 12.1 us -> 12.8 us  [swaps(): late = lax.ppermute(second, axis, pairs(1))]
  transfers between devices with their start and end apart: 10 -> 11, of which waited for: 3 -> 4; matrix products, arithmetic and copies ran while one was open for 0% -> 0% of each run, Pallas kernels for 3% -> 3%
where the time goes in v5:
time: 70.1 us; the launch traced here: 69.8 us
  blocking collectives  24.6 us (35%)
  Pallas kernels  19.9 us (28%)
  starting transfers between devices  18.9 us (27%)
  waiting for transfers between devices  5.62 us (8%)
  between operations  0.77 us (1%)
    all_to_all x1, blocking collectives, per_device(): whole = lax.all_to_all(packed, ('gx', 'gy'), 0, 0, tiled=True)  24.6 us
    pallas_call x8, Pallas kernels, call(): pl.pallas_call(body, out_shape=[jax.ShapeDtypeStruct(s, F32) for s in out...  19.9 us
    ppermute x5, starting transfers between devices, swaps(): late = lax.ppermute(second, axis, pairs(1))  12.8 us
    ppermute x5, starting transfers between devices, swaps(): return (lax.ppermute(first, axis, pairs(0)), late)  6.1 us
    ppermute x5, waiting for transfers between devices, swaps(): late = lax.ppermute(second, axis, pairs(1))  3.05 us
  transfers between devices with their start and end apart: 11, of which 4 were waited for; matrix products, arithmetic and copies ran while one was open for 0% of the time, Pallas kernels for 3%

profile of v5, /device:TPU:1, one launch (start us, length us, event | category | flops | bytes accessed | tf_op | source)
XLA Modules:
  0.0 69.8 jit_solution(3856636574265116844)
XLA Ops:
  0.6 1.6 %begin.1 = (f32[16,64,128]{2,1,0:T(8,128)S(1)}, f32[16,64,128]{2,1,0:T(8,128)S(1)}, f32[32,8,128]{2,1,0:T(8,128)S(1)}, f32[32,8,128]{2,1,0:T(8,128)S(1)}) custom-call(f32[16,64,128]{2,1,0:T(8,128)} %source.1, f32[16,64,128]{2,1,0:T(8,128)} %density.1, f32[16,64,128]{2,1,0:T(8,128)} %drag.1, s32[64]{0:T(128)} %porous.1), custom_call_target="tpu_custom_call" | custom-call | tf_op jit(solution)/shard_map/begin/pallas_call | solution.py:23
  2.2 2.1 %collective-permute-start.2 = (f32[32,8,128]{2,1,0:T(8,128)S(1)}, f32[32,8,128]{2,1,0:T(8,128)S(1)}, u32[]{:S(2)}, u32[]{:S(2)}) collective-permute-start(f32[32,8,128]{2,1,0:T(8,128)S(1)} %get-tuple-element.54), channel_id=1, source_target_pairs={{0,1},{1,0},{2,3},{3,2},{4,5},{5,4},{6,7},{7,6},{8,9},{9,8},{10,11... | collective-permute-start | bytes 393224 | tf_op jit(solution)/shard_map/ppermute | solution.py:670
  4.4 0.7 collective-permute-start.3
  5.0 0.1 edges.1
  5.1 4.0 %collective-permute-start.1 = (f32[14,64,128]{2,1,0:T(8,128)S(1)}, f32[14,64,128]{2,1,0:T(8,128)S(1)}, u32[]{:S(2)}, u32[]{:S(2)}) collective-permute-start(f32[14,64,128]{2,1,0:T(8,128)S(1)} %get-tuple-element.53), channel_id=1, source_target_pairs={{4,8},{8,4},{12,16},{16,12},{20,24},{24,20},{28,32},{32,28},{36,40... | collective-permute-start | bytes 1376264 | tf_op jit(solution)/shard_map/ppermute | solution.py:669
  9.2 0.1 collective-permute-start
  9.3 0.0 collective-permute-done.2.y0
  9.3 0.0 collective-permute-done.3.y1
  9.3 3.6 %collective-permute-start.5 = (f32[6,16,128]{2,1,0:T(8,128)S(1)}, f32[6,16,128]{2,1,0:T(8,128)S(1)}, u32[]{:S(2)}, u32[]{:S(2)}) collective-permute-start(f32[6,16,128]{2,1,0:T(8,128)S(1)} %get-tuple-element.57), channel_id=1, source_target_pairs={{4,8},{8,4},{12,16},{16,12},{20,24},{24,20},{28,32},{32,28},{36,40... | collective-permute-start | bytes 147464 | tf_op jit(solution)/shard_map/ppermute | solution.py:669
  12.9 0.1 collective-permute-start.4
  13.0 2.2 %inner.1 = (f32[18,96,128]{2,1,0:T(8,128)S(1)}, f32[18,96,128]{2,1,0:T(8,128)S(1)}, f32[18,96,128]{2,1,0:T(8,128)S(1)}, f32[18,96,128]{2,1,0:T(8,128)S(1)}, f32[...) custom-call(f32[16,64,128]{2,1,0:T(8,128)S(1)} %get-tuple-element.50, ...), custom_call_target="tpu_custom_call" | custom-call | flops 10000000000 | tf_op jit(solution)/shard_map/inner/pallas_call | solution.py:23
  15.2 0.6 collective-permute-done.5.k1
  15.8 0.0 collective-permute-done.4.k0
  15.8 0.0 collective-permute-done.1.x1
  15.8 0.0 collective-permute-done.x0
  15.9 5.2 %down.1 = (f32[36,96,128]{2,1,0:T(8,128)S(1)}, f32[36,96,128]{2,1,0:T(8,128)S(1)}, f32[36,96,128]{2,1,0:T(8,128)S(1)}, f32[36,96,128]{2,1,0:T(8,128)S(1)}, f32[3...) custom-call(f32[21,64,128]{2,1,0:T(8,128)S(1)} %collective-permute-d, ...), custom_call_target="tpu_custom_call" | custom-call | tf_op jit(solution)/shard_map/down/pallas_call | solution.py:23
  21.0 3.7 %collective-permute-start.6 = (f32[8,8,128]{2,1,0:T(8,128)S(1)}, f32[8,8,128]{2,1,0:T(8,128)S(1)}, u32[]{:S(2)}, u32[]{:S(2)}) collective-permute-start(f32[8,8,128]{2,1,0:T(8,128)S(1)} %get-tuple-element.75), channel_id=1, source_target_pairs={{0,1},{1,0},{2,3},{3,2},{4,5},{5,4},{6,7},{7,6},{8,9},{9,8},{10,11... | collective-permute-start | bytes 98312 | tf_op jit(solution)/shard_map/ppermute | solution.py:670
  24.8 0.7 collective-permute-start.7
  25.4 1.2 %collective-permute-done.6.y0 = f32[8,8,128]{2,1,0:T(8,128)S(1)} collective-permute-done((f32[8,8,128]{2,1,0:T(8,128)S(1)}, f32[8,8,128]{2,1,0:T(8,128)S(1)}, u32[]{:S(2)}, u32[]{:S(2)}) %collective-permute-start.6) | collective-permute-done | bytes 32800 | tf_op jit(solution)/shard_map/ppermute | solution.py:670
  26.7 0.0 collective-permute-done.7.y1
  26.7 0.2 edges2.1
  26.9 3.9 %collective-permute-start.9 = (f32[232,128]{1,0:T(8,128)S(1)}, f32[232,128]{1,0:T(8,128)S(1)}, u32[]{:S(2)}, u32[]{:S(2)}) collective-permute-start(f32[232,128]{1,0:T(8,128)S(1)} %get-tuple-element.79), channel_id=1, source_target_pairs={{4,8},{8,4},{12,16},{16,12},{20,24},{24,20},{28,32},{32,28},{36,40... | collective-permute-start | bytes 356360 | tf_op jit(solution)/shard_map/ppermute | solution.py:669
  30.8 0.1 collective-permute-start.8
  30.9 2.4 %collective-permute-done.9.x1 = f32[232,128]{1,0:T(8,128)S(1)} collective-permute-done((f32[232,128]{1,0:T(8,128)S(1)}, f32[232,128]{1,0:T(8,128)S(1)}, u32[]{:S(2)}, u32[]{:S(2)}) %collective-permute-start.9) | collective-permute-done | bytes 118816 | tf_op jit(solution)/shard_map/ppermute | solution.py:669
  33.3 0.0 collective-permute-start.10
  33.3 0.0 collective-permute-done.8.x0
  33.3 1.3 %collective-permute-done.10.far = f32[232,128]{1,0:T(8,128)S(1)} collective-permute-done((f32[232,128]{1,0:T(8,128)S(1)}, f32[232,128]{1,0:T(8,128)S(1)}, u32[]{:S(2)}, u32[]{:S(2)}) %collective-permute-start.10) | collective-permute-done | bytes 118816 | tf_op jit(solution)/shard_map/ppermute | solution.py:668
  34.6 1.0 %level2.1 = (f32[16,48,128]{2,1,0:T(8,128)S(1)}, f32[16,48,128]{2,1,0:T(8,128)S(1)}, f32[16,48,128]{2,1,0:T(8,128)S(1)}, f32[16,48,128]{2,1,0:T(8,128)S(1)}, f32...) custom-call(f32[18,64,128]{2,1,0:T(8,128)S(1)} %get-tuple-element.72., ...), custom_call_target="tpu_custom_call" | custom-call | tf_op jit(solution)/shard_map/level2/pallas_call | solution.py:23
  35.6 24.6 %all_to_all.11 = f32[128,4,128]{2,1,0:T(4,128)S(1)} all-to-all(f32[128,4,128]{2,1,0:T(4,128)S(1)} %bitcast.3), channel_id=1, replica_groups=mesh['gx'=32,'gy'=4] {'gx','gy'}, dimensions={0} | all-to-all | bytes 524288 | tf_op jit(solution)/shard_map/all_to_all | solution.py:717
  60.2 9.6 %up.1 = (f32[16,64,128]{2,1,0:T(8,128)}, f32[16,64,128]{2,1,0:T(8,128)}) custom-call(f32[512,128]{1,0:T(8,128)S(1)} %bitcast.2, f32[8,8,128]{2,1,0:T(8,128)S(1)} %collective-permute-done.6.y0, f32[8,8,128]{2,1,0:T(8,128)S(1)} %collective-permute-done.7.y1, f32[232,128]{1,0:T(8,128)S(1)} %collective-permute-done.9.x1, ...), custom_call_target="tpu_custom_call" | custom-call | tf_op jit(solution)/shard_map/up/pallas_call | solution.py:23
  (1 shorter events, 0.0 us)
Async XLA Ops:
  2.2 7.0 %collective-permute-start.2 = (f32[32,8,128]{2,1,0:T(8,128)S(1)}, f32[32,8,128]{2,1,0:T(8,128)S(1)}, u32[]{:S(2)}, u32[]{:S(2)}) collective-permute-start(f32[32,8,128]{2,1,0:T(8,128)S(1)} %get-tuple-element.54), channel_id=1, source_target_pairs={{0,1},{1,0},{2,3},{3,2},{4,5},{5,4},{6,7},{7,6},{8,9},{9,8},{10,11... | collective-permute-start | bytes 393224 | tf_op jit(solution)/shard_map/ppermute | solution.py:670
  4.4 4.9 %collective-permute-start.3 = (f32[32,8,128]{2,1,0:T(8,128)S(1)}, f32[32,8,128]{2,1,0:T(8,128)S(1)}, u32[]{:S(2)}, u32[]{:S(2)}) collective-permute-start(f32[32,8,128]{2,1,0:T(8,128)S(1)} %get-tuple-element.55), channel_id=1, source_target_pairs={{1,2},{2,1},{5,6},{6,5},{9,10},{10,9},{13,14},{14,13},{17,18},{18,... | collective-permute-start | bytes 393224 | tf_op jit(solution)/shard_map/ppermute | solution.py:669
  5.1 10.7 %collective-permute-start.1 = (f32[14,64,128]{2,1,0:T(8,128)S(1)}, f32[14,64,128]{2,1,0:T(8,128)S(1)}, u32[]{:S(2)}, u32[]{:S(2)}) collective-permute-start(f32[14,64,128]{2,1,0:T(8,128)S(1)} %get-tuple-element.53), channel_id=1, source_target_pairs={{4,8},{8,4},{12,16},{16,12},{20,24},{24,20},{28,32},{32,28},{36,40... | collective-permute-start | bytes 1376264 | tf_op jit(solution)/shard_map/ppermute | solution.py:669
  9.2 6.7 %collective-permute-start = (f32[21,64,128]{2,1,0:T(8,128)S(1)}, f32[21,64,128]{2,1,0:T(8,128)S(1)}, u32[]{:S(2)}, u32[]{:S(2)}) collective-permute-start(f32[21,64,128]{2,1,0:T(8,128)S(1)} %get-tuple-element.52), channel_id=1, source_target_pairs={{0,4},{4,0},{8,12},{12,8},{16,20},{20,16},{24,28},{28,24},{32,36},... | collective-permute-start | bytes 2064392 | tf_op jit(solution)/shard_map/ppermute | solution.py:670
  9.3 6.5 %collective-permute-start.5 = (f32[6,16,128]{2,1,0:T(8,128)S(1)}, f32[6,16,128]{2,1,0:T(8,128)S(1)}, u32[]{:S(2)}, u32[]{:S(2)}) collective-permute-start(f32[6,16,128]{2,1,0:T(8,128)S(1)} %get-tuple-element.57), channel_id=1, source_target_pairs={{4,8},{8,4},{12,16},{16,12},{20,24},{24,20},{28,32},{32,28},{36,40... | collective-permute-start | bytes 147464 | tf_op jit(solution)/shard_map/ppermute | solution.py:669
  12.9 3.0 %collective-permute-start.4 = (f32[13,16,128]{2,1,0:T(8,128)S(1)}, f32[13,16,128]{2,1,0:T(8,128)S(1)}, u32[]{:S(2)}, u32[]{:S(2)}) collective-permute-start(f32[13,16,128]{2,1,0:T(8,128)S(1)} %get-tuple-element.56), channel_id=1, source_target_pairs={{0,4},{4,0},{8,12},{12,8},{16,20},{20,16},{24,28},{28,24},{32,36},... | collective-permute-start | bytes 319496 | tf_op jit(solution)/shard_map/ppermute | solution.py:670
  21.0 5.6 %collective-permute-start.6 = (f32[8,8,128]{2,1,0:T(8,128)S(1)}, f32[8,8,128]{2,1,0:T(8,128)S(1)}, u32[]{:S(2)}, u32[]{:S(2)}) collective-permute-start(f32[8,8,128]{2,1,0:T(8,128)S(1)} %get-tuple-element.75), channel_id=1, source_target_pairs={{0,1},{1,0},{2,3},{3,2},{4,5},{5,4},{6,7},{7,6},{8,9},{9,8},{10,11... | collective-permute-start | bytes 98312 | tf_op jit(solution)/shard_map/ppermute | solution.py:670
  24.8 1.9 %collective-permute-start.7 = (f32[8,8,128]{2,1,0:T(8,128)S(1)}, f32[8,8,128]{2,1,0:T(8,128)S(1)}, u32[]{:S(2)}, u32[]{:S(2)}) collective-permute-start(f32[8,8,128]{2,1,0:T(8,128)S(1)} %get-tuple-element.76), channel_id=1, source_target_pairs={{1,2},{2,1},{5,6},{6,5},{9,10},{10,9},{13,14},{14,13},{17,18},{18,... | collective-permute-start | bytes 98312 | tf_op jit(solution)/shard_map/ppermute | solution.py:669
  26.9 6.4 %collective-permute-start.9 = (f32[232,128]{1,0:T(8,128)S(1)}, f32[232,128]{1,0:T(8,128)S(1)}, u32[]{:S(2)}, u32[]{:S(2)}) collective-permute-start(f32[232,128]{1,0:T(8,128)S(1)} %get-tuple-element.79), channel_id=1, source_target_pairs={{4,8},{8,4},{12,16},{16,12},{20,24},{24,20},{28,32},{32,28},{36,40... | collective-permute-start | bytes 356360 | tf_op jit(solution)/shard_map/ppermute | solution.py:669
  30.8 2.5 %collective-permute-start.8 = (f32[232,128]{1,0:T(8,128)S(1)}, f32[232,128]{1,0:T(8,128)S(1)}, u32[]{:S(2)}, u32[]{:S(2)}) collective-permute-start(f32[232,128]{1,0:T(8,128)S(1)} %get-tuple-element.78), channel_id=1, source_target_pairs={{0,4},{4,0},{8,12},{12,8},{16,20},{20,16},{24,28},{28,24},{32,36},... | collective-permute-start | bytes 356360 | tf_op jit(solution)/shard_map/ppermute | solution.py:670
  33.3 1.3 %collective-permute-start.10 = (f32[232,128]{1,0:T(8,128)S(1)}, f32[232,128]{1,0:T(8,128)S(1)}, u32[]{:S(2)}, u32[]{:S(2)}) collective-permute-start(f32[232,128]{1,0:T(8,128)S(1)} %collective-permute-done.9.x1), channel_id=1, source_target_pairs={{0,4},{4,0},{8,12},{12,8},{16,20},{20,16},{24,28},{28,24},{32,36},... | collective-permute-start | bytes 356360 | tf_op jit(solution)/shard_map/ppermute | solution.py:668

commit v6 on v5

--- a/solution.py
+++ b/solution.py
@@ -439,6 +439,16 @@
     return jnp.dot(a, b, precision=lax.Precision.HIGHEST, preferred_element_type=F32)
 
 
+def halves(v):
+    high = v.astype(jnp.bfloat16)
+    return high, (v - high.astype(F32)).astype(jnp.bfloat16)
+
+
+def split_dot(a, b):
+    (a1, a2), (b1, b2) = halves(a), halves(b)
+    return jnp.dot(jnp.concatenate([a1, a2, a1], 1), jnp.concatenate([b1, b1, b2], 0), preferred_element_type=F32)
+
+
 def level2_kernel(
     u1_in, c2_in, b2_in, y0, y1, x0, x1, far,
     fx, fy, fz, w, b2, u2, u1, gather,
@@ -554,13 +564,42 @@
         return scale * pair_lanes(pair_lanes(v, self.s), self.st)
 
 
+def coarsest(level, g):
+    def column(v):
+        v = v.reshape(32, NZ)
+        low = lane(v.shape) % 16 < 8
+        return jnp.concatenate([jnp.where(low, v, lroll(v, 8)), jnp.where(low, lroll(v, -8), v)], 0)
+
+    shape = (64, NZ)
+    i, j = lax.broadcasted_iota(jnp.int32, shape, 0), lane(shape)
+
+    def pad(v):
+        return jnp.concatenate([v, jnp.zeros(shape, F32)], 0)
+
+    m = jnp.where(i == j, KEEP, 0.0)
+    w = level.w
+    for coef, at in (
+        (w * level.fxp, i + 1),
+        (w * level.fxm, i - 1),
+        (w * level.fyp, i + 8),
+        (w * level.fym, i - 8),
+        (w * (level.fzp + level.fzm), i ^ 32),
+    ):
+        m = m + jnp.where(j == at, column(coef), 0.0)
+    total = m + jnp.where(i == j, 1.0, 0.0)
+    for _ in range(3):
+        m = split_dot(m, pad(m))
+        total = total + split_dot(m, pad(total))
+    u = split_dot(total, pad(column(g)))
+    low = lane((32, NZ)) % 16 < 8
+    return jnp.where(low, u[:32], u[32:]).reshape(g.shape)
+
+
 def whole_cycle(depth, b, c):
     level = Whole(depth, b, c)
     v = level.w * b
     if depth == 6:
-        for _ in range(SWEEPS_COARSE - 1):
-            v = level.sweep(v)
-        return v
+        return coarsest(level, v)
     v = level.sweep(v)
     below = whole_cycle(depth + 1, level.coarse(level.residual(v), 0.5), level.coarse(c, 0.125))
     v = v + jnp.concatenate([below[k // 2 : k // 2 + 1] for k in range(v.shape[0])], 0)
@@ -619,7 +658,7 @@
 
     rows(0, 8, grow1)
 
-    copy_rows([(b1_in, b1)], 3, 17)
+    copy_rows([(b1_in, b1)], 2, 18)
     set_y1(b1, y0, y1, oy, 1)
     for j, v in enumerate(unpack_lanes(x1[pl.ds(176, 40), :], 2)):
         b1[X1 - 1 - j, pl.ds(12, 40), :] = v

time: 70.1 us -> 69.2 us (0.987)
  Pallas kernels: 19.9 us -> 19 us
    pallas_call x8, Pallas kernels: 19.9 us -> 19 us  [call(): pl.pallas_call(body, out_shape=[jax.ShapeDtypeStruct(s, F32) for s in out...]
where the time goes in v6:
time: 69.2 us; the launch traced here: 68.9 us
  blocking collectives  24.6 us (36%)
  Pallas kernels  19 us (27%)
  starting transfers between devices  18.9 us (27%)
  waiting for transfers between devices  5.62 us (8%)
  between operations  0.77 us (1%)
    all_to_all x1, blocking collectives, per_device(): whole = lax.all_to_all(packed, ('gx', 'gy'), 0, 0, tiled=True)  24.6 us
    pallas_call x8, Pallas kernels, call(): pl.pallas_call(body, out_shape=[jax.ShapeDtypeStruct(s, F32) for s in out...  19 us
    ppermute x5, starting transfers between devices, swaps(): late = lax.ppermute(second, axis, pairs(1))  12.8 us
    ppermute x5, starting transfers between devices, swaps(): return (lax.ppermute(first, axis, pairs(0)), late)  6.1 us
    ppermute x5, waiting for transfers between devices, swaps(): late = lax.ppermute(second, axis, pairs(1))  3.05 us
  transfers between devices with their start and end apart: 11, of which 4 were waited for; matrix products, arithmetic and copies ran while one was open for 0% of the time, Pallas kernels for 3%

profile of v6, /device:TPU:1, one launch (start us, length us, event | category | flops | bytes accessed | tf_op | source)
XLA Modules:
  0.0 68.9 jit_solution(5155977675717871795)
XLA Ops:
  0.6 1.6 %begin.1 = (f32[16,64,128]{2,1,0:T(8,128)S(1)}, f32[16,64,128]{2,1,0:T(8,128)S(1)}, f32[32,8,128]{2,1,0:T(8,128)S(1)}, f32[32,8,128]{2,1,0:T(8,128)S(1)}) custom-call(f32[16,64,128]{2,1,0:T(8,128)} %source.1, f32[16,64,128]{2,1,0:T(8,128)} %density.1, f32[16,64,128]{2,1,0:T(8,128)} %drag.1, s32[64]{0:T(128)} %porous.1), custom_call_target="tpu_custom_call" | custom-call | tf_op jit(solution)/shard_map/begin/pallas_call | solution.py:23
  2.2 2.1 %collective-permute-start.2 = (f32[32,8,128]{2,1,0:T(8,128)S(1)}, f32[32,8,128]{2,1,0:T(8,128)S(1)}, u32[]{:S(2)}, u32[]{:S(2)}) collective-permute-start(f32[32,8,128]{2,1,0:T(8,128)S(1)} %get-tuple-element.54), channel_id=1, source_target_pairs={{0,1},{1,0},{2,3},{3,2},{4,5},{5,4},{6,7},{7,6},{8,9},{9,8},{10,11... | collective-permute-start | bytes 393224 | tf_op jit(solution)/shard_map/ppermute | solution.py:709
  4.4 0.7 collective-permute-start.3
  5.0 0.1 edges.1
  5.1 4.0 %collective-permute-start.1 = (f32[14,64,128]{2,1,0:T(8,128)S(1)}, f32[14,64,128]{2,1,0:T(8,128)S(1)}, u32[]{:S(2)}, u32[]{:S(2)}) collective-permute-start(f32[14,64,128]{2,1,0:T(8,128)S(1)} %get-tuple-element.53), channel_id=1, source_target_pairs={{4,8},{8,4},{12,16},{16,12},{20,24},{24,20},{28,32},{32,28},{36,40... | collective-permute-start | bytes 1376264 | tf_op jit(solution)/shard_map/ppermute | solution.py:708
  9.2 0.1 collective-permute-start
  9.3 0.0 collective-permute-done.2.y0
  9.3 0.0 collective-permute-done.3.y1
  9.3 3.6 %collective-permute-start.5 = (f32[6,16,128]{2,1,0:T(8,128)S(1)}, f32[6,16,128]{2,1,0:T(8,128)S(1)}, u32[]{:S(2)}, u32[]{:S(2)}) collective-permute-start(f32[6,16,128]{2,1,0:T(8,128)S(1)} %get-tuple-element.57), channel_id=1, source_target_pairs={{4,8},{8,4},{12,16},{16,12},{20,24},{24,20},{28,32},{32,28},{36,40... | collective-permute-start | bytes 147464 | tf_op jit(solution)/shard_map/ppermute | solution.py:708
  12.9 0.1 collective-permute-start.4
  13.0 2.2 %inner.1 = (f32[18,96,128]{2,1,0:T(8,128)S(1)}, f32[18,96,128]{2,1,0:T(8,128)S(1)}, f32[18,96,128]{2,1,0:T(8,128)S(1)}, f32[18,96,128]{2,1,0:T(8,128)S(1)}, f32[...) custom-call(f32[16,64,128]{2,1,0:T(8,128)S(1)} %get-tuple-element.50, ...), custom_call_target="tpu_custom_call" | custom-call | flops 10000000000 | tf_op jit(solution)/shard_map/inner/pallas_call | solution.py:23
  15.2 0.6 collective-permute-done.5.k1
  15.8 0.0 collective-permute-done.4.k0
  15.8 0.0 collective-permute-done.1.x1
  15.8 0.0 collective-permute-done.x0
  15.9 5.2 %down.1 = (f32[36,96,128]{2,1,0:T(8,128)S(1)}, f32[36,96,128]{2,1,0:T(8,128)S(1)}, f32[36,96,128]{2,1,0:T(8,128)S(1)}, f32[36,96,128]{2,1,0:T(8,128)S(1)}, f32[3...) custom-call(f32[21,64,128]{2,1,0:T(8,128)S(1)} %collective-permute-d, ...), custom_call_target="tpu_custom_call" | custom-call | tf_op jit(solution)/shard_map/down/pallas_call | solution.py:23
  21.0 3.7 %collective-permute-start.6 = (f32[8,8,128]{2,1,0:T(8,128)S(1)}, f32[8,8,128]{2,1,0:T(8,128)S(1)}, u32[]{:S(2)}, u32[]{:S(2)}) collective-permute-start(f32[8,8,128]{2,1,0:T(8,128)S(1)} %get-tuple-element.75), channel_id=1, source_target_pairs={{0,1},{1,0},{2,3},{3,2},{4,5},{5,4},{6,7},{7,6},{8,9},{9,8},{10,11... | collective-permute-start | bytes 98312 | tf_op jit(solution)/shard_map/ppermute | solution.py:709
  24.8 0.7 collective-permute-start.7
  25.4 1.2 %collective-permute-done.6.y0 = f32[8,8,128]{2,1,0:T(8,128)S(1)} collective-permute-done((f32[8,8,128]{2,1,0:T(8,128)S(1)}, f32[8,8,128]{2,1,0:T(8,128)S(1)}, u32[]{:S(2)}, u32[]{:S(2)}) %collective-permute-start.6) | collective-permute-done | bytes 32800 | tf_op jit(solution)/shard_map/ppermute | solution.py:709
  26.7 0.0 collective-permute-done.7.y1
  26.7 0.2 edges2.1
  26.9 3.9 %collective-permute-start.9 = (f32[232,128]{1,0:T(8,128)S(1)}, f32[232,128]{1,0:T(8,128)S(1)}, u32[]{:S(2)}, u32[]{:S(2)}) collective-permute-start(f32[232,128]{1,0:T(8,128)S(1)} %get-tuple-element.79), channel_id=1, source_target_pairs={{4,8},{8,4},{12,16},{16,12},{20,24},{24,20},{28,32},{32,28},{36,40... | collective-permute-start | bytes 356360 | tf_op jit(solution)/shard_map/ppermute | solution.py:708
  30.8 0.1 collective-permute-start.8
  30.9 2.4 %collective-permute-done.9.x1 = f32[232,128]{1,0:T(8,128)S(1)} collective-permute-done((f32[232,128]{1,0:T(8,128)S(1)}, f32[232,128]{1,0:T(8,128)S(1)}, u32[]{:S(2)}, u32[]{:S(2)}) %collective-permute-start.9) | collective-permute-done | bytes 118816 | tf_op jit(solution)/shard_map/ppermute | solution.py:708
  33.3 0.0 collective-permute-start.10
  33.3 0.0 collective-permute-done.8.x0
  33.3 1.3 %collective-permute-done.10.far = f32[232,128]{1,0:T(8,128)S(1)} collective-permute-done((f32[232,128]{1,0:T(8,128)S(1)}, f32[232,128]{1,0:T(8,128)S(1)}, u32[]{:S(2)}, u32[]{:S(2)}) %collective-permute-start.10) | collective-permute-done | bytes 118816 | tf_op jit(solution)/shard_map/ppermute | solution.py:707
  34.6 1.0 %level2.1 = (f32[16,48,128]{2,1,0:T(8,128)S(1)}, f32[16,48,128]{2,1,0:T(8,128)S(1)}, f32[16,48,128]{2,1,0:T(8,128)S(1)}, f32[16,48,128]{2,1,0:T(8,128)S(1)}, f32...) custom-call(f32[18,64,128]{2,1,0:T(8,128)S(1)} %get-tuple-element.72., ...), custom_call_target="tpu_custom_call" | custom-call | tf_op jit(solution)/shard_map/level2/pallas_call | solution.py:23
  35.6 24.6 %all_to_all.11 = f32[128,4,128]{2,1,0:T(4,128)S(1)} all-to-all(f32[128,4,128]{2,1,0:T(4,128)S(1)} %bitcast.3), channel_id=1, replica_groups=mesh['gx'=32,'gy'=4] {'gx','gy'}, dimensions={0} | all-to-all | bytes 524288 | tf_op jit(solution)/shard_map/all_to_all | solution.py:756
  60.2 8.8 %up.1 = (f32[16,64,128]{2,1,0:T(8,128)}, f32[16,64,128]{2,1,0:T(8,128)}) custom-call(f32[512,128]{1,0:T(8,128)S(1)} %bitcast.2, f32[8,8,128]{2,1,0:T(8,128)S(1)} %collective-permute-done.6.y0, f32[8,8,128]{2,1,0:T(8,128)S(1)} %collective-permute-done.7.y1, f32[232,128]{1,0:T(8,128)S(1)} %collective-permute-done.9.x1, ...), custom_call_target="tpu_custom_call" | custom-call | tf_op jit(solution)/shard_map/up/pallas_call | solution.py:23
  (1 shorter events, 0.0 us)
Async XLA Ops:
  2.2 7.0 %collective-permute-start.2 = (f32[32,8,128]{2,1,0:T(8,128)S(1)}, f32[32,8,128]{2,1,0:T(8,128)S(1)}, u32[]{:S(2)}, u32[]{:S(2)}) collective-permute-start(f32[32,8,128]{2,1,0:T(8,128)S(1)} %get-tuple-element.54), channel_id=1, source_target_pairs={{0,1},{1,0},{2,3},{3,2},{4,5},{5,4},{6,7},{7,6},{8,9},{9,8},{10,11... | collective-permute-start | bytes 393224 | tf_op jit(solution)/shard_map/ppermute | solution.py:709
  4.4 4.9 %collective-permute-start.3 = (f32[32,8,128]{2,1,0:T(8,128)S(1)}, f32[32,8,128]{2,1,0:T(8,128)S(1)}, u32[]{:S(2)}, u32[]{:S(2)}) collective-permute-start(f32[32,8,128]{2,1,0:T(8,128)S(1)} %get-tuple-element.55), channel_id=1, source_target_pairs={{1,2},{2,1},{5,6},{6,5},{9,10},{10,9},{13,14},{14,13},{17,18},{18,... | collective-permute-start | bytes 393224 | tf_op jit(solution)/shard_map/ppermute | solution.py:708
  5.1 10.7 %collective-permute-start.1 = (f32[14,64,128]{2,1,0:T(8,128)S(1)}, f32[14,64,128]{2,1,0:T(8,128)S(1)}, u32[]{:S(2)}, u32[]{:S(2)}) collective-permute-start(f32[14,64,128]{2,1,0:T(8,128)S(1)} %get-tuple-element.53), channel_id=1, source_target_pairs={{4,8},{8,4},{12,16},{16,12},{20,24},{24,20},{28,32},{32,28},{36,40... | collective-permute-start | bytes 1376264 | tf_op jit(solution)/shard_map/ppermute | solution.py:708
  9.2 6.7 %collective-permute-start = (f32[21,64,128]{2,1,0:T(8,128)S(1)}, f32[21,64,128]{2,1,0:T(8,128)S(1)}, u32[]{:S(2)}, u32[]{:S(2)}) collective-permute-start(f32[21,64,128]{2,1,0:T(8,128)S(1)} %get-tuple-element.52), channel_id=1, source_target_pairs={{0,4},{4,0},{8,12},{12,8},{16,20},{20,16},{24,28},{28,24},{32,36},... | collective-permute-start | bytes 2064392 | tf_op jit(solution)/shard_map/ppermute | solution.py:709
  9.3 6.5 %collective-permute-start.5 = (f32[6,16,128]{2,1,0:T(8,128)S(1)}, f32[6,16,128]{2,1,0:T(8,128)S(1)}, u32[]{:S(2)}, u32[]{:S(2)}) collective-permute-start(f32[6,16,128]{2,1,0:T(8,128)S(1)} %get-tuple-element.57), channel_id=1, source_target_pairs={{4,8},{8,4},{12,16},{16,12},{20,24},{24,20},{28,32},{32,28},{36,40... | collective-permute-start | bytes 147464 | tf_op jit(solution)/shard_map/ppermute | solution.py:708
  12.9 3.0 %collective-permute-start.4 = (f32[13,16,128]{2,1,0:T(8,128)S(1)}, f32[13,16,128]{2,1,0:T(8,128)S(1)}, u32[]{:S(2)}, u32[]{:S(2)}) collective-permute-start(f32[13,16,128]{2,1,0:T(8,128)S(1)} %get-tuple-element.56), channel_id=1, source_target_pairs={{0,4},{4,0},{8,12},{12,8},{16,20},{20,16},{24,28},{28,24},{32,36},... | collective-permute-start | bytes 319496 | tf_op jit(solution)/shard_map/ppermute | solution.py:709
  21.0 5.6 %collective-permute-start.6 = (f32[8,8,128]{2,1,0:T(8,128)S(1)}, f32[8,8,128]{2,1,0:T(8,128)S(1)}, u32[]{:S(2)}, u32[]{:S(2)}) collective-permute-start(f32[8,8,128]{2,1,0:T(8,128)S(1)} %get-tuple-element.75), channel_id=1, source_target_pairs={{0,1},{1,0},{2,3},{3,2},{4,5},{5,4},{6,7},{7,6},{8,9},{9,8},{10,11... | collective-permute-start | bytes 98312 | tf_op jit(solution)/shard_map/ppermute | solution.py:709
  24.8 1.9 %collective-permute-start.7 = (f32[8,8,128]{2,1,0:T(8,128)S(1)}, f32[8,8,128]{2,1,0:T(8,128)S(1)}, u32[]{:S(2)}, u32[]{:S(2)}) collective-permute-start(f32[8,8,128]{2,1,0:T(8,128)S(1)} %get-tuple-element.76), channel_id=1, source_target_pairs={{1,2},{2,1},{5,6},{6,5},{9,10},{10,9},{13,14},{14,13},{17,18},{18,... | collective-permute-start | bytes 98312 | tf_op jit(solution)/shard_map/ppermute | solution.py:708
  26.9 6.4 %collective-permute-start.9 = (f32[232,128]{1,0:T(8,128)S(1)}, f32[232,128]{1,0:T(8,128)S(1)}, u32[]{:S(2)}, u32[]{:S(2)}) collective-permute-start(f32[232,128]{1,0:T(8,128)S(1)} %get-tuple-element.79), channel_id=1, source_target_pairs={{4,8},{8,4},{12,16},{16,12},{20,24},{24,20},{28,32},{32,28},{36,40... | collective-permute-start | bytes 356360 | tf_op jit(solution)/shard_map/ppermute | solution.py:708
  30.8 2.5 %collective-permute-start.8 = (f32[232,128]{1,0:T(8,128)S(1)}, f32[232,128]{1,0:T(8,128)S(1)}, u32[]{:S(2)}, u32[]{:S(2)}) collective-permute-start(f32[232,128]{1,0:T(8,128)S(1)} %get-tuple-element.78), channel_id=1, source_target_pairs={{0,4},{4,0},{8,12},{12,8},{16,20},{20,16},{24,28},{28,24},{32,36},... | collective-permute-start | bytes 356360 | tf_op jit(solution)/shard_map/ppermute | solution.py:709
  33.3 1.3 %collective-permute-start.10 = (f32[232,128]{1,0:T(8,128)S(1)}, f32[232,128]{1,0:T(8,128)S(1)}, u32[]{:S(2)}, u32[]{:S(2)}) collective-permute-start(f32[232,128]{1,0:T(8,128)S(1)} %collective-permute-done.9.x1), channel_id=1, source_target_pairs={{0,4},{4,0},{8,12},{12,8},{16,20},{20,16},{24,28},{28,24},{32,36},... | collective-permute-start | bytes 356360 | tf_op jit(solution)/shard_map/ppermute | solution.py:707

commit v7 on v6

--- a/solution.py
+++ b/solution.py
@@ -418,15 +418,16 @@
         for k in range(2):
             t = [u1[edge1 + sign * (2 * k + j), pl.ds(12, 40), :] for j in range(2)]
             pack[pl.ds(k * 40, 40), :] = pack_lanes(t)
-        t = [c2[edge2 + sign * d, pl.ds(8, 32), :] for d in range(6)]
-        t += [b2[edge2 + sign * d, pl.ds(8, 32), :] for d in range(5 if sign == 1 else 4)]
+        t = [c2[edge2 + sign * d, pl.ds(10, 28), :] for d in range(6)]
+        t += [b2[edge2 + sign * d, pl.ds(10, 28), :] for d in range(5 if sign == 1 else 4)]
         t += t[:1] * (12 - len(t))
         for k in range(3):
-            pack[pl.ds(80 + k * 32, 32), :] = pack_lanes(t[4 * k : 4 * k + 4])
-        t = [b1[edge1 + sign * j, pl.ds(12, 40), :] for j in range(2)]
-        pack[pl.ds(176, 40), :] = pack_lanes(t)
+            pack[pl.ds(80 + k * 28, 28), :] = pack_lanes(t[4 * k : 4 * k + 4])
+        for n, y in enumerate((12, 48)):
+            t = [b1[edge1 + sign * j, pl.ds(y, 4), :] for j in range(2)]
+            pack[pl.ds(164 + 4 * n, 4), :] = pack_lanes(t)
         t = [b1[edge1 + sign * 2, pl.ds(16 + 16 * j, 16), :] for j in range(2)]
-        pack[pl.ds(216, 16), :] = pack_lanes(t)
+        pack[pl.ds(172, 16), :] = pack_lanes(t)
 
 
 def one_hot(shape, f):
@@ -450,7 +451,7 @@
 
 
 def level2_kernel(
-    u1_in, c2_in, b2_in, y0, y1, x0, x1, far,
+    u1_in, c2_in, b2_in, y0, y1, x0, x1,
     fx, fy, fz, w, b2, u2, u1, gather,
     c2, ua, tmp, b3, c3,
 ):
@@ -466,12 +467,11 @@
                 u1[edge1 + sign * (2 * k + j + 1), pl.ds(12, 40), :] = v
         t = []
         for k in range(3):
-            t += unpack_lanes(pack[pl.ds(80 + k * 32, 32), :], 4)
+            t += unpack_lanes(pack[pl.ds(80 + k * 28, 28), :], 4)
         for d in range(6):
-            c2[edge2 + sign * (d + 1), pl.ds(8, 32), :] = t[d]
+            c2[edge2 + sign * (d + 1), pl.ds(10, 28), :] = t[d]
         for d in range(5 if sign == -1 else 4):
-            b2[edge2 + sign * (d + 1), pl.ds(8, 32), :] = t[6 + d]
-    b2[X2 + 8, pl.ds(8, 32), :] = unpack_lanes(far[pl.ds(112, 32), :], 4)[2]
+            b2[edge2 + sign * (d + 1), pl.ds(10, 28), :] = t[6 + d]
 
     low = Level(2, c2, b2, fx, fy, fz, w, 8, 40)
     low.faces(0, 15)
@@ -607,7 +607,7 @@
 
 
 def up_kernel(
-    gather, y0, y1, x1,
+    gather, y0, y1, x1, far,
     hx, hy, hz, hw, b2, u2,
     gx_, gy_, gz_, gw_, b1_in, u1,
     fx, fy, fz, w, b, u0,
@@ -616,6 +616,11 @@
 ):
     ix, iy = lax.axis_index("gx"), lax.axis_index("gy")
     ox, oy = ix % 2, iy % 2
+    low = Level(2, None, b2, hx, hy, hz, hw, 8, 40)
+    wide = pl.ds(8, 32)
+    low.start(ha, X2 + 6, X2 + 8)
+    ha[X2 + 8, pl.ds(10, 28), :] = hw[X2 + 8, pl.ds(10, 28), :] * unpack_lanes(far[pl.ds(108, 28), :], 4)[2]
+    low.sweep(ha, hb, X2 + 7, X2 + 8)
 
     def field(k):
         return jnp.stack(
@@ -646,8 +651,7 @@
         e2[k, pl.ds(1, 24, stride=2), :] = t
 
     for x in range(2, 14):
-        ha[x] = u2[x] + e2[(x - 2) // 2]
-    low = Level(2, None, b2, hx, hy, hz, hw, 8, 40)
+        ha[x, wide, :] = (hb if x == X2 + 7 else u2)[x, wide, :] + e2[(x - 2) // 2, wide, :]
     low.sweep(ha, hb, 3, 13)
     low.sweep(hb, ha, 4, 12)
 
@@ -660,9 +664,10 @@
 
     copy_rows([(b1_in, b1)], 2, 18)
     set_y1(b1, y0, y1, oy, 1)
-    for j, v in enumerate(unpack_lanes(x1[pl.ds(176, 40), :], 2)):
-        b1[X1 - 1 - j, pl.ds(12, 40), :] = v
-    for j, v in enumerate(unpack_lanes(x1[pl.ds(216, 16), :], 2)):
+    for j, v in enumerate(unpack_lanes(x1[pl.ds(164, 8), :], 2)):
+        b1[X1 - 1 - j, pl.ds(12, 4), :] = v[0:4]
+        b1[X1 - 1 - j, pl.ds(48, 4), :] = v[4:8]
+    for j, v in enumerate(unpack_lanes(x1[pl.ds(172, 16), :], 2)):
         b1[X1 - 3, pl.ds(16 + 16 * j, 16), :] = v
 
     def add1(k):
@@ -742,23 +747,24 @@
     level0, level1 = down[:6], down[6:12]
     u1, c2, b2, p0, p1 = down[11:]
     y0, y1 = swaps("gy", p0, p1)
-    p0, p1 = call(edge2_kernel, [(232, NZ)] * 2, [one, one, two, two], (u1, level1[4], c2, b2, y0, y1), "edges2", 16)
+    p0, p1 = call(edge2_kernel, [(192, NZ)] * 2, [one, one, two, two], (u1, level1[4], c2, b2, y0, y1), "edges2", 16)
     x0, x1 = swaps("gx", p0, p1)
     far = swaps("gx", x1)
     *level2, u1, packed = call(
         level2_kernel,
         [two] * 6 + [one, (512, NZ)],
         [two] * 2 + [(2, 48, NZ)] * 3,
-        (u1, c2, b2, y0, y1, x0, x1, far),
+        (u1, c2, b2, y0, y1, x0, x1),
         "level2",
         16,
     )
+    packed, far = lax.optimization_barrier((packed, far))
     whole = lax.all_to_all(packed, ("gx", "gy"), 0, 0, tiled=True)
     out, res = call(
         up_kernel,
         [block] * 2,
         [(6, 80, NZ), (6, 48, NZ), (8, 64, NZ), (12, 96, NZ)] + [two] * 2 + [one] * 3 + [zero] * 2,
-        (whole, y0, y1, x1, *level2, *level1[:5], u1, *level0),
+        (whole, y0, y1, x1, far, *level2, *level1[:5], u1, *level0),
         "up",
         24,
     )

time: 69.2 us -> 67.7 us (0.978)
  waiting for transfers between devices: 5.62 us -> 4.39 us
    ppermute x1, waiting for transfers between devices: 1.32 us -> 0.3 us  [swaps(): return lax.ppermute(first, axis, pairs(0))]
  transfers between devices with their start and end apart: 11 -> 11, of which waited for: 4 -> 4; matrix products, arithmetic and copies ran while one was open for 0% -> 0% of each run, Pallas kernels for 3% -> 5%
where the time goes in v7:
time: 67.7 us; the launch traced here: 67.4 us
  blocking collectives  24.6 us (36%)
  starting transfers between devices  18.9 us (28%)
  Pallas kernels  18.7 us (28%)
  waiting for transfers between devices  4.39 us (6%)
  between operations  0.77 us (1%)
    all_to_all x1, blocking collectives, per_device(): whole = lax.all_to_all(packed, ('gx', 'gy'), 0, 0, tiled=True)  24.6 us
    pallas_call x8, Pallas kernels, call(): pl.pallas_call(body, out_shape=[jax.ShapeDtypeStruct(s, F32) for s in out...  18.7 us
    ppermute x5, starting transfers between devices, swaps(): late = lax.ppermute(second, axis, pairs(1))  12.8 us
    ppermute x5, starting transfers between devices, swaps(): return (lax.ppermute(first, axis, pairs(0)), late)  6.1 us
    ppermute x5, waiting for transfers between devices, swaps(): late = lax.ppermute(second, axis, pairs(1))  2.83 us
  transfers between devices with their start and end apart: 11, of which 4 were waited for; matrix products, arithmetic and copies ran while one was open for 0% of the time, Pallas kernels for 5%

profile of v7, /device:TPU:1, one launch (start us, length us, event | category | flops | bytes accessed | tf_op | source)
XLA Modules:
  0.0 67.4 jit_solution(6736759495696543243)
XLA Ops:
  0.6 1.6 %begin.1 = (f32[16,64,128]{2,1,0:T(8,128)S(1)}, f32[16,64,128]{2,1,0:T(8,128)S(1)}, f32[32,8,128]{2,1,0:T(8,128)S(1)}, f32[32,8,128]{2,1,0:T(8,128)S(1)}) custom-call(f32[16,64,128]{2,1,0:T(8,128)} %source.1, f32[16,64,128]{2,1,0:T(8,128)} %density.1, f32[16,64,128]{2,1,0:T(8,128)} %drag.1, s32[64]{0:T(128)} %porous.1), custom_call_target="tpu_custom_call" | custom-call | tf_op jit(solution)/shard_map/begin/pallas_call | solution.py:23
  2.2 2.1 %collective-permute-start.2 = (f32[32,8,128]{2,1,0:T(8,128)S(1)}, f32[32,8,128]{2,1,0:T(8,128)S(1)}, u32[]{:S(2)}, u32[]{:S(2)}) collective-permute-start(f32[32,8,128]{2,1,0:T(8,128)S(1)} %get-tuple-element.56), channel_id=1, source_target_pairs={{0,1},{1,0},{2,3},{3,2},{4,5},{5,4},{6,7},{7,6},{8,9},{9,8},{10,11... | collective-permute-start | bytes 393224 | tf_op jit(solution)/shard_map/ppermute | solution.py:714
  4.4 0.7 collective-permute-start.3
  5.0 0.1 edges.1
  5.1 4.0 %collective-permute-start.1 = (f32[14,64,128]{2,1,0:T(8,128)S(1)}, f32[14,64,128]{2,1,0:T(8,128)S(1)}, u32[]{:S(2)}, u32[]{:S(2)}) collective-permute-start(f32[14,64,128]{2,1,0:T(8,128)S(1)} %get-tuple-element.55), channel_id=1, source_target_pairs={{4,8},{8,4},{12,16},{16,12},{20,24},{24,20},{28,32},{32,28},{36,40... | collective-permute-start | bytes 1376264 | tf_op jit(solution)/shard_map/ppermute | solution.py:713
  9.2 0.1 collective-permute-start
  9.3 0.0 collective-permute-done.2.y0
  9.3 0.0 collective-permute-done.3.y1
  9.3 3.6 %collective-permute-start.5 = (f32[6,16,128]{2,1,0:T(8,128)S(1)}, f32[6,16,128]{2,1,0:T(8,128)S(1)}, u32[]{:S(2)}, u32[]{:S(2)}) collective-permute-start(f32[6,16,128]{2,1,0:T(8,128)S(1)} %get-tuple-element.59), channel_id=1, source_target_pairs={{4,8},{8,4},{12,16},{16,12},{20,24},{24,20},{28,32},{32,28},{36,40... | collective-permute-start | bytes 147464 | tf_op jit(solution)/shard_map/ppermute | solution.py:713
  12.9 0.1 collective-permute-start.4
  13.0 2.2 %inner.1 = (f32[18,96,128]{2,1,0:T(8,128)S(1)}, f32[18,96,128]{2,1,0:T(8,128)S(1)}, f32[18,96,128]{2,1,0:T(8,128)S(1)}, f32[18,96,128]{2,1,0:T(8,128)S(1)}, f32[...) custom-call(f32[16,64,128]{2,1,0:T(8,128)S(1)} %get-tuple-element.52, ...), custom_call_target="tpu_custom_call" | custom-call | flops 10000000000 | tf_op jit(solution)/shard_map/inner/pallas_call | solution.py:23
  15.2 0.6 collective-permute-done.5.k1
  15.8 0.0 collective-permute-done.4.k0
  15.8 0.0 collective-permute-done.1.x1
  15.8 0.0 collective-permute-done.x0
  15.9 5.1 %down.1 = (f32[36,96,128]{2,1,0:T(8,128)S(1)}, f32[36,96,128]{2,1,0:T(8,128)S(1)}, f32[36,96,128]{2,1,0:T(8,128)S(1)}, f32[36,96,128]{2,1,0:T(8,128)S(1)}, f32[3...) custom-call(f32[21,64,128]{2,1,0:T(8,128)S(1)} %collective-permute-d, ...), custom_call_target="tpu_custom_call" | custom-call | tf_op jit(solution)/shard_map/down/pallas_call | solution.py:23
  21.0 3.7 %collective-permute-start.6 = (f32[8,8,128]{2,1,0:T(8,128)S(1)}, f32[8,8,128]{2,1,0:T(8,128)S(1)}, u32[]{:S(2)}, u32[]{:S(2)}) collective-permute-start(f32[8,8,128]{2,1,0:T(8,128)S(1)} %get-tuple-element.77), channel_id=1, source_target_pairs={{0,1},{1,0},{2,3},{3,2},{4,5},{5,4},{6,7},{7,6},{8,9},{9,8},{10,11... | collective-permute-start | bytes 98312 | tf_op jit(solution)/shard_map/ppermute | solution.py:714
  24.7 0.7 collective-permute-start.7
  25.4 1.2 %collective-permute-done.6.y0 = f32[8,8,128]{2,1,0:T(8,128)S(1)} collective-permute-done((f32[8,8,128]{2,1,0:T(8,128)S(1)}, f32[8,8,128]{2,1,0:T(8,128)S(1)}, u32[]{:S(2)}, u32[]{:S(2)}) %collective-permute-start.6) | collective-permute-done | bytes 32800 | tf_op jit(solution)/shard_map/ppermute | solution.py:714
  26.6 0.0 collective-permute-done.7.y1
  26.6 0.2 edges2.1
  26.8 3.9 %collective-permute-start.9 = (f32[192,128]{1,0:T(8,128)S(1)}, f32[192,128]{1,0:T(8,128)S(1)}, u32[]{:S(2)}, u32[]{:S(2)}) collective-permute-start(f32[192,128]{1,0:T(8,128)S(1)} %get-tuple-element.81), channel_id=1, source_target_pairs={{4,8},{8,4},{12,16},{16,12},{20,24},{24,20},{28,32},{32,28},{36,40... | collective-permute-start | bytes 294920 | tf_op jit(solution)/shard_map/ppermute | solution.py:713
  30.7 0.1 collective-permute-start.8
  30.8 2.2 %collective-permute-done.9.x1 = f32[192,128]{1,0:T(8,128)S(1)} collective-permute-done((f32[192,128]{1,0:T(8,128)S(1)}, f32[192,128]{1,0:T(8,128)S(1)}, u32[]{:S(2)}, u32[]{:S(2)}) %collective-permute-start.9) | collective-permute-done | bytes 98336 | tf_op jit(solution)/shard_map/ppermute | solution.py:713
  33.0 0.0 collective-permute-start.10
  33.0 0.0 collective-permute-done.8.x0
  33.0 1.0 %level2.1 = (f32[16,48,128]{2,1,0:T(8,128)S(1)}, f32[16,48,128]{2,1,0:T(8,128)S(1)}, f32[16,48,128]{2,1,0:T(8,128)S(1)}, f32[16,48,128]{2,1,0:T(8,128)S(1)}, f32...) custom-call(f32[18,64,128]{2,1,0:T(8,128)S(1)} %get-tuple-element.74., ...), custom_call_target="tpu_custom_call" | custom-call | tf_op jit(solution)/shard_map/level2/pallas_call | solution.py:23
  34.0 0.3 collective-permute-done.10.far
  34.3 24.6 %all_to_all.11 = f32[128,4,128]{2,1,0:T(4,128)S(1)} all-to-all(f32[128,4,128]{2,1,0:T(4,128)S(1)} %bitcast.3), channel_id=1, replica_groups=mesh['gx'=32,'gy'=4] {'gx','gy'}, dimensions={0} | all-to-all | bytes 524288 | tf_op jit(solution)/shard_map/all_to_all | solution.py:762
  59.0 8.5 %up.1 = (f32[16,64,128]{2,1,0:T(8,128)}, f32[16,64,128]{2,1,0:T(8,128)}) custom-call(f32[512,128]{1,0:T(8,128)S(1)} %bitcast.2, f32[8,8,128]{2,1,0:T(8,128)S(1)} %collective-permute-done.6.y0, f32[8,8,128]{2,1,0:T(8,128)S(1)} %collective-permute-done.7.y1, f32[192,128]{1,0:T(8,128)S(1)} %collective-permute-done.9.x1, ...), custom_call_target="tpu_custom_call" | custom-call | tf_op jit(solution)/shard_map/up/pallas_call | solution.py:23
  (1 shorter events, 0.0 us)
Async XLA Ops:
  2.2 7.0 %collective-permute-start.2 = (f32[32,8,128]{2,1,0:T(8,128)S(1)}, f32[32,8,128]{2,1,0:T(8,128)S(1)}, u32[]{:S(2)}, u32[]{:S(2)}) collective-permute-start(f32[32,8,128]{2,1,0:T(8,128)S(1)} %get-tuple-element.56), channel_id=1, source_target_pairs={{0,1},{1,0},{2,3},{3,2},{4,5},{5,4},{6,7},{7,6},{8,9},{9,8},{10,11... | collective-permute-start | bytes 393224 | tf_op jit(solution)/shard_map/ppermute | solution.py:714
  4.4 4.9 %collective-permute-start.3 = (f32[32,8,128]{2,1,0:T(8,128)S(1)}, f32[32,8,128]{2,1,0:T(8,128)S(1)}, u32[]{:S(2)}, u32[]{:S(2)}) collective-permute-start(f32[32,8,128]{2,1,0:T(8,128)S(1)} %get-tuple-element.57), channel_id=1, source_target_pairs={{1,2},{2,1},{5,6},{6,5},{9,10},{10,9},{13,14},{14,13},{17,18},{18,... | collective-permute-start | bytes 393224 | tf_op jit(solution)/shard_map/ppermute | solution.py:713
  5.1 10.7 %collective-permute-start.1 = (f32[14,64,128]{2,1,0:T(8,128)S(1)}, f32[14,64,128]{2,1,0:T(8,128)S(1)}, u32[]{:S(2)}, u32[]{:S(2)}) collective-permute-start(f32[14,64,128]{2,1,0:T(8,128)S(1)} %get-tuple-element.55), channel_id=1, source_target_pairs={{4,8},{8,4},{12,16},{16,12},{20,24},{24,20},{28,32},{32,28},{36,40... | collective-permute-start | bytes 1376264 | tf_op jit(solution)/shard_map/ppermute | solution.py:713
  9.2 6.7 %collective-permute-start = (f32[21,64,128]{2,1,0:T(8,128)S(1)}, f32[21,64,128]{2,1,0:T(8,128)S(1)}, u32[]{:S(2)}, u32[]{:S(2)}) collective-permute-start(f32[21,64,128]{2,1,0:T(8,128)S(1)} %get-tuple-element.54), channel_id=1, source_target_pairs={{0,4},{4,0},{8,12},{12,8},{16,20},{20,16},{24,28},{28,24},{32,36},... | collective-permute-start | bytes 2064392 | tf_op jit(solution)/shard_map/ppermute | solution.py:714
  9.3 6.5 %collective-permute-start.5 = (f32[6,16,128]{2,1,0:T(8,128)S(1)}, f32[6,16,128]{2,1,0:T(8,128)S(1)}, u32[]{:S(2)}, u32[]{:S(2)}) collective-permute-start(f32[6,16,128]{2,1,0:T(8,128)S(1)} %get-tuple-element.59), channel_id=1, source_target_pairs={{4,8},{8,4},{12,16},{16,12},{20,24},{24,20},{28,32},{32,28},{36,40... | collective-permute-start | bytes 147464 | tf_op jit(solution)/shard_map/ppermute | solution.py:713
  12.9 3.0 %collective-permute-start.4 = (f32[13,16,128]{2,1,0:T(8,128)S(1)}, f32[13,16,128]{2,1,0:T(8,128)S(1)}, u32[]{:S(2)}, u32[]{:S(2)}) collective-permute-start(f32[13,16,128]{2,1,0:T(8,128)S(1)} %get-tuple-element.58), channel_id=1, source_target_pairs={{0,4},{4,0},{8,12},{12,8},{16,20},{20,16},{24,28},{28,24},{32,36},... | collective-permute-start | bytes 319496 | tf_op jit(solution)/shard_map/ppermute | solution.py:714
  21.0 5.6 %collective-permute-start.6 = (f32[8,8,128]{2,1,0:T(8,128)S(1)}, f32[8,8,128]{2,1,0:T(8,128)S(1)}, u32[]{:S(2)}, u32[]{:S(2)}) collective-permute-start(f32[8,8,128]{2,1,0:T(8,128)S(1)} %get-tuple-element.77), channel_id=1, source_target_pairs={{0,1},{1,0},{2,3},{3,2},{4,5},{5,4},{6,7},{7,6},{8,9},{9,8},{10,11... | collective-permute-start | bytes 98312 | tf_op jit(solution)/shard_map/ppermute | solution.py:714
  24.7 1.9 %collective-permute-start.7 = (f32[8,8,128]{2,1,0:T(8,128)S(1)}, f32[8,8,128]{2,1,0:T(8,128)S(1)}, u32[]{:S(2)}, u32[]{:S(2)}) collective-permute-start(f32[8,8,128]{2,1,0:T(8,128)S(1)} %get-tuple-element.78), channel_id=1, source_target_pairs={{1,2},{2,1},{5,6},{6,5},{9,10},{10,9},{13,14},{14,13},{17,18},{18,... | collective-permute-start | bytes 98312 | tf_op jit(solution)/shard_map/ppermute | solution.py:713
  26.8 6.2 %collective-permute-start.9 = (f32[192,128]{1,0:T(8,128)S(1)}, f32[192,128]{1,0:T(8,128)S(1)}, u32[]{:S(2)}, u32[]{:S(2)}) collective-permute-start(f32[192,128]{1,0:T(8,128)S(1)} %get-tuple-element.81), channel_id=1, source_target_pairs={{4,8},{8,4},{12,16},{16,12},{20,24},{24,20},{28,32},{32,28},{36,40... | collective-permute-start | bytes 294920 | tf_op jit(solution)/shard_map/ppermute | solution.py:713
  30.7 2.3 %collective-permute-start.8 = (f32[192,128]{1,0:T(8,128)S(1)}, f32[192,128]{1,0:T(8,128)S(1)}, u32[]{:S(2)}, u32[]{:S(2)}) collective-permute-start(f32[192,128]{1,0:T(8,128)S(1)} %get-tuple-element.80), channel_id=1, source_target_pairs={{0,4},{4,0},{8,12},{12,8},{16,20},{20,16},{24,28},{28,24},{32,36},... | collective-permute-start | bytes 294920 | tf_op jit(solution)/shard_map/ppermute | solution.py:714
  33.0 1.3 %collective-permute-start.10 = (f32[192,128]{1,0:T(8,128)S(1)}, f32[192,128]{1,0:T(8,128)S(1)}, u32[]{:S(2)}, u32[]{:S(2)}) collective-permute-start(f32[192,128]{1,0:T(8,128)S(1)} %collective-permute-done.9.x1), channel_id=1, source_target_pairs={{0,4},{4,0},{8,12},{12,8},{16,20},{20,16},{24,28},{28,24},{32,36},... | collective-permute-start | bytes 294920 | tf_op jit(solution)/shard_map/ppermute | solution.py:712

commit v8 on v7

--- a/solution.py
+++ b/solution.py
@@ -190,7 +190,7 @@
     return lax.axis_index(axis) % 2
 
 
-PARTS = 4
+PARTS = 2
 
 
 def stored(x):
@@ -283,7 +283,7 @@
 
 def levels_down(c, b, fx, fy, fz, w, c1, b1, gx_, gy_, gz_, gw_):
     top = Level(0, c, b, fx, fy, fz, w, 8, 88)
-    return top, Level(1, c1, b1, gx_, gy_, gz_, gw_, 8, 56)
+    return top, Level(1, c1, b1, gx_, gy_, gz_, gw_, 12, 52)
 
 
 def inner_kernel(cond, source, y0, y1, c, b, fx, fy, fz, w, ua, ub, c1, b1, gx_, gy_, gz_, gw_, tmp):
@@ -436,13 +436,16 @@
     return jnp.where(f(i, j), 1.0, 0.0).astype(F32)
 
 
-def exact_dot(a, b):
-    return jnp.dot(a, b, precision=lax.Precision.HIGHEST, preferred_element_type=F32)
-
-
 def halves(v):
     high = v.astype(jnp.bfloat16)
     return high, (v - high.astype(F32)).astype(jnp.bfloat16)
+
+
+def pick_dot(a, b):
+    a1, rest = halves(a)[0], a - halves(a)[0].astype(F32)
+    a2, a3 = halves(rest)
+    b = b.astype(jnp.bfloat16)
+    return jnp.dot(jnp.concatenate([a1, a2, a3], 1), jnp.concatenate([b, b, b], 0), preferred_element_type=F32)
 
 
 def split_dot(a, b):
@@ -482,7 +485,7 @@
     both = jnp.concatenate(
         [b3[0, pl.ds(16, 8), :], b3[1, pl.ds(16, 8), :], c3[0, pl.ds(16, 8), :], c3[1, pl.ds(16, 8), :]], 0
     )
-    spread = exact_dot(both, one_hot((NZ, NZ), lambda i, j: i == 8 * (j % 16)))
+    spread = pick_dot(both, one_hot((NZ, NZ), lambda i, j: i == 8 * (j % 16)))
     shape = (8, NZ)
     mine = lane(shape) // 16 == lax.broadcasted_iota(jnp.int32, shape, 0)
     packed = [
@@ -616,7 +619,7 @@
 ):
     ix, iy = lax.axis_index("gx"), lax.axis_index("gy")
     ox, oy = ix % 2, iy % 2
-    low = Level(2, None, b2, hx, hy, hz, hw, 8, 40)
+    low = Level(2, None, b2, hx, hy, hz, hw, 12, 36)
     wide = pl.ds(8, 32)
     low.start(ha, X2 + 6, X2 + 8)
     ha[X2 + 8, pl.ds(10, 28), :] = hw[X2 + 8, pl.ds(10, 28), :] * unpack_lanes(far[pl.ds(108, 28), :], 4)[2]
@@ -644,7 +647,7 @@
         for g in range(3):
             row = s3[iy + g, pl.ds(2 * ix + 6 + 5 * ox + (1 - 2 * ox) * k, 1), :]
             tiles.append(jnp.where(mine, jnp.broadcast_to(row, shape), 0.0))
-    spread = exact_dot(jnp.concatenate(tiles, 0), one_hot((NZ, NZ), lambda i, j: i % 16 == j // 8))
+    spread = pick_dot(jnp.concatenate(tiles, 0), one_hot((NZ, NZ), lambda i, j: i % 16 == j // 8))
     for k in range(6):
         t = spread[24 * k : 24 * k + 24]
         e2[k, pl.ds(0, 24, stride=2), :] = t
@@ -675,7 +678,7 @@
             ga_[1 + 2 * k + j] = u1[1 + 2 * k + j] + e1[k]
 
     rows(0, 8, add1)
-    mid = Level(1, None, b1, gx_, gy_, gz_, gw_, 8, 56)
+    mid = Level(1, None, b1, gx_, gy_, gz_, gw_, 12, 52)
     mid.sweep(ga_, gb_, 2, 16)
     mid.sweep(gb_, ga_, 3, 15)
 
@@ -690,7 +693,7 @@
 
     rows(0, 12, grow0, 4)
     rows(0, 12, add0, 4)
-    top = Level(0, None, b, fx, fy, fz, w, 8, 88)
+    top = Level(0, None, b, fx, fy, fz, w, 12, 84)
     top.sweep(ua, ub, 7, 27)
     top.sweep(ub, ua, 8, 26)
 

time: 67.7 us -> 67.3 us (level)
  no operation moved by 1% of the time
where the time goes in v8:
time: 67.3 us; the launch traced here: 67.1 us
  blocking collectives  24.6 us (37%)
  starting transfers between devices  18.9 us (28%)
  Pallas kernels  18.3 us (27%)
  waiting for transfers between devices  4.51 us (7%)
  between operations  0.77 us (1%)
    all_to_all x1, blocking collectives, per_device(): whole = lax.all_to_all(packed, ('gx', 'gy'), 0, 0, tiled=True)  24.6 us
    pallas_call x8, Pallas kernels, call(): pl.pallas_call(body, out_shape=[jax.ShapeDtypeStruct(s, F32) for s in out...  18.3 us
    ppermute x5, starting transfers between devices, swaps(): late = lax.ppermute(second, axis, pairs(1))  12.8 us
    ppermute x5, starting transfers between devices, swaps(): return (lax.ppermute(first, axis, pairs(0)), late)  6.1 us
    ppermute x5, waiting for transfers between devices, swaps(): late = lax.ppermute(second, axis, pairs(1))  2.87 us
  transfers between devices with their start and end apart: 11, of which 4 were waited for; matrix products, arithmetic and copies ran while one was open for 0% of the time, Pallas kernels for 5%

profile of v8, /device:TPU:1, one launch (start us, length us, event | category | flops | bytes accessed | tf_op | source)
XLA Modules:
  0.0 67.1 jit_solution(6830903630438373885)
XLA Ops:
  0.6 1.5 %begin.1 = (f32[16,64,128]{2,1,0:T(8,128)S(1)}, f32[16,64,128]{2,1,0:T(8,128)S(1)}, f32[32,8,128]{2,1,0:T(8,128)S(1)}, f32[32,8,128]{2,1,0:T(8,128)S(1)}) custom-call(f32[16,64,128]{2,1,0:T(8,128)} %source.1, f32[16,64,128]{2,1,0:T(8,128)} %density.1, f32[16,64,128]{2,1,0:T(8,128)} %drag.1, s32[64]{0:T(128)} %porous.1), custom_call_target="tpu_custom_call" | custom-call | tf_op jit(solution)/shard_map/begin/pallas_call | solution.py:23
  2.1 2.1 %collective-permute-start.2 = (f32[32,8,128]{2,1,0:T(8,128)S(1)}, f32[32,8,128]{2,1,0:T(8,128)S(1)}, u32[]{:S(2)}, u32[]{:S(2)}) collective-permute-start(f32[32,8,128]{2,1,0:T(8,128)S(1)} %get-tuple-element.56), channel_id=1, source_target_pairs={{0,1},{1,0},{2,3},{3,2},{4,5},{5,4},{6,7},{7,6},{8,9},{9,8},{10,11... | collective-permute-start | bytes 393224 | tf_op jit(solution)/shard_map/ppermute | solution.py:717
  4.3 0.7 collective-permute-start.3
  4.9 0.1 edges.1
  5.0 4.0 %collective-permute-start.1 = (f32[14,64,128]{2,1,0:T(8,128)S(1)}, f32[14,64,128]{2,1,0:T(8,128)S(1)}, u32[]{:S(2)}, u32[]{:S(2)}) collective-permute-start(f32[14,64,128]{2,1,0:T(8,128)S(1)} %get-tuple-element.55), channel_id=1, source_target_pairs={{4,8},{8,4},{12,16},{16,12},{20,24},{24,20},{28,32},{32,28},{36,40... | collective-permute-start | bytes 1376264 | tf_op jit(solution)/shard_map/ppermute | solution.py:716
  9.1 0.1 collective-permute-start
  9.2 0.0 collective-permute-done.2.y0
  9.2 0.0 collective-permute-done.3.y1
  9.2 3.6 %collective-permute-start.5 = (f32[6,16,128]{2,1,0:T(8,128)S(1)}, f32[6,16,128]{2,1,0:T(8,128)S(1)}, u32[]{:S(2)}, u32[]{:S(2)}) collective-permute-start(f32[6,16,128]{2,1,0:T(8,128)S(1)} %get-tuple-element.59), channel_id=1, source_target_pairs={{4,8},{8,4},{12,16},{16,12},{20,24},{24,20},{28,32},{32,28},{36,40... | collective-permute-start | bytes 147464 | tf_op jit(solution)/shard_map/ppermute | solution.py:716
  12.8 0.1 collective-permute-start.4
  12.9 2.2 %inner.1 = (f32[18,96,128]{2,1,0:T(8,128)S(1)}, f32[18,96,128]{2,1,0:T(8,128)S(1)}, f32[18,96,128]{2,1,0:T(8,128)S(1)}, f32[18,96,128]{2,1,0:T(8,128)S(1)}, f32[...) custom-call(f32[16,64,128]{2,1,0:T(8,128)S(1)} %get-tuple-element.52, ...), custom_call_target="tpu_custom_call" | custom-call | flops 10000000000 | tf_op jit(solution)/shard_map/inner/pallas_call | solution.py:23
  15.1 0.7 %collective-permute-done.5.k1 = f32[6,16,128]{2,1,0:T(8,128)S(1)} collective-permute-done((f32[6,16,128]{2,1,0:T(8,128)S(1)}, f32[6,16,128]{2,1,0:T(8,128)S(1)}, u32[]{:S(2)}, u32[]{:S(2)}) %collective-permute-start.5) | collective-permute-done | bytes 49184 | tf_op jit(solution)/shard_map/ppermute | solution.py:716
  15.7 0.0 collective-permute-done.4.k0
  15.7 0.0 collective-permute-done.1.x1
  15.7 0.0 collective-permute-done.x0
  15.8 5.1 %down.1 = (f32[36,96,128]{2,1,0:T(8,128)S(1)}, f32[36,96,128]{2,1,0:T(8,128)S(1)}, f32[36,96,128]{2,1,0:T(8,128)S(1)}, f32[36,96,128]{2,1,0:T(8,128)S(1)}, f32[3...) custom-call(f32[21,64,128]{2,1,0:T(8,128)S(1)} %collective-permute-d, ...), custom_call_target="tpu_custom_call" | custom-call | tf_op jit(solution)/shard_map/down/pallas_call | solution.py:23
  20.8 3.7 %collective-permute-start.6 = (f32[8,8,128]{2,1,0:T(8,128)S(1)}, f32[8,8,128]{2,1,0:T(8,128)S(1)}, u32[]{:S(2)}, u32[]{:S(2)}) collective-permute-start(f32[8,8,128]{2,1,0:T(8,128)S(1)} %get-tuple-element.77), channel_id=1, source_target_pairs={{0,1},{1,0},{2,3},{3,2},{4,5},{5,4},{6,7},{7,6},{8,9},{9,8},{10,11... | collective-permute-start | bytes 98312 | tf_op jit(solution)/shard_map/ppermute | solution.py:717
  24.6 0.7 collective-permute-start.7
  25.2 1.3 %collective-permute-done.6.y0 = f32[8,8,128]{2,1,0:T(8,128)S(1)} collective-permute-done((f32[8,8,128]{2,1,0:T(8,128)S(1)}, f32[8,8,128]{2,1,0:T(8,128)S(1)}, u32[]{:S(2)}, u32[]{:S(2)}) %collective-permute-start.6) | collective-permute-done | bytes 32800 | tf_op jit(solution)/shard_map/ppermute | solution.py:717
  26.5 0.0 collective-permute-done.7.y1
  26.5 0.2 edges2.1
  26.7 3.9 %collective-permute-start.9 = (f32[192,128]{1,0:T(8,128)S(1)}, f32[192,128]{1,0:T(8,128)S(1)}, u32[]{:S(2)}, u32[]{:S(2)}) collective-permute-start(f32[192,128]{1,0:T(8,128)S(1)} %get-tuple-element.81), channel_id=1, source_target_pairs={{4,8},{8,4},{12,16},{16,12},{20,24},{24,20},{28,32},{32,28},{36,40... | collective-permute-start | bytes 294920 | tf_op jit(solution)/shard_map/ppermute | solution.py:716
  30.6 0.1 collective-permute-start.8
  30.7 2.2 %collective-permute-done.9.x1 = f32[192,128]{1,0:T(8,128)S(1)} collective-permute-done((f32[192,128]{1,0:T(8,128)S(1)}, f32[192,128]{1,0:T(8,128)S(1)}, u32[]{:S(2)}, u32[]{:S(2)}) %collective-permute-start.9) | collective-permute-done | bytes 98336 | tf_op jit(solution)/shard_map/ppermute | solution.py:716
  32.9 0.0 collective-permute-start.10
  32.9 0.0 collective-permute-done.8.x0
  32.9 0.9 %level2.1 = (f32[16,48,128]{2,1,0:T(8,128)S(1)}, f32[16,48,128]{2,1,0:T(8,128)S(1)}, f32[16,48,128]{2,1,0:T(8,128)S(1)}, f32[16,48,128]{2,1,0:T(8,128)S(1)}, f32...) custom-call(f32[18,64,128]{2,1,0:T(8,128)S(1)} %get-tuple-element.74., ...), custom_call_target="tpu_custom_call" | custom-call | tf_op jit(solution)/shard_map/level2/pallas_call | solution.py:23
  33.8 0.3 collective-permute-done.10.far
  34.2 24.6 %all_to_all.11 = f32[128,4,128]{2,1,0:T(4,128)S(1)} all-to-all(f32[128,4,128]{2,1,0:T(4,128)S(1)} %bitcast.3), channel_id=1, replica_groups=mesh['gx'=32,'gy'=4] {'gx','gy'}, dimensions={0} | all-to-all | bytes 524288 | tf_op jit(solution)/shard_map/all_to_all | solution.py:765
  58.8 8.3 %up.1 = (f32[16,64,128]{2,1,0:T(8,128)}, f32[16,64,128]{2,1,0:T(8,128)}) custom-call(f32[512,128]{1,0:T(8,128)S(1)} %bitcast.2, f32[8,8,128]{2,1,0:T(8,128)S(1)} %collective-permute-done.6.y0, f32[8,8,128]{2,1,0:T(8,128)S(1)} %collective-permute-done.7.y1, f32[192,128]{1,0:T(8,128)S(1)} %collective-permute-done.9.x1, ...), custom_call_target="tpu_custom_call" | custom-call | tf_op jit(solution)/shard_map/up/pallas_call | solution.py:23
  (1 shorter events, 0.0 us)
Async XLA Ops:
  2.1 7.0 %collective-permute-start.2 = (f32[32,8,128]{2,1,0:T(8,128)S(1)}, f32[32,8,128]{2,1,0:T(8,128)S(1)}, u32[]{:S(2)}, u32[]{:S(2)}) collective-permute-start(f32[32,8,128]{2,1,0:T(8,128)S(1)} %get-tuple-element.56), channel_id=1, source_target_pairs={{0,1},{1,0},{2,3},{3,2},{4,5},{5,4},{6,7},{7,6},{8,9},{9,8},{10,11... | collective-permute-start | bytes 393224 | tf_op jit(solution)/shard_map/ppermute | solution.py:717
  4.3 4.9 %collective-permute-start.3 = (f32[32,8,128]{2,1,0:T(8,128)S(1)}, f32[32,8,128]{2,1,0:T(8,128)S(1)}, u32[]{:S(2)}, u32[]{:S(2)}) collective-permute-start(f32[32,8,128]{2,1,0:T(8,128)S(1)} %get-tuple-element.57), channel_id=1, source_target_pairs={{1,2},{2,1},{5,6},{6,5},{9,10},{10,9},{13,14},{14,13},{17,18},{18,... | collective-permute-start | bytes 393224 | tf_op jit(solution)/shard_map/ppermute | solution.py:716
  5.0 10.7 %collective-permute-start.1 = (f32[14,64,128]{2,1,0:T(8,128)S(1)}, f32[14,64,128]{2,1,0:T(8,128)S(1)}, u32[]{:S(2)}, u32[]{:S(2)}) collective-permute-start(f32[14,64,128]{2,1,0:T(8,128)S(1)} %get-tuple-element.55), channel_id=1, source_target_pairs={{4,8},{8,4},{12,16},{16,12},{20,24},{24,20},{28,32},{32,28},{36,40... | collective-permute-start | bytes 1376264 | tf_op jit(solution)/shard_map/ppermute | solution.py:716
  9.1 6.7 %collective-permute-start = (f32[21,64,128]{2,1,0:T(8,128)S(1)}, f32[21,64,128]{2,1,0:T(8,128)S(1)}, u32[]{:S(2)}, u32[]{:S(2)}) collective-permute-start(f32[21,64,128]{2,1,0:T(8,128)S(1)} %get-tuple-element.54), channel_id=1, source_target_pairs={{0,4},{4,0},{8,12},{12,8},{16,20},{20,16},{24,28},{28,24},{32,36},... | collective-permute-start | bytes 2064392 | tf_op jit(solution)/shard_map/ppermute | solution.py:717
  9.2 6.5 %collective-permute-start.5 = (f32[6,16,128]{2,1,0:T(8,128)S(1)}, f32[6,16,128]{2,1,0:T(8,128)S(1)}, u32[]{:S(2)}, u32[]{:S(2)}) collective-permute-start(f32[6,16,128]{2,1,0:T(8,128)S(1)} %get-tuple-element.59), channel_id=1, source_target_pairs={{4,8},{8,4},{12,16},{16,12},{20,24},{24,20},{28,32},{32,28},{36,40... | collective-permute-start | bytes 147464 | tf_op jit(solution)/shard_map/ppermute | solution.py:716
  12.8 3.0 %collective-permute-start.4 = (f32[13,16,128]{2,1,0:T(8,128)S(1)}, f32[13,16,128]{2,1,0:T(8,128)S(1)}, u32[]{:S(2)}, u32[]{:S(2)}) collective-permute-start(f32[13,16,128]{2,1,0:T(8,128)S(1)} %get-tuple-element.58), channel_id=1, source_target_pairs={{0,4},{4,0},{8,12},{12,8},{16,20},{20,16},{24,28},{28,24},{32,36},... | collective-permute-start | bytes 319496 | tf_op jit(solution)/shard_map/ppermute | solution.py:717
  20.8 5.7 %collective-permute-start.6 = (f32[8,8,128]{2,1,0:T(8,128)S(1)}, f32[8,8,128]{2,1,0:T(8,128)S(1)}, u32[]{:S(2)}, u32[]{:S(2)}) collective-permute-start(f32[8,8,128]{2,1,0:T(8,128)S(1)} %get-tuple-element.77), channel_id=1, source_target_pairs={{0,1},{1,0},{2,3},{3,2},{4,5},{5,4},{6,7},{7,6},{8,9},{9,8},{10,11... | collective-permute-start | bytes 98312 | tf_op jit(solution)/shard_map/ppermute | solution.py:717
  24.6 1.9 %collective-permute-start.7 = (f32[8,8,128]{2,1,0:T(8,128)S(1)}, f32[8,8,128]{2,1,0:T(8,128)S(1)}, u32[]{:S(2)}, u32[]{:S(2)}) collective-permute-start(f32[8,8,128]{2,1,0:T(8,128)S(1)} %get-tuple-element.78), channel_id=1, source_target_pairs={{1,2},{2,1},{5,6},{6,5},{9,10},{10,9},{13,14},{14,13},{17,18},{18,... | collective-permute-start | bytes 98312 | tf_op jit(solution)/shard_map/ppermute | solution.py:716
  26.7 6.2 %collective-permute-start.9 = (f32[192,128]{1,0:T(8,128)S(1)}, f32[192,128]{1,0:T(8,128)S(1)}, u32[]{:S(2)}, u32[]{:S(2)}) collective-permute-start(f32[192,128]{1,0:T(8,128)S(1)} %get-tuple-element.81), channel_id=1, source_target_pairs={{4,8},{8,4},{12,16},{16,12},{20,24},{24,20},{28,32},{32,28},{36,40... | collective-permute-start | bytes 294920 | tf_op jit(solution)/shard_map/ppermute | solution.py:716
  30.6 2.3 %collective-permute-start.8 = (f32[192,128]{1,0:T(8,128)S(1)}, f32[192,128]{1,0:T(8,128)S(1)}, u32[]{:S(2)}, u32[]{:S(2)}) collective-permute-start(f32[192,128]{1,0:T(8,128)S(1)} %get-tuple-element.80), channel_id=1, source_target_pairs={{0,4},{4,0},{8,12},{12,8},{16,20},{20,16},{24,28},{28,24},{32,36},... | collective-permute-start | bytes 294920 | tf_op jit(solution)/shard_map/ppermute | solution.py:717
  32.9 1.3 %collective-permute-start.10 = (f32[192,128]{1,0:T(8,128)S(1)}, f32[192,128]{1,0:T(8,128)S(1)}, u32[]{:S(2)}, u32[]{:S(2)}) collective-permute-start(f32[192,128]{1,0:T(8,128)S(1)} %collective-permute-done.9.x1), channel_id=1, source_target_pairs={{0,4},{4,0},{8,12},{12,8},{16,20},{20,16},{24,28},{28,24},{32,36},... | collective-permute-start | bytes 294920 | tf_op jit(solution)/shard_map/ppermute | solution.py:715

commit v9 on v8

--- a/solution.py
+++ b/solution.py
@@ -766,7 +766,7 @@
     out, res = call(
         up_kernel,
         [block] * 2,
-        [(6, 80, NZ), (6, 48, NZ), (8, 64, NZ), (12, 96, NZ)] + [two] * 2 + [one] * 3 + [zero] * 2,
+        [(6, 88, NZ), (6, 48, NZ), (8, 64, NZ), (12, 96, NZ)] + [two] * 2 + [one] * 3 + [zero] * 2,
         (whole, y0, y1, x1, far, *level2, *level1[:5], u1, *level0),
         "up",
         24,

time: 67.3 us -> 67.1 us (level)
  no operation moved by 1% of the time
where the time goes in v9:
time: 67.1 us; the launch traced here: 66.9 us
  blocking collectives  24.6 us (37%)
  starting transfers between devices  18.9 us (28%)
  Pallas kernels  18.1 us (27%)
  waiting for transfers between devices  4.51 us (7%)
  between operations  0.77 us (1%)
    all_to_all x1, blocking collectives, per_device(): whole = lax.all_to_all(packed, ('gx', 'gy'), 0, 0, tiled=True)  24.6 us
    pallas_call x8, Pallas kernels, call(): pl.pallas_call(body, out_shape=[jax.ShapeDtypeStruct(s, F32) for s in out...  18.1 us
    ppermute x5, starting transfers between devices, swaps(): late = lax.ppermute(second, axis, pairs(1))  12.8 us
    ppermute x5, starting transfers between devices, swaps(): return (lax.ppermute(first, axis, pairs(0)), late)  6.1 us
    ppermute x5, waiting for transfers between devices, swaps(): late = lax.ppermute(second, axis, pairs(1))  2.87 us
  transfers between devices with their start and end apart: 11, of which 4 were waited for; matrix products, arithmetic and copies ran while one was open for 0% of the time, Pallas kernels for 5%

profile of v9, /device:TPU:1, one launch (start us, length us, event | category | flops | bytes accessed | tf_op | source)
XLA Modules:
  0.0 66.9 jit_solution(12601982759907304419)
XLA Ops:
  0.6 1.5 %begin.1 = (f32[16,64,128]{2,1,0:T(8,128)S(1)}, f32[16,64,128]{2,1,0:T(8,128)S(1)}, f32[32,8,128]{2,1,0:T(8,128)S(1)}, f32[32,8,128]{2,1,0:T(8,128)S(1)}) custom-call(f32[16,64,128]{2,1,0:T(8,128)} %source.1, f32[16,64,128]{2,1,0:T(8,128)} %density.1, f32[16,64,128]{2,1,0:T(8,128)} %drag.1, s32[64]{0:T(128)} %porous.1), custom_call_target="tpu_custom_call" | custom-call | tf_op jit(solution)/shard_map/begin/pallas_call | solution.py:23
  2.1 2.1 %collective-permute-start.2 = (f32[32,8,128]{2,1,0:T(8,128)S(1)}, f32[32,8,128]{2,1,0:T(8,128)S(1)}, u32[]{:S(2)}, u32[]{:S(2)}) collective-permute-start(f32[32,8,128]{2,1,0:T(8,128)S(1)} %get-tuple-element.56), channel_id=1, source_target_pairs={{0,1},{1,0},{2,3},{3,2},{4,5},{5,4},{6,7},{7,6},{8,9},{9,8},{10,11... | collective-permute-start | bytes 393224 | tf_op jit(solution)/shard_map/ppermute | solution.py:717
  4.3 0.7 collective-permute-start.3
  4.9 0.1 edges.1
  5.0 4.0 %collective-permute-start.1 = (f32[14,64,128]{2,1,0:T(8,128)S(1)}, f32[14,64,128]{2,1,0:T(8,128)S(1)}, u32[]{:S(2)}, u32[]{:S(2)}) collective-permute-start(f32[14,64,128]{2,1,0:T(8,128)S(1)} %get-tuple-element.55), channel_id=1, source_target_pairs={{4,8},{8,4},{12,16},{16,12},{20,24},{24,20},{28,32},{32,28},{36,40... | collective-permute-start | bytes 1376264 | tf_op jit(solution)/shard_map/ppermute | solution.py:716
  9.1 0.1 collective-permute-start
  9.2 0.0 collective-permute-done.2.y0
  9.2 0.0 collective-permute-done.3.y1
  9.2 3.6 %collective-permute-start.5 = (f32[6,16,128]{2,1,0:T(8,128)S(1)}, f32[6,16,128]{2,1,0:T(8,128)S(1)}, u32[]{:S(2)}, u32[]{:S(2)}) collective-permute-start(f32[6,16,128]{2,1,0:T(8,128)S(1)} %get-tuple-element.59), channel_id=1, source_target_pairs={{4,8},{8,4},{12,16},{16,12},{20,24},{24,20},{28,32},{32,28},{36,40... | collective-permute-start | bytes 147464 | tf_op jit(solution)/shard_map/ppermute | solution.py:716
  12.8 0.1 collective-permute-start.4
  12.9 2.2 %inner.1 = (f32[18,96,128]{2,1,0:T(8,128)S(1)}, f32[18,96,128]{2,1,0:T(8,128)S(1)}, f32[18,96,128]{2,1,0:T(8,128)S(1)}, f32[18,96,128]{2,1,0:T(8,128)S(1)}, f32[...) custom-call(f32[16,64,128]{2,1,0:T(8,128)S(1)} %get-tuple-element.52, ...), custom_call_target="tpu_custom_call" | custom-call | flops 10000000000 | tf_op jit(solution)/shard_map/inner/pallas_call | solution.py:23
  15.1 0.7 %collective-permute-done.5.k1 = f32[6,16,128]{2,1,0:T(8,128)S(1)} collective-permute-done((f32[6,16,128]{2,1,0:T(8,128)S(1)}, f32[6,16,128]{2,1,0:T(8,128)S(1)}, u32[]{:S(2)}, u32[]{:S(2)}) %collective-permute-start.5) | collective-permute-done | bytes 49184 | tf_op jit(solution)/shard_map/ppermute | solution.py:716
  15.7 0.0 collective-permute-done.4.k0
  15.7 0.0 collective-permute-done.1.x1
  15.7 0.0 collective-permute-done.x0
  15.8 5.1 %down.1 = (f32[36,96,128]{2,1,0:T(8,128)S(1)}, f32[36,96,128]{2,1,0:T(8,128)S(1)}, f32[36,96,128]{2,1,0:T(8,128)S(1)}, f32[36,96,128]{2,1,0:T(8,128)S(1)}, f32[3...) custom-call(f32[21,64,128]{2,1,0:T(8,128)S(1)} %collective-permute-d, ...), custom_call_target="tpu_custom_call" | custom-call | tf_op jit(solution)/shard_map/down/pallas_call | solution.py:23
  20.8 3.7 %collective-permute-start.6 = (f32[8,8,128]{2,1,0:T(8,128)S(1)}, f32[8,8,128]{2,1,0:T(8,128)S(1)}, u32[]{:S(2)}, u32[]{:S(2)}) collective-permute-start(f32[8,8,128]{2,1,0:T(8,128)S(1)} %get-tuple-element.77), channel_id=1, source_target_pairs={{0,1},{1,0},{2,3},{3,2},{4,5},{5,4},{6,7},{7,6},{8,9},{9,8},{10,11... | collective-permute-start | bytes 98312 | tf_op jit(solution)/shard_map/ppermute | solution.py:717
  24.6 0.7 collective-permute-start.7
  25.2 1.3 %collective-permute-done.6.y0 = f32[8,8,128]{2,1,0:T(8,128)S(1)} collective-permute-done((f32[8,8,128]{2,1,0:T(8,128)S(1)}, f32[8,8,128]{2,1,0:T(8,128)S(1)}, u32[]{:S(2)}, u32[]{:S(2)}) %collective-permute-start.6) | collective-permute-done | bytes 32800 | tf_op jit(solution)/shard_map/ppermute | solution.py:717
  26.5 0.0 collective-permute-done.7.y1
  26.5 0.2 edges2.1
  26.7 3.9 %collective-permute-start.9 = (f32[192,128]{1,0:T(8,128)S(1)}, f32[192,128]{1,0:T(8,128)S(1)}, u32[]{:S(2)}, u32[]{:S(2)}) collective-permute-start(f32[192,128]{1,0:T(8,128)S(1)} %get-tuple-element.81), channel_id=1, source_target_pairs={{4,8},{8,4},{12,16},{16,12},{20,24},{24,20},{28,32},{32,28},{36,40... | collective-permute-start | bytes 294920 | tf_op jit(solution)/shard_map/ppermute | solution.py:716
  30.6 0.1 collective-permute-start.8
  30.7 2.2 %collective-permute-done.9.x1 = f32[192,128]{1,0:T(8,128)S(1)} collective-permute-done((f32[192,128]{1,0:T(8,128)S(1)}, f32[192,128]{1,0:T(8,128)S(1)}, u32[]{:S(2)}, u32[]{:S(2)}) %collective-permute-start.9) | collective-permute-done | bytes 98336 | tf_op jit(solution)/shard_map/ppermute | solution.py:716
  32.9 0.0 collective-permute-start.10
  32.9 0.0 collective-permute-done.8.x0
  32.9 0.9 %level2.1 = (f32[16,48,128]{2,1,0:T(8,128)S(1)}, f32[16,48,128]{2,1,0:T(8,128)S(1)}, f32[16,48,128]{2,1,0:T(8,128)S(1)}, f32[16,48,128]{2,1,0:T(8,128)S(1)}, f32...) custom-call(f32[18,64,128]{2,1,0:T(8,128)S(1)} %get-tuple-element.74., ...), custom_call_target="tpu_custom_call" | custom-call | tf_op jit(solution)/shard_map/level2/pallas_call | solution.py:23
  33.8 0.3 collective-permute-done.10.far
  34.2 24.6 %all_to_all.11 = f32[128,4,128]{2,1,0:T(4,128)S(1)} all-to-all(f32[128,4,128]{2,1,0:T(4,128)S(1)} %bitcast.3), channel_id=1, replica_groups=mesh['gx'=32,'gy'=4] {'gx','gy'}, dimensions={0} | all-to-all | bytes 524288 | tf_op jit(solution)/shard_map/all_to_all | solution.py:765
  58.8 8.1 %up.1 = (f32[16,64,128]{2,1,0:T(8,128)}, f32[16,64,128]{2,1,0:T(8,128)}) custom-call(f32[512,128]{1,0:T(8,128)S(1)} %bitcast.2, f32[8,8,128]{2,1,0:T(8,128)S(1)} %collective-permute-done.6.y0, f32[8,8,128]{2,1,0:T(8,128)S(1)} %collective-permute-done.7.y1, f32[192,128]{1,0:T(8,128)S(1)} %collective-permute-done.9.x1, ...), custom_call_target="tpu_custom_call" | custom-call | tf_op jit(solution)/shard_map/up/pallas_call | solution.py:23
  (1 shorter events, 0.0 us)
Async XLA Ops:
  2.1 7.0 %collective-permute-start.2 = (f32[32,8,128]{2,1,0:T(8,128)S(1)}, f32[32,8,128]{2,1,0:T(8,128)S(1)}, u32[]{:S(2)}, u32[]{:S(2)}) collective-permute-start(f32[32,8,128]{2,1,0:T(8,128)S(1)} %get-tuple-element.56), channel_id=1, source_target_pairs={{0,1},{1,0},{2,3},{3,2},{4,5},{5,4},{6,7},{7,6},{8,9},{9,8},{10,11... | collective-permute-start | bytes 393224 | tf_op jit(solution)/shard_map/ppermute | solution.py:717
  4.3 4.9 %collective-permute-start.3 = (f32[32,8,128]{2,1,0:T(8,128)S(1)}, f32[32,8,128]{2,1,0:T(8,128)S(1)}, u32[]{:S(2)}, u32[]{:S(2)}) collective-permute-start(f32[32,8,128]{2,1,0:T(8,128)S(1)} %get-tuple-element.57), channel_id=1, source_target_pairs={{1,2},{2,1},{5,6},{6,5},{9,10},{10,9},{13,14},{14,13},{17,18},{18,... | collective-permute-start | bytes 393224 | tf_op jit(solution)/shard_map/ppermute | solution.py:716
  5.0 10.7 %collective-permute-start.1 = (f32[14,64,128]{2,1,0:T(8,128)S(1)}, f32[14,64,128]{2,1,0:T(8,128)S(1)}, u32[]{:S(2)}, u32[]{:S(2)}) collective-permute-start(f32[14,64,128]{2,1,0:T(8,128)S(1)} %get-tuple-element.55), channel_id=1, source_target_pairs={{4,8},{8,4},{12,16},{16,12},{20,24},{24,20},{28,32},{32,28},{36,40... | collective-permute-start | bytes 1376264 | tf_op jit(solution)/shard_map/ppermute | solution.py:716
  9.1 6.7 %collective-permute-start = (f32[21,64,128]{2,1,0:T(8,128)S(1)}, f32[21,64,128]{2,1,0:T(8,128)S(1)}, u32[]{:S(2)}, u32[]{:S(2)}) collective-permute-start(f32[21,64,128]{2,1,0:T(8,128)S(1)} %get-tuple-element.54), channel_id=1, source_target_pairs={{0,4},{4,0},{8,12},{12,8},{16,20},{20,16},{24,28},{28,24},{32,36},... | collective-permute-start | bytes 2064392 | tf_op jit(solution)/shard_map/ppermute | solution.py:717
  9.2 6.5 %collective-permute-start.5 = (f32[6,16,128]{2,1,0:T(8,128)S(1)}, f32[6,16,128]{2,1,0:T(8,128)S(1)}, u32[]{:S(2)}, u32[]{:S(2)}) collective-permute-start(f32[6,16,128]{2,1,0:T(8,128)S(1)} %get-tuple-element.59), channel_id=1, source_target_pairs={{4,8},{8,4},{12,16},{16,12},{20,24},{24,20},{28,32},{32,28},{36,40... | collective-permute-start | bytes 147464 | tf_op jit(solution)/shard_map/ppermute | solution.py:716
  12.8 3.0 %collective-permute-start.4 = (f32[13,16,128]{2,1,0:T(8,128)S(1)}, f32[13,16,128]{2,1,0:T(8,128)S(1)}, u32[]{:S(2)}, u32[]{:S(2)}) collective-permute-start(f32[13,16,128]{2,1,0:T(8,128)S(1)} %get-tuple-element.58), channel_id=1, source_target_pairs={{0,4},{4,0},{8,12},{12,8},{16,20},{20,16},{24,28},{28,24},{32,36},... | collective-permute-start | bytes 319496 | tf_op jit(solution)/shard_map/ppermute | solution.py:717
  20.8 5.7 %collective-permute-start.6 = (f32[8,8,128]{2,1,0:T(8,128)S(1)}, f32[8,8,128]{2,1,0:T(8,128)S(1)}, u32[]{:S(2)}, u32[]{:S(2)}) collective-permute-start(f32[8,8,128]{2,1,0:T(8,128)S(1)} %get-tuple-element.77), channel_id=1, source_target_pairs={{0,1},{1,0},{2,3},{3,2},{4,5},{5,4},{6,7},{7,6},{8,9},{9,8},{10,11... | collective-permute-start | bytes 98312 | tf_op jit(solution)/shard_map/ppermute | solution.py:717
  24.6 1.9 %collective-permute-start.7 = (f32[8,8,128]{2,1,0:T(8,128)S(1)}, f32[8,8,128]{2,1,0:T(8,128)S(1)}, u32[]{:S(2)}, u32[]{:S(2)}) collective-permute-start(f32[8,8,128]{2,1,0:T(8,128)S(1)} %get-tuple-element.78), channel_id=1, source_target_pairs={{1,2},{2,1},{5,6},{6,5},{9,10},{10,9},{13,14},{14,13},{17,18},{18,... | collective-permute-start | bytes 98312 | tf_op jit(solution)/shard_map/ppermute | solution.py:716
  26.7 6.2 %collective-permute-start.9 = (f32[192,128]{1,0:T(8,128)S(1)}, f32[192,128]{1,0:T(8,128)S(1)}, u32[]{:S(2)}, u32[]{:S(2)}) collective-permute-start(f32[192,128]{1,0:T(8,128)S(1)} %get-tuple-element.81), channel_id=1, source_target_pairs={{4,8},{8,4},{12,16},{16,12},{20,24},{24,20},{28,32},{32,28},{36,40... | collective-permute-start | bytes 294920 | tf_op jit(solution)/shard_map/ppermute | solution.py:716
  30.6 2.3 %collective-permute-start.8 = (f32[192,128]{1,0:T(8,128)S(1)}, f32[192,128]{1,0:T(8,128)S(1)}, u32[]{:S(2)}, u32[]{:S(2)}) collective-permute-start(f32[192,128]{1,0:T(8,128)S(1)} %get-tuple-element.80), channel_id=1, source_target_pairs={{0,4},{4,0},{8,12},{12,8},{16,20},{20,16},{24,28},{28,24},{32,36},... | collective-permute-start | bytes 294920 | tf_op jit(solution)/shard_map/ppermute | solution.py:717
  32.9 1.3 %collective-permute-start.10 = (f32[192,128]{1,0:T(8,128)S(1)}, f32[192,128]{1,0:T(8,128)S(1)}, u32[]{:S(2)}, u32[]{:S(2)}) collective-permute-start(f32[192,128]{1,0:T(8,128)S(1)} %collective-permute-done.9.x1), channel_id=1, source_target_pairs={{0,4},{4,0},{8,12},{12,8},{16,20},{20,16},{24,28},{28,24},{32,36},... | collective-permute-start | bytes 294920 | tf_op jit(solution)/shard_map/ppermute | solution.py:715

commit v10 on v9

--- a/solution.py
+++ b/solution.py
@@ -316,7 +316,7 @@
     c, ua, c1, ga_, tmp, ctmp, tmp1,
 ):
     oy = odd("gy")
-    here, here1 = pl.ds(8, 80), pl.ds(8, 48)
+    here, here1 = pl.ds(8, 80), pl.ds(12, 40)
     sides = ((x0, k0, HIGH, HIGH_C, HIGH_B, X0 + NX - 1, 1), (x1, k1, LOW, LOW_C, LOW_B, X0, -1))
     for x, pack, corners, nc, nb, edge, sign in sides:
         for d in range(1, nc + 1):
@@ -398,19 +398,21 @@
                 c2[X2 - 2 + 4 * k + j, pl.ds(a, 8), :] = v
 
 
-def copy_rows(pairs, lo, hi):
+def copy_rows(pairs, lo, hi, y, n):
+    here = pl.ds(y, n)
+
     def body(x):
         for src, dst in pairs:
-            dst[x] = src[x]
+            dst[x, here, :] = src[x, here, :]
 
     rows(lo, hi, body)
 
 
 def edge2_kernel(u1_in, b1_in, c2_in, b2_in, y0, y1, high, low, u1, b1, c2, b2):
     oy = odd("gy")
-    copy_rows([(u1_in, u1), (b1_in, b1)], X1, X1 + 8)
-    copy_rows([(c2_in, c2)], X2 - 2, X2 + 6)
-    copy_rows([(b2_in, b2)], X2, X2 + 5)
+    copy_rows([(u1_in, u1), (b1_in, b1)], X1, X1 + 8, Y1, 32)
+    copy_rows([(c2_in, c2)], X2 - 2, X2 + 6, Y2, 16)
+    copy_rows([(b2_in, b2)], X2, X2 + 5, Y2, 16)
     set_y1(u1, y0, y1, oy, 0)
     set_y1(b1, y0, y1, oy, 1)
     set_y2(c2, b2, y0, y1, oy)
@@ -459,9 +461,9 @@
     c2, ua, tmp, b3, c3,
 ):
     ox, oy = odd("gx"), odd("gy")
-    copy_rows([(u1_in, u1)], X1, X1 + 8)
-    copy_rows([(c2_in, c2)], X2 - 2, X2 + 6)
-    copy_rows([(b2_in, b2)], X2, X2 + 5)
+    copy_rows([(u1_in, u1)], X1, X1 + 8, Y1, 32)
+    copy_rows([(c2_in, c2)], X2 - 2, X2 + 6, Y2, 16)
+    copy_rows([(b2_in, b2)], X2, X2 + 5, Y2, 16)
     set_y1(u1, y0, y1, oy, 0)
     set_y2(c2, b2, y0, y1, oy)
     for pack, edge1, edge2, sign in ((x0, X1 + 7, X2 + 3, 1), (x1, X1, X2, -1)):
@@ -665,7 +667,7 @@
 
     rows(0, 8, grow1)
 
-    copy_rows([(b1_in, b1)], 2, 18)
+    copy_rows([(b1_in, b1)], 2, 18, 8, 48)
     set_y1(b1, y0, y1, oy, 1)
     for j, v in enumerate(unpack_lanes(x1[pl.ds(164, 8), :], 2)):
         b1[X1 - 1 - j, pl.ds(12, 4), :] = v[0:4]

time: 67.1 us -> 67.1 us (level)
  no operation moved by 1% of the time
where the time goes in v10:
time: 67.1 us; the launch traced here: 66.8 us
  blocking collectives  24.6 us (37%)
  starting transfers between devices  18.9 us (28%)
  Pallas kernels  18 us (27%)
  waiting for transfers between devices  4.52 us (7%)
  between operations  0.77 us (1%)
    all_to_all x1, blocking collectives, per_device(): whole = lax.all_to_all(packed, ('gx', 'gy'), 0, 0, tiled=True)  24.6 us
    pallas_call x8, Pallas kernels, call(): pl.pallas_call(body, out_shape=[jax.ShapeDtypeStruct(s, F32) for s in out...  18 us
    ppermute x5, starting transfers between devices, swaps(): late = lax.ppermute(second, axis, pairs(1))  12.8 us
    ppermute x5, starting transfers between devices, swaps(): return (lax.ppermute(first, axis, pairs(0)), late)  6.1 us
    ppermute x5, waiting for transfers between devices, swaps(): late = lax.ppermute(second, axis, pairs(1))  2.87 us
  transfers between devices with their start and end apart: 11, of which 4 were waited for; matrix products, arithmetic and copies ran while one was open for 0% of the time, Pallas kernels for 5%

profile of v10, /device:TPU:1, one launch (start us, length us, event | category | flops | bytes accessed | tf_op | source)
XLA Modules:
  0.0 66.8 jit_solution(6030879792854012289)
XLA Ops:
  0.6 1.5 %begin.1 = (f32[16,64,128]{2,1,0:T(8,128)S(1)}, f32[16,64,128]{2,1,0:T(8,128)S(1)}, f32[32,8,128]{2,1,0:T(8,128)S(1)}, f32[32,8,128]{2,1,0:T(8,128)S(1)}) custom-call(f32[16,64,128]{2,1,0:T(8,128)} %source.1, f32[16,64,128]{2,1,0:T(8,128)} %density.1, f32[16,64,128]{2,1,0:T(8,128)} %drag.1, s32[64]{0:T(128)} %porous.1), custom_call_target="tpu_custom_call" | custom-call | tf_op jit(solution)/shard_map/begin/pallas_call | solution.py:23
  2.1 2.1 %collective-permute-start.2 = (f32[32,8,128]{2,1,0:T(8,128)S(1)}, f32[32,8,128]{2,1,0:T(8,128)S(1)}, u32[]{:S(2)}, u32[]{:S(2)}) collective-permute-start(f32[32,8,128]{2,1,0:T(8,128)S(1)} %get-tuple-element.56), channel_id=1, source_target_pairs={{0,1},{1,0},{2,3},{3,2},{4,5},{5,4},{6,7},{7,6},{8,9},{9,8},{10,11... | collective-permute-start | bytes 393224 | tf_op jit(solution)/shard_map/ppermute | solution.py:719
  4.3 0.7 collective-permute-start.3
  4.9 0.1 edges.1
  5.0 4.0 %collective-permute-start.1 = (f32[14,64,128]{2,1,0:T(8,128)S(1)}, f32[14,64,128]{2,1,0:T(8,128)S(1)}, u32[]{:S(2)}, u32[]{:S(2)}) collective-permute-start(f32[14,64,128]{2,1,0:T(8,128)S(1)} %get-tuple-element.55), channel_id=1, source_target_pairs={{4,8},{8,4},{12,16},{16,12},{20,24},{24,20},{28,32},{32,28},{36,40... | collective-permute-start | bytes 1376264 | tf_op jit(solution)/shard_map/ppermute | solution.py:718
  9.1 0.1 collective-permute-start
  9.2 0.0 collective-permute-done.2.y0
  9.2 0.0 collective-permute-done.3.y1
  9.2 3.6 %collective-permute-start.5 = (f32[6,16,128]{2,1,0:T(8,128)S(1)}, f32[6,16,128]{2,1,0:T(8,128)S(1)}, u32[]{:S(2)}, u32[]{:S(2)}) collective-permute-start(f32[6,16,128]{2,1,0:T(8,128)S(1)} %get-tuple-element.59), channel_id=1, source_target_pairs={{4,8},{8,4},{12,16},{16,12},{20,24},{24,20},{28,32},{32,28},{36,40... | collective-permute-start | bytes 147464 | tf_op jit(solution)/shard_map/ppermute | solution.py:718
  12.8 0.1 collective-permute-start.4
  12.9 2.2 %inner.1 = (f32[18,96,128]{2,1,0:T(8,128)S(1)}, f32[18,96,128]{2,1,0:T(8,128)S(1)}, f32[18,96,128]{2,1,0:T(8,128)S(1)}, f32[18,96,128]{2,1,0:T(8,128)S(1)}, f32[...) custom-call(f32[16,64,128]{2,1,0:T(8,128)S(1)} %get-tuple-element.52, ...), custom_call_target="tpu_custom_call" | custom-call | flops 10000000000 | tf_op jit(solution)/shard_map/inner/pallas_call | solution.py:23
  15.1 0.7 %collective-permute-done.5.k1 = f32[6,16,128]{2,1,0:T(8,128)S(1)} collective-permute-done((f32[6,16,128]{2,1,0:T(8,128)S(1)}, f32[6,16,128]{2,1,0:T(8,128)S(1)}, u32[]{:S(2)}, u32[]{:S(2)}) %collective-permute-start.5) | collective-permute-done | bytes 49184 | tf_op jit(solution)/shard_map/ppermute | solution.py:718
  15.7 0.0 collective-permute-done.4.k0
  15.7 0.0 collective-permute-done.1.x1
  15.7 0.0 collective-permute-done.x0
  15.8 5.1 %down.1 = (f32[36,96,128]{2,1,0:T(8,128)S(1)}, f32[36,96,128]{2,1,0:T(8,128)S(1)}, f32[36,96,128]{2,1,0:T(8,128)S(1)}, f32[36,96,128]{2,1,0:T(8,128)S(1)}, f32[3...) custom-call(f32[21,64,128]{2,1,0:T(8,128)S(1)} %collective-permute-d, ...), custom_call_target="tpu_custom_call" | custom-call | tf_op jit(solution)/shard_map/down/pallas_call | solution.py:23
  20.8 3.7 %collective-permute-start.6 = (f32[8,8,128]{2,1,0:T(8,128)S(1)}, f32[8,8,128]{2,1,0:T(8,128)S(1)}, u32[]{:S(2)}, u32[]{:S(2)}) collective-permute-start(f32[8,8,128]{2,1,0:T(8,128)S(1)} %get-tuple-element.77), channel_id=1, source_target_pairs={{0,1},{1,0},{2,3},{3,2},{4,5},{5,4},{6,7},{7,6},{8,9},{9,8},{10,11... | collective-permute-start | bytes 98312 | tf_op jit(solution)/shard_map/ppermute | solution.py:719
  24.6 0.7 collective-permute-start.7
  25.2 1.3 %collective-permute-done.6.y0 = f32[8,8,128]{2,1,0:T(8,128)S(1)} collective-permute-done((f32[8,8,128]{2,1,0:T(8,128)S(1)}, f32[8,8,128]{2,1,0:T(8,128)S(1)}, u32[]{:S(2)}, u32[]{:S(2)}) %collective-permute-start.6) | collective-permute-done | bytes 32800 | tf_op jit(solution)/shard_map/ppermute | solution.py:719
  26.5 0.0 collective-permute-done.7.y1
  26.5 0.2 edges2.1
  26.7 3.9 %collective-permute-start.9 = (f32[192,128]{1,0:T(8,128)S(1)}, f32[192,128]{1,0:T(8,128)S(1)}, u32[]{:S(2)}, u32[]{:S(2)}) collective-permute-start(f32[192,128]{1,0:T(8,128)S(1)} %get-tuple-element.81), channel_id=1, source_target_pairs={{4,8},{8,4},{12,16},{16,12},{20,24},{24,20},{28,32},{32,28},{36,40... | collective-permute-start | bytes 294920 | tf_op jit(solution)/shard_map/ppermute | solution.py:718
  30.6 0.1 collective-permute-start.8
  30.7 2.2 %collective-permute-done.9.x1 = f32[192,128]{1,0:T(8,128)S(1)} collective-permute-done((f32[192,128]{1,0:T(8,128)S(1)}, f32[192,128]{1,0:T(8,128)S(1)}, u32[]{:S(2)}, u32[]{:S(2)}) %collective-permute-start.9) | collective-permute-done | bytes 98336 | tf_op jit(solution)/shard_map/ppermute | solution.py:718
  32.8 0.0 collective-permute-start.10
  32.9 0.0 collective-permute-done.8.x0
  32.9 0.9 %level2.1 = (f32[16,48,128]{2,1,0:T(8,128)S(1)}, f32[16,48,128]{2,1,0:T(8,128)S(1)}, f32[16,48,128]{2,1,0:T(8,128)S(1)}, f32[16,48,128]{2,1,0:T(8,128)S(1)}, f32...) custom-call(f32[18,64,128]{2,1,0:T(8,128)S(1)} %get-tuple-element.74., ...), custom_call_target="tpu_custom_call" | custom-call | tf_op jit(solution)/shard_map/level2/pallas_call | solution.py:23
  33.8 0.4 collective-permute-done.10.far
  34.2 24.6 %all_to_all.11 = f32[128,4,128]{2,1,0:T(4,128)S(1)} all-to-all(f32[128,4,128]{2,1,0:T(4,128)S(1)} %bitcast.3), channel_id=1, replica_groups=mesh['gx'=32,'gy'=4] {'gx','gy'}, dimensions={0} | all-to-all | bytes 524288 | tf_op jit(solution)/shard_map/all_to_all | solution.py:767
  58.8 8.1 %up.1 = (f32[16,64,128]{2,1,0:T(8,128)}, f32[16,64,128]{2,1,0:T(8,128)}) custom-call(f32[512,128]{1,0:T(8,128)S(1)} %bitcast.2, f32[8,8,128]{2,1,0:T(8,128)S(1)} %collective-permute-done.6.y0, f32[8,8,128]{2,1,0:T(8,128)S(1)} %collective-permute-done.7.y1, f32[192,128]{1,0:T(8,128)S(1)} %collective-permute-done.9.x1, ...), custom_call_target="tpu_custom_call" | custom-call | tf_op jit(solution)/shard_map/up/pallas_call | solution.py:23
  (1 shorter events, 0.0 us)
Async XLA Ops:
  2.1 7.0 %collective-permute-start.2 = (f32[32,8,128]{2,1,0:T(8,128)S(1)}, f32[32,8,128]{2,1,0:T(8,128)S(1)}, u32[]{:S(2)}, u32[]{:S(2)}) collective-permute-start(f32[32,8,128]{2,1,0:T(8,128)S(1)} %get-tuple-element.56), channel_id=1, source_target_pairs={{0,1},{1,0},{2,3},{3,2},{4,5},{5,4},{6,7},{7,6},{8,9},{9,8},{10,11... | collective-permute-start | bytes 393224 | tf_op jit(solution)/shard_map/ppermute | solution.py:719
  4.3 4.9 %collective-permute-start.3 = (f32[32,8,128]{2,1,0:T(8,128)S(1)}, f32[32,8,128]{2,1,0:T(8,128)S(1)}, u32[]{:S(2)}, u32[]{:S(2)}) collective-permute-start(f32[32,8,128]{2,1,0:T(8,128)S(1)} %get-tuple-element.57), channel_id=1, source_target_pairs={{1,2},{2,1},{5,6},{6,5},{9,10},{10,9},{13,14},{14,13},{17,18},{18,... | collective-permute-start | bytes 393224 | tf_op jit(solution)/shard_map/ppermute | solution.py:718
  5.0 10.7 %collective-permute-start.1 = (f32[14,64,128]{2,1,0:T(8,128)S(1)}, f32[14,64,128]{2,1,0:T(8,128)S(1)}, u32[]{:S(2)}, u32[]{:S(2)}) collective-permute-start(f32[14,64,128]{2,1,0:T(8,128)S(1)} %get-tuple-element.55), channel_id=1, source_target_pairs={{4,8},{8,4},{12,16},{16,12},{20,24},{24,20},{28,32},{32,28},{36,40... | collective-permute-start | bytes 1376264 | tf_op jit(solution)/shard_map/ppermute | solution.py:718
  9.1 6.7 %collective-permute-start = (f32[21,64,128]{2,1,0:T(8,128)S(1)}, f32[21,64,128]{2,1,0:T(8,128)S(1)}, u32[]{:S(2)}, u32[]{:S(2)}) collective-permute-start(f32[21,64,128]{2,1,0:T(8,128)S(1)} %get-tuple-element.54), channel_id=1, source_target_pairs={{0,4},{4,0},{8,12},{12,8},{16,20},{20,16},{24,28},{28,24},{32,36},... | collective-permute-start | bytes 2064392 | tf_op jit(solution)/shard_map/ppermute | solution.py:719
  9.2 6.5 %collective-permute-start.5 = (f32[6,16,128]{2,1,0:T(8,128)S(1)}, f32[6,16,128]{2,1,0:T(8,128)S(1)}, u32[]{:S(2)}, u32[]{:S(2)}) collective-permute-start(f32[6,16,128]{2,1,0:T(8,128)S(1)} %get-tuple-element.59), channel_id=1, source_target_pairs={{4,8},{8,4},{12,16},{16,12},{20,24},{24,20},{28,32},{32,28},{36,40... | collective-permute-start | bytes 147464 | tf_op jit(solution)/shard_map/ppermute | solution.py:718
  12.8 3.0 %collective-permute-start.4 = (f32[13,16,128]{2,1,0:T(8,128)S(1)}, f32[13,16,128]{2,1,0:T(8,128)S(1)}, u32[]{:S(2)}, u32[]{:S(2)}) collective-permute-start(f32[13,16,128]{2,1,0:T(8,128)S(1)} %get-tuple-element.58), channel_id=1, source_target_pairs={{0,4},{4,0},{8,12},{12,8},{16,20},{20,16},{24,28},{28,24},{32,36},... | collective-permute-start | bytes 319496 | tf_op jit(solution)/shard_map/ppermute | solution.py:719
  20.8 5.7 %collective-permute-start.6 = (f32[8,8,128]{2,1,0:T(8,128)S(1)}, f32[8,8,128]{2,1,0:T(8,128)S(1)}, u32[]{:S(2)}, u32[]{:S(2)}) collective-permute-start(f32[8,8,128]{2,1,0:T(8,128)S(1)} %get-tuple-element.77), channel_id=1, source_target_pairs={{0,1},{1,0},{2,3},{3,2},{4,5},{5,4},{6,7},{7,6},{8,9},{9,8},{10,11... | collective-permute-start | bytes 98312 | tf_op jit(solution)/shard_map/ppermute | solution.py:719
  24.6 1.9 %collective-permute-start.7 = (f32[8,8,128]{2,1,0:T(8,128)S(1)}, f32[8,8,128]{2,1,0:T(8,128)S(1)}, u32[]{:S(2)}, u32[]{:S(2)}) collective-permute-start(f32[8,8,128]{2,1,0:T(8,128)S(1)} %get-tuple-element.78), channel_id=1, source_target_pairs={{1,2},{2,1},{5,6},{6,5},{9,10},{10,9},{13,14},{14,13},{17,18},{18,... | collective-permute-start | bytes 98312 | tf_op jit(solution)/shard_map/ppermute | solution.py:718
  26.7 6.2 %collective-permute-start.9 = (f32[192,128]{1,0:T(8,128)S(1)}, f32[192,128]{1,0:T(8,128)S(1)}, u32[]{:S(2)}, u32[]{:S(2)}) collective-permute-start(f32[192,128]{1,0:T(8,128)S(1)} %get-tuple-element.81), channel_id=1, source_target_pairs={{4,8},{8,4},{12,16},{16,12},{20,24},{24,20},{28,32},{32,28},{36,40... | collective-permute-start | bytes 294920 | tf_op jit(solution)/shard_map/ppermute | solution.py:718
  30.6 2.3 %collective-permute-start.8 = (f32[192,128]{1,0:T(8,128)S(1)}, f32[192,128]{1,0:T(8,128)S(1)}, u32[]{:S(2)}, u32[]{:S(2)}) collective-permute-start(f32[192,128]{1,0:T(8,128)S(1)} %get-tuple-element.80), channel_id=1, source_target_pairs={{0,4},{4,0},{8,12},{12,8},{16,20},{20,16},{24,28},{28,24},{32,36},... | collective-permute-start | bytes 294920 | tf_op jit(solution)/shard_map/ppermute | solution.py:719
  32.8 1.3 %collective-permute-start.10 = (f32[192,128]{1,0:T(8,128)S(1)}, f32[192,128]{1,0:T(8,128)S(1)}, u32[]{:S(2)}, u32[]{:S(2)}) collective-permute-start(f32[192,128]{1,0:T(8,128)S(1)} %collective-permute-done.9.x1), channel_id=1, source_target_pairs={{0,4},{4,0},{8,12},{12,8},{16,20},{20,16},{24,28},{28,24},{32,36},... | collective-permute-start | bytes 294920 | tf_op jit(solution)/shard_map/ppermute | solution.py:717
